TPU v7x, 32 devices: a whole 2x2x4 slice. The times are simulated.
32 devices in a mesh: dp: 4 (over x, core), ctx: 8 (over z, y).
Axes of the slice: x: 2, y: 2, z: 4, core: 2. Of those that a mesh axis runs over, the one named last changes fastest.
Arguments:
- tokens: bfloat16 [4096, 4096], P(('dp', 'ctx')), parts along dimension 0, may hold values from -6 to 6
- pick_flags: int32 [4096], P(('dp', 'ctx')), parts along dimension 0, may hold values from 0 to 1, as said below
- gate_scales: bfloat16 [4096], P(('dp', 'ctx')), parts along dimension 0, may hold values from 0.099609375 to 1
- attn_gain: float32 [4096], replicated, may hold values from 0.4 to 1.6
- query_weight: bfloat16 [4096, 4096], P(None, 'ctx')
- key_weight: bfloat16 [4096, 1024], P(None, 'ctx')
- value_matrix: bfloat16 [4096, 1024], P(None, 'ctx'), may hold values from -0.09375 to 0.09375
- output_weight: bfloat16 [4096, 4096], P('ctx'), may hold values from -0.09375 to 0.09375
- ffn_gain: float32 [4096], replicated, may hold values from 0.25 to 1.75
- gate_weight: bfloat16 [4096, 11264], P(None, 'ctx'), may hold values from -0.09375 to 0.09375
- up_weight: bfloat16 [4096, 11264], P(None, 'ctx'), may hold values from -0.09375 to 0.09375
- down_weight: bfloat16 [11264, 4096], P('ctx'), may hold values from -0.0546875 to 0.0546875
Outputs:
- block_out: bfloat16 [4096, 4096], P(('dp', 'ctx')), parts along dimension 0
There are 4 independent parts, one for each index of `dp`. A program takes and returns all parts, laid end to end along the dimension named above; an argument that names none is the same for every part. Nothing has to cross between parts.
Inputs may be any that keep to these rules, and one draw needn't show every extreme that they name: `pick_flags`: each device's 128 tokens hold at most 32 picks, the first device exactly 32; each document holds exactly 128 picks; a device may hold none.
All inputs are finite; a program needn't handle non-finite values.
Results may differ from a plain program's by a relative error of at most 0.01.
Values may be sent and summed in bfloat16 or wider, within the bound.
No kernel may reach another device: no remote copies, remote signals or barrier semaphores. Data moves between devices by JAX's collectives and lax.ppermute only.
A program may use at most 128 MiB of HBM per device.

v0:
```python
import jax
import jax.numpy as jnp
from jax import lax
from jax.sharding import PartitionSpec as P

QUERY_HEADS = 32
KEY_VALUE_HEADS = 8
HEAD_SIZE = 128
PICK_DEV = 16
MOST = 32


norm_eps = 1e-05
rope_base = 500000.0


def rms_scale(matrix, gain_vec):
    mean_square = jnp.mean(matrix * matrix, axis=-1, keepdims=True)
    return matrix * lax.rsqrt(mean_square + norm_eps) * gain_vec


def apply_rotary(values, token_positions):
    half_dim = values.shape[-1] // 2
    frequency = rope_base ** (-(jnp.arange(half_dim, dtype=jnp.float32) * 2.0) / values.shape[-1])
    angles = token_positions.astype(jnp.float32)[:, None] * frequency[None, :]
    cosine = jnp.cos(angles)[:, None, :]
    sine_part = jnp.sin(angles)[:, None, :]
    lower_half = values[..., :half_dim]
    upper_half = values[..., half_dim:]
    return jnp.concatenate(
        (
            lower_half * cosine - upper_half * sine_part,
            upper_half * cosine + lower_half * sine_part,
        ),
        axis=-1,
    )


def body(
    tokens,
    pick_flags,
    gate_scales,
    attn_gain,
    query_weight,
    key_weight,
    value_matrix,
    output_weight,
    ffn_gain,
    gate_weight,
    up_weight,
    down_weight,
):
    tok_local = tokens.shape[0]
    ctx_size = lax.axis_size("ctx")
    my_index = lax.axis_index("ctx")
    picked_count = PICK_DEV * ctx_size
    half_pick = PICK_DEV // 2
    half_cycle = ctx_size // 2
    slot_of = jnp.cumsum(pick_flags) - 1
    token_ids = jnp.arange(tok_local, dtype=jnp.int32)
    slot_match = (jnp.arange(MOST, dtype=jnp.int32)[:, None] == slot_of[None, :]) & (
        pick_flags[None, :] == 1
    )
    chosen = jnp.sum(jnp.where(slot_match, token_ids[None, :], 0), axis=1)
    filled = jnp.any(slot_match, axis=1)
    local_index = jnp.where(filled, chosen, -1)
    padded_rows = jnp.where(filled[:, None], tokens[chosen], jnp.zeros((), jnp.bfloat16))
    padded_gate = jnp.where(filled, gate_scales[chosen], jnp.zeros((), jnp.bfloat16))
    all_rows, all_gate, all_index = (
        lax.all_gather(padded_rows, "ctx", axis=0, tiled=True),
        lax.all_gather(padded_gate, "ctx", axis=0, tiled=True),
        lax.all_gather(local_index, "ctx", axis=0, tiled=True),
    )
    counts = jnp.sum((all_index >= 0).reshape(ctx_size, MOST).astype(jnp.int32), axis=1)
    run_ends = jnp.cumsum(counts)
    run_starts = run_ends - counts
    order_ids = jnp.arange(picked_count, dtype=jnp.int32)
    owner_of = order_ids // PICK_DEV
    within = order_ids % PICK_DEV
    low_part = within < half_pick
    rank_block = jnp.where(low_part, owner_of, (owner_of + half_cycle) % ctx_size)
    rank_inner = jnp.where(low_part, 2 * within, 2 * (within - half_pick) + 1)
    rank_ids = rank_block * PICK_DEV + rank_inner
    source = jnp.sum((run_ends[None, :] <= rank_ids[:, None]).astype(jnp.int32), axis=1)
    flat_row = source * MOST + rank_ids - run_starts[source]
    picked_rows = all_rows[flat_row]
    scales = all_gate[flat_row].astype(jnp.float32)
    token_positions = source * tok_local + all_index[flat_row]
    normalized_rows = rms_scale(picked_rows.astype(jnp.float32), attn_gain).astype(jnp.bfloat16)
    heads_here = query_weight.shape[1] // HEAD_SIZE
    queries = jnp.dot(normalized_rows, query_weight, preferred_element_type=jnp.float32).reshape(
        picked_count, heads_here, HEAD_SIZE
    )
    queries = apply_rotary(queries, token_positions).astype(jnp.bfloat16)
    kv_weight = jnp.concatenate((key_weight, value_matrix), axis=1)
    kv_local = jnp.einsum(
        "pd,dc->cp", normalized_rows, kv_weight, preferred_element_type=jnp.float32
    ).astype(jnp.bfloat16)
    kv_all = lax.all_gather(kv_local, "ctx", axis=0, tiled=True)
    col_count = key_weight.shape[1]
    key_value_parts = kv_all.reshape(ctx_size, 2, col_count, picked_count)
    key_columns = key_value_parts[:, 0].reshape(HEAD_SIZE * KEY_VALUE_HEADS, picked_count)
    value_columns = key_value_parts[:, 1].reshape(HEAD_SIZE * KEY_VALUE_HEADS, picked_count)
    key_heads = jnp.transpose(
        key_columns.T.astype(jnp.float32).reshape(picked_count, HEAD_SIZE, KEY_VALUE_HEADS),
        (0, 2, 1),
    )
    rotated_keys = apply_rotary(key_heads, token_positions).astype(jnp.bfloat16)
    repeated_values = jnp.transpose(
        value_columns.T.reshape(picked_count, HEAD_SIZE, KEY_VALUE_HEADS), (0, 2, 1)
    )
    query_group_width = QUERY_HEADS // KEY_VALUE_HEADS
    kv_pick = (my_index * heads_here + jnp.arange(heads_here, dtype=jnp.int32)) // query_group_width
    keys_here = jnp.take(rotated_keys, kv_pick, axis=1)
    values_here = jnp.take(repeated_values, kv_pick, axis=1)
    scores = jnp.einsum(
        "qhd,khd->hqk", queries, keys_here, preferred_element_type=jnp.float32
    ) / jnp.sqrt(jnp.float32(HEAD_SIZE))
    allowed = token_positions[None, :] <= token_positions[:, None]
    scores = jnp.where(allowed[None, :, :], scores, -jnp.inf)
    row_max = jnp.max(scores, axis=2, keepdims=True)
    exp_terms = jnp.exp(scores - row_max)
    prob_bf = (exp_terms / jnp.sum(exp_terms, axis=2, keepdims=True)).astype(jnp.bfloat16)
    head_out = jnp.einsum(
        "hqk,khd->qhd", prob_bf, values_here, preferred_element_type=jnp.float32
    ).astype(jnp.bfloat16)
    head_out = head_out.reshape(picked_count, heads_here * HEAD_SIZE)
    own_start = my_index * PICK_DEV
    own_rows = lax.dynamic_slice_in_dim(picked_rows, own_start, PICK_DEV, 0).astype(jnp.float32)
    row_block = head_out
    attn_own = lax.psum_scatter(
        jnp.dot(row_block, output_weight, preferred_element_type=jnp.float32).astype(jnp.bfloat16),
        "ctx",
        scatter_dimension=0,
        tiled=True,
    ).astype(jnp.float32)
    mixed_own = own_rows + attn_own
    normed_own = rms_scale(mixed_own, ffn_gain).astype(jnp.bfloat16)
    normed_ffn = lax.all_gather(normed_own, "ctx", axis=0, tiled=True)
    row_block = normed_ffn
    gate_proj = jnp.dot(row_block, gate_weight, preferred_element_type=jnp.float32)
    up_proj = jnp.dot(row_block, up_weight, preferred_element_type=jnp.float32)
    hidden = (jax.nn.silu(gate_proj) * up_proj).astype(jnp.bfloat16)
    ffn_own = lax.psum_scatter(
        jnp.dot(hidden, down_weight, preferred_element_type=jnp.float32).astype(jnp.bfloat16),
        "ctx",
        scatter_dimension=0,
        tiled=True,
    ).astype(jnp.float32)
    scale_own = lax.dynamic_slice_in_dim(scales, own_start, PICK_DEV, 0)
    final_own = (own_rows + scale_own[:, None] * (attn_own + ffn_own)).astype(jnp.bfloat16)
    final_all = lax.all_gather(final_own, "ctx", axis=0, tiled=True)
    my_start = run_starts[my_index]
    rank_here = jnp.clip(my_start + slot_of, 0, picked_count - 1)
    inner_here = rank_here % PICK_DEV
    odd_here = inner_here % 2
    owner_here = (rank_here // PICK_DEV + odd_here * half_cycle) % ctx_size
    take_rows = owner_here * PICK_DEV + inner_here // 2 + odd_here * half_pick
    return jnp.where(pick_flags[:, None] == 1, final_all[take_rows], tokens)


def solution(mesh):
    in_specs = (
        P(("dp", "ctx"), None),
        P(("dp", "ctx")),
        P(("dp", "ctx")),
        P(),
        P(None, "ctx"),
        P(None, "ctx"),
        P(None, "ctx"),
        P("ctx", None),
        P(),
        P(None, "ctx"),
        P(None, "ctx"),
        P("ctx", None),
    )
    out_specs = P(("dp", "ctx"), None)
    return jax.shard_map(body, mesh=mesh, in_specs=in_specs, out_specs=out_specs, check_vma=False)
```

profile of v0, /device:TPU:0, one launch (start us, length us, event | category | flops | bytes accessed | tf_op | source)
XLA Modules:
  0.0 350.9 jit_solution(11912297505597011540)
XLA Ops:
  6.5 0.7 broadcast_compare_fusion.1
  7.2 0.8 copy.58
  8.5 2.3 gather_fusion
  10.8 0.8 broadcast_select_fusion.1
  11.7 1.3 dynamic-slice
  13.7 13.1 %all-reduce = s32[256]{0:T(256)S(1)} all-reduce(s32[256]{0:T(256)S(1)} %select_dynamic-update-slice_fusion), channel_id=1, replica_groups=mesh['dp'=4,'ctx'=8] {'ctx'}, use_global_device_ids=true, to_apply=%add | all-reduce | flops 256 | bytes 2048
  27.3 0.7 fusion.69
  28.1 4.9 %fusion.52 = s32[128]{0:T(128)S(1)} fusion(s32[128]{0:T(128)S(1)} %convert_reduce_fusion, s32[]{:T(128)} %bitcast.10, s32[]{:T(128)} %bitcast.11, s32[]{:T(128)} %bitcast.12, s32[]{:T(128)} %bitcast.13, s32[]{:T(128)} %bitcast.14, s32[]{:T(128)} %bitcast.16, s32[]{:T(128)} %bitcast.15, s32[]{:T(128)} %bitcast.9), kind=kLoop, calls=%fused_computation.134 | loop fusion | flops 7168 | bytes 1056 | tf_op jit(solution)/shard_map/select_n | solution.py:86
  33.0 1.3 gather_fusion.4
  34.8 29.0 %all-gather.4.cloned.1.call-done = bf16[256,4096]{1,0:T(8,128)(2,1)} async-done(((bf16[32,4096]{1,0:T(8,128)(2,1)}), bf16[256,4096]{1,0:T(8,128)(2,1)}) %all-gather.4.cloned.1.call-update) | async-done | bytes 2097168 | tf_op jit(solution)/shard_map/all_gather | solution.py:70
  63.8 4.1 %gather_fusion.1 = bf16[128,4096]{1,0:T(8,128)(2,1)S(1)} fusion(bf16[256,4096]{1,0:T(8,128)(2,1)} %all-gather.4.cloned.1.call-done, s32[1024]{0:T(1024)S(1)} %pad_clamp_fusion.2), kind=kCustom, calls=%fused_computation.3 | custom fusion | bytes 2097664 | tf_op jit(solution)/shard_map/gather | solution.py:86
  68.2 3.0 fusion.16
  71.5 2.3 fusion.12
  73.8 31.4 %all_gather.21 = bf16[2048,128]{1,0:T(8,128)(2,1)S(1)} all-gather(bf16[256,128]{1,0:T(8,128)(2,1)S(1)} %fusion.12), channel_id=1, replica_groups=mesh['dp'=4,'ctx'=8] {'ctx'}, dimensions={0}, use_global_device_ids=true | all-gather | bytes 589824 | tf_op jit(solution)/shard_map/all_gather | solution.py:99
  106.1 0.6 gather_fusion.7
  107.6 0.6 gather_fusion.6
  108.5 3.9 %convolution_convert_fusion.1 = bf16[128,4096]{1,0:T(8,128)(2,1)} fusion(bf16[128,512]{0,1:T(8,128)(2,1)S(1)} %bitcast.98, bf16[512,4096]{1,0:T(8,128)(2,1)} %param.21), kind=kOutput, calls=%fused_computation.10 | convolution fusion | flops 537395200 | bytes 5373952 | tf_op jit(solution)/shard_map/dot_general | solution.py:132
  112.5 62.3 %reduce-scatter.3.cloned.1.call-done = bf16[16,4096]{1,0:T(8,128)(2,1)} async-done(((bf16[128,4096]{1,0:T(8,128)(2,1)}), bf16[16,4096]{1,0:T(8,128)(2,1)}) %reduce-scatter.3.cloned.1.call-update) | async-done | bytes 131088 | tf_op jit(solution)/shard_map/reduce_scatter | solution.py:131
  174.8 1.1 multiply_reduce_fusion
  175.8 1.7 multiply_convert_fusion
  177.8 39.2 %all-gather.6.cloned.1.call-done = bf16[128,4096]{1,0:T(8,128)(2,1)} async-done(((bf16[16,4096]{1,0:T(8,128)(2,1)}), bf16[128,4096]{1,0:T(8,128)(2,1)}) %all-gather.6.cloned.1.call-update) | async-done | bytes 1048592 | tf_op jit(solution)/shard_map/all_gather | solution.py:139
  216.9 6.5 %fusion.75 = f32[128,1408]{1,0:T(8,128)S(1)} fusion(bf16[128,4096]{1,0:T(8,128)(2,1)} %all-gather.6.cloned.1.call-done, bf16[4096,1408]{1,0:T(8,128)(2,1)} %param.23), kind=kOutput, calls=%fused_computation.161 | convolution fusion | flops 1476395008 | bytes 13303808 | tf_op jit(solution)/shard_map/dot_general | solution.py:141
  223.4 12.2 %convolution_convert_fusion = bf16[128,4096]{1,0:T(8,128)(2,1)} fusion(bf16[1408,4096]{1,0:T(8,128)(2,1)} %param.25, bf16[128,4096]{1,0:T(8,128)(2,1)S(1)} %copy-done.2, bf16[4096,1408]{1,0:T(8,128)(2,1)} %param.24, f32[128,1408]{1,0:T(8,128)S(1)} %fusion.75), kind=kOutput, calls=%fused_computation.9 | convolution fusion | flops 2954395648 | bytes 25886720 | tf_op jit(solution)/shard_map/dot_general | solution.py:145
  235.7 0.7 gather_fusion.2
  236.7 19.2 %all-reduce.1 = bf16[256]{0:T(256)(128)(2,1)S(1)} all-reduce(bf16[256]{0:T(256)(128)(2,1)S(1)} %dynamic-update-slice.1), channel_id=1, replica_groups=mesh['dp'=4,'ctx'=8] {'ctx'}, use_global_device_ids=true, to_apply=%add.1 | all-reduce | flops 256 | bytes 1024
  255.9 1.2 gather_fusion.3
  257.2 41.2 %reduce-scatter.5.cloned.1.call-done = bf16[16,4096]{1,0:T(8,128)(2,1)} async-done(((bf16[128,4096]{1,0:T(8,128)(2,1)}), bf16[16,4096]{1,0:T(8,128)(2,1)}) %reduce-scatter.5.cloned.1.call-update) | async-done | bytes 131088 | tf_op jit(solution)/shard_map/reduce_scatter | solution.py:144
  298.4 1.7 fusion.19
  300.1 0.7 fusion.53
  300.8 38.9 %all-gather.8.cloned.1.call-done = bf16[128,4096]{1,0:T(8,128)(2,1)} async-done(((bf16[16,4096]{1,0:T(8,128)(2,1)}), bf16[128,4096]{1,0:T(8,128)(2,1)}) %all-gather.8.cloned.1.call-update) | async-done | bytes 1048592 | tf_op jit(solution)/shard_map/all_gather | solution.py:152
  339.7 3.6 %gather_fusion.5 = bf16[128,4096]{1,0:T(8,128)(2,1)S(1)} fusion(bf16[128,4096]{1,0:T(8,128)(2,1)} %all-gather.8.cloned.1.call-done, s32[1024]{0:T(1024)S(1)} %pad_clamp_fusion), kind=kCustom, calls=%fused_computation.7 | custom fusion | bytes 2097664 | tf_op jit(solution)/shard_map/gather | solution.py:159
  343.3 1.1 broadcast_select_fusion
  (66 shorter events, 4.9 us)
Async XLA Ops:
  6.5 229.2 %copy-start = (bf16[128]{0:T(256)(128)(2,1)S(1)}, bf16[128]{0:T(256)(128)(2,1)}, u32[]{:S(2)}) copy-start(bf16[128]{0:T(256)(128)(2,1)} %param.16) | copy-start | bytes 772
  6.5 57.3 %all-gather.4.cloned.1.call-start = ((), (), s32[]{:S(2)}) async-start(), calls=%async_computation.2 | async-start | bytes 2359296 | tf_op jit(solution)/shard_map/all_gather | solution.py:70
  11.6 163.1 %reduce-scatter.3.cloned.1.call-start = ((), (), s32[]{:S(2)}) async-start(), calls=%async_computation.3 | async-start | bytes 1179648 | tf_op jit(solution)/shard_map/reduce_scatter | solution.py:131
  34.8 33.4 %copy-start.5 = (f32[4096]{0:T(1024)S(1)}, f32[4096]{0:T(1024)}, u32[]{:S(2)}) copy-start(f32[4096]{0:T(1024)} %param.17) | copy-start | bytes 49156
  107.6 68.3 %copy-start.4 = (f32[4096]{0:T(1024)S(1)}, f32[4096]{0:T(1024)}, u32[]{:S(2)}) copy-start(f32[4096]{0:T(1024)} %param.22) | copy-start | bytes 49156
  112.4 104.5 %all-gather.6.cloned.1.call-start = ((), (), s32[]{:S(2)}) async-start(), calls=%async_computation.4 | async-start | bytes 1179648 | tf_op jit(solution)/shard_map/all_gather | solution.py:139
  177.5 120.9 %reduce-scatter.5.cloned.1.call-start = ((), (), s32[]{:S(2)}) async-start(), calls=%async_computation.5 | async-start | bytes 1179648 | tf_op jit(solution)/shard_map/reduce_scatter | solution.py:144
  216.9 6.5 %copy-start.2 = (bf16[128,4096]{1,0:T(8,128)(2,1)S(1)}, bf16[128,4096]{1,0:T(8,128)(2,1)}, u32[]{:S(2)}) copy-start(bf16[128,4096]{1,0:T(8,128)(2,1)} %all-gather.6.cloned.1.call-done) | copy-start | bytes 3145732
  223.4 75.0 %copy-start.3 = (bf16[16,4096]{1,0:T(8,128)(2,1)S(1)}, bf16[16,4096]{1,0:T(8,128)(2,1)}, u32[]{:S(2)}) copy-start(bf16[16,4096]{1,0:T(8,128)(2,1)} %reduce-scatter.3.cloned.1.call-done) | copy-start | bytes 393220
  235.7 104.0 %all-gather.8.cloned.1.call-start = ((), (), s32[]{:S(2)}) async-start(), calls=%async_computation.6 | async-start | bytes 1179648 | tf_op jit(solution)/shard_map/all_gather | solution.py:152
  300.8 42.5 %copy-start.1 = (bf16[128,4096]{1,0:T(8,128)(2,1)S(1)}, bf16[128,4096]{1,0:T(8,128)(2,1)}, u32[]{:S(2)}) copy-start(bf16[128,4096]{1,0:T(8,128)(2,1)} %param.14) | copy-start | bytes 3145732
Sparse Core Ops, SparseCore 0:
  11.7 52.0 all-gather.3
  112.5 62.1 reduce-scatter.2
  177.6 39.2 all-gather.5
  235.8 62.5 reduce-scatter.4
  300.4 39.2 all-gather.7
where the time goes:
time: 351 us
  waiting for transfers between devices  211 us (60%)
  blocking collectives  63.8 us (18%)
  matrix products  28.9 us (8%)
  local copies, waits for them, and re-layouts  18.3 us (5%)
  other arithmetic  14.8 us (4%)
  between operations  14.1 us (4%)
    reduce_scatter x1, waiting for transfers between devices, body(): lax.psum_scatter(jnp.dot(row_block, output_weight, preferred_element_type...  62.3 us
    reduce_scatter x1, waiting for transfers between devices, body(): lax.psum_scatter(jnp.dot(hidden, down_weight, preferred_element_type=jnp....  41.2 us
    all_gather x1, waiting for transfers between devices, body(): normed_ffn = lax.all_gather(normed_own, 'ctx', axis=0, tiled=True)  39.2 us
    all_gather x1, waiting for transfers between devices, body(): final_all = lax.all_gather(final_own, 'ctx', axis=0, tiled=True)  38.9 us
    unnamed x2, blocking collectives  32.3 us
    all_gather x1, blocking collectives, body(): kv_all = lax.all_gather(kv_local, 'ctx', axis=0, tiled=True)  31.4 us
    all_gather x1, waiting for transfers between devices, body(): lax.all_gather(padded_rows, 'ctx', axis=0, tiled=True)  29 us
    dot_general x1, matrix products, body(): jnp.dot(hidden, down_weight, preferred_element_type=jnp.float32)  12.2 us
  transfers between devices with their start and end apart: 5, of which 5 were waited for; matrix products, arithmetic and copies ran while one was open for 3% of the time, Pallas kernels for 0%

commit v1 on v0

v1 whole, which is shorter than its diff:
```python
import jax
import jax.numpy as jnp
from jax import lax
from jax.sharding import PartitionSpec as P

QUERY_HEADS = 32
KEY_VALUE_HEADS = 8
HEAD_SIZE = 128
PICK_DEV = 16
MOST = 32
NEAR = 4

norm_eps = 1e-05
rope_base = 500000.0

f32 = jnp.float32
bf16 = jnp.bfloat16


def swap(value, mask):
    size = lax.axis_size("ctx")
    return lax.ppermute(value, "ctx", [(i, i ^ mask) for i in range(size)])


def at(stack, index):
    return lax.dynamic_index_in_dim(stack, index, 0, keepdims=False)


def dot(a, b):
    return jnp.dot(a, b, preferred_element_type=f32)


def rms_scale(matrix, gain_vec):
    mean_square = jnp.mean(matrix * matrix, axis=-1, keepdims=True)
    return matrix * lax.rsqrt(mean_square + norm_eps) * gain_vec


def quarters(matrix):
    rows, cols = matrix.shape
    return [matrix[:, a * (cols // NEAR) : (a + 1) * (cols // NEAR)] for a in range(NEAR)]


def near_scatter(matrix, near):
    stack = jnp.stack(quarters(matrix))
    total = at(stack, near).astype(f32)
    for k in (3, 1, 2):
        total = total + swap(at(stack, near ^ k), k).astype(f32)
    return total


def near_gather(block, near):
    stack = jnp.stack([block] + [swap(block, k) for k in (1, 2, 3)])
    return jnp.concatenate([at(stack, near ^ a) for a in range(NEAR)], axis=1)


def far_sum(block, far_size):
    sent = block.astype(bf16)
    total = sent.astype(f32)
    for k in range(1, far_size):
        total = total + swap(sent, NEAR * k).astype(f32)
    return total


def body(
    tokens,
    pick_flags,
    gate_scales,
    attn_gain,
    query_weight,
    key_weight,
    value_matrix,
    output_weight,
    ffn_gain,
    gate_weight,
    up_weight,
    down_weight,
):
    tok_local, width = tokens.shape
    size = lax.axis_size("ctx")
    far_size = size // NEAR
    me = lax.axis_index("ctx")
    near = me % NEAR
    far = me // NEAR
    picked_count = PICK_DEV * size
    quarter = width // NEAR

    token_ids = jnp.arange(tok_local, dtype=jnp.int32)
    upto = (token_ids[:, None] <= token_ids[None, :]).astype(bf16)
    slot_of = dot(pick_flags.astype(bf16)[None, :], upto).astype(jnp.int32)[0] - 1
    match = (jnp.arange(MOST, dtype=jnp.int32)[:, None] == slot_of[None, :]) & (pick_flags[None, :] == 1)
    hot = match.astype(bf16)
    local_index = jnp.sum(jnp.where(match, token_ids[None, :] + 1, 0), axis=1) - 1
    rows_here = dot(hot, tokens).astype(bf16)
    meta = jnp.broadcast_to(local_index.astype(bf16)[:, None], (MOST, 128))
    parts = jnp.stack([jnp.concatenate((part, meta), axis=1) for part in quarters(rows_here)])

    near_rows = jnp.concatenate([at(parts, near)] + [swap(at(parts, near ^ k), k) for k in (1, 2, 3)], axis=0)
    all_rows = jnp.concatenate([near_rows] + [swap(near_rows, NEAR * k) for k in range(1, far_size)], axis=0)
    slots = size * MOST
    all_index = all_rows[:, quarter].astype(jnp.int32)
    order = jnp.arange(slots, dtype=jnp.int32)
    device_of = (far ^ (order // (NEAR * MOST))) * NEAR + (near ^ (order // MOST % NEAR))
    taken = (all_index >= 0).astype(f32)
    earlier = (device_of[:, None] < device_of[None, :]).astype(f32)
    rank_of = jnp.sum(earlier * taken[:, None], axis=0).astype(jnp.int32) + order % MOST
    pick_ids = jnp.arange(picked_count, dtype=jnp.int32)
    select = (pick_ids[:, None] == rank_of[None, :]) & (all_index >= 0)[None, :]
    token_positions = jnp.sum(jnp.where(select, (device_of * tok_local + all_index)[None, :], 0), axis=1)
    select = select.astype(bf16)
    rows_quarter = dot(select, all_rows[:, :quarter]).astype(bf16)
    picked_rows = near_gather(rows_quarter, near)

    normalized_rows = rms_scale(picked_rows.astype(f32), attn_gain).astype(bf16)
    heads_here = query_weight.shape[1] // HEAD_SIZE
    group_width = QUERY_HEADS // KEY_VALUE_HEADS
    kv_here = max(1, heads_here // group_width)
    kv_weight = jnp.concatenate((key_weight, value_matrix), axis=1)
    kv_cols = jnp.einsum("pd,dc->cp", normalized_rows, kv_weight, preferred_element_type=f32).astype(bf16)
    comps = key_weight.shape[1] // KEY_VALUE_HEADS
    kv_cols = kv_cols.reshape(2, comps, KEY_VALUE_HEADS, picked_count)
    sends = []
    for target in range(size):
        first = target * heads_here // group_width
        sends.append(kv_cols[:, :, first : first + kv_here])
    sends = jnp.stack(sends).reshape(far_size, NEAR, 2 * comps * kv_here, picked_count)
    sends = jnp.transpose(sends, (1, 0, 2, 3))
    got = jnp.stack([at(sends, near)] + [swap(at(sends, near ^ k), k) for k in (1, 2, 3)])
    got = jnp.transpose(got, (1, 0, 2, 3))
    got = jnp.stack([at(got, far)] + [swap(at(got, far ^ k), NEAR * k) for k in range(1, far_size)])
    ordered = jnp.stack(
        [at(at(got, far ^ (d // NEAR)), near ^ (d % NEAR)) for d in range(size)]
    ).reshape(size, 2, comps, kv_here, picked_count)
    ordered = jnp.transpose(ordered, (1, 3, 0, 2, 4)).reshape(2, kv_here, HEAD_SIZE, picked_count)

    half_dim = HEAD_SIZE // 2
    frequency = rope_base ** (-(jnp.arange(half_dim, dtype=f32) * 2.0) / HEAD_SIZE)
    positions = token_positions.astype(f32)
    angles = positions[:, None] * frequency[None, :]
    cosine, sine = jnp.cos(angles), jnp.sin(angles)
    raw_q = dot(normalized_rows, query_weight).reshape(picked_count, heads_here, HEAD_SIZE)
    low, high = raw_q[..., :half_dim], raw_q[..., half_dim:]
    queries = jnp.concatenate(
        (
            low * cosine[:, None, :] - high * sine[:, None, :],
            high * cosine[:, None, :] + low * sine[:, None, :],
        ),
        axis=-1,
    ).astype(bf16)
    raw_k = ordered[0].astype(f32)
    low, high = raw_k[:, :half_dim], raw_k[:, half_dim:]
    keys = jnp.concatenate(
        (low * cosine.T - high * sine.T, high * cosine.T + low * sine.T), axis=1
    ).astype(bf16)
    values = ordered[1]
    shared = heads_here // kv_here
    queries = queries.reshape(picked_count, kv_here, shared, HEAD_SIZE)
    scores = jnp.einsum("qgsd,gdk->gsqk", queries, keys, preferred_element_type=f32) / jnp.sqrt(f32(HEAD_SIZE))
    allowed = pick_ids[None, :] <= pick_ids[:, None]
    scores = jnp.where(allowed, scores, -jnp.inf)
    row_max = jnp.max(scores, axis=-1, keepdims=True)
    exp_terms = jnp.exp(scores - row_max)
    probs = (exp_terms / jnp.sum(exp_terms, axis=-1, keepdims=True)).astype(bf16)
    head_out = jnp.einsum("gsqk,gdk->qgsd", probs, values, preferred_element_type=f32).astype(bf16)
    head_out = head_out.reshape(picked_count, heads_here * HEAD_SIZE)

    attn_quarter = far_sum(near_scatter(dot(head_out, output_weight).astype(bf16), near), far_size)
    mixed_quarter = rows_quarter.astype(f32) + attn_quarter
    mixed = near_gather(mixed_quarter.astype(bf16), near)
    normed_ffn = rms_scale(mixed.astype(f32), ffn_gain).astype(bf16)
    gate_proj = dot(normed_ffn, gate_weight)
    up_proj = dot(normed_ffn, up_weight)
    hidden = (jax.nn.silu(gate_proj) * up_proj).astype(bf16)
    ffn_part = near_scatter(dot(hidden, down_weight).astype(bf16), near).astype(bf16)

    spread = select.reshape(picked_count, far_size, NEAR * MOST)
    delta = dot(spread[:, 0].T, ffn_part) + dot(spread[:, 0].T, attn_quarter.astype(bf16))
    for k in range(1, far_size):
        delta = delta + swap(dot(spread[:, k].T, ffn_part).astype(bf16), NEAR * k).astype(f32)
    delta = delta.astype(bf16).reshape(NEAR, MOST, quarter)
    back = jnp.stack([delta[0]] + [swap(delta[k], k) for k in (1, 2, 3)])
    back = jnp.concatenate([at(back, near ^ a) for a in range(NEAR)], axis=1)
    spread_back = dot(hot.T, back)
    final = tokens.astype(f32) + gate_scales.astype(f32)[:, None] * spread_back
    return jnp.where(pick_flags[:, None] == 1, final.astype(bf16), tokens)


def solution(mesh):
    in_specs = (
        P(("dp", "ctx"), None),
        P(("dp", "ctx")),
        P(("dp", "ctx")),
        P(),
        P(None, "ctx"),
        P(None, "ctx"),
        P(None, "ctx"),
        P("ctx", None),
        P(),
        P(None, "ctx"),
        P(None, "ctx"),
        P("ctx", None),
    )
    out_specs = P(("dp", "ctx"), None)
    return jax.shard_map(body, mesh=mesh, in_specs=in_specs, out_specs=out_specs, check_vma=False)
```

time: 351 us -> 162 us (0.46)
  waiting for transfers between devices: 211 us -> 86.3 us
  blocking collectives: 63.8 us -> 0 us
  starting transfers between devices: 0.35 us -> 37.4 us
  local copies, waits for them, and re-layouts: 18.3 us -> 3.45 us
  between operations: 14.1 us -> 0.57 us
  other arithmetic: 14.8 us -> 4.1 us
    all_gather x3 -> x0, waiting for transfers between devices: 107 us -> none  [the longest x1 39.2 us: body(): normed_ffn = lax.all_gather(normed_own, 'ctx', axis=0, tiled=True)]
    reduce_scatter x2 -> x0, waiting for transfers between devices: 104 us -> none  [the longest x1 62.3 us: body(): lax.psum_scatter(jnp.dot(row_block, output_weight, preferred_element_type...]
    ppermute x0 -> x25, waiting for transfers between devices: none -> 86.3 us  [swap(): return lax.ppermute(value, 'ctx', [(i, i ^ mask) for i in range(size)])]
    ppermute x0 -> x25, starting transfers between devices: none -> 37.4 us  [swap(): return lax.ppermute(value, 'ctx', [(i, i ^ mask) for i in range(size)])]
    unnamed x2 -> x0, blocking collectives: 32.3 us -> none
    all_gather x1 -> x0, blocking collectives: 31.4 us -> none  [body(): kv_all = lax.all_gather(kv_local, 'ctx', axis=0, tiled=True)]
    gather x8 -> x0, local copies, waits for them, and re-layouts: 14.3 us -> none  [the longest x1 4.06 us: body(): picked_rows = all_rows[flat_row]]
    select_n x7 -> x0, other arithmetic: 7.56 us -> none  [the longest x1 4.94 us: body(): picked_rows = all_rows[flat_row]]
  transfers between devices with their start and end apart: 5 -> 25, of which waited for: 5 -> 23; matrix products, arithmetic and copies ran while one was open for 3% -> 1% of each run, Pallas kernels for 0% -> 0%
where the time goes in v1:
time: 162 us
  waiting for transfers between devices  86.3 us (53%)
  starting transfers between devices  37.4 us (23%)
  matrix products  30 us (19%)
  other arithmetic  4.1 us (3%)
  local copies, waits for them, and re-layouts  3.45 us (2%)
    ppermute x25, waiting for transfers between devices, swap(): return lax.ppermute(value, 'ctx', [(i, i ^ mask) for i in range(size)])  86.3 us
    ppermute x25, starting transfers between devices, swap(): return lax.ppermute(value, 'ctx', [(i, i ^ mask) for i in range(size)])  37.4 us
    dot_general x11, matrix products, dot(): return jnp.dot(a, b, preferred_element_type=f32)  27.2 us
  transfers between devices with their start and end apart: 25, of which 23 were waited for; matrix products, arithmetic and copies ran while one was open for 1% of the time, Pallas kernels for 0%

profile of v1, /device:TPU:0, one launch (start us, length us, event | category | flops | bytes accessed | tf_op | source)
XLA Modules:
  0.0 161.9 jit_solution(10436125948197815970)
XLA Ops:
  1.6 1.5 convolution_convert_fusion.2
  3.3 4.0 %collective-permute-start.2 = (bf16[32,1152]{1,0:T(8,128)(2,1)S(1)}, bf16[32,1152]{1,0:T(8,128)(2,1)S(1)}, u32[]{:S(2)}, u32[]{:S(2)}) collective-permute-start(bf16[32,1152]{1,0:T(8,128)(2,1)S(1)} %get-tuple-element.31), channel_id=1, source_target_pairs={{0,3},{1,2},{2,1},{3,0},{4,7},{5,6},{6,5},{7,4},{8,11},{9,10},{10,... | collective-permute-start | bytes 221192 | tf_op jit(solution)/shard_map/ppermute | solution.py:22
  8.1 1.9 %collective-permute-done.2 = bf16[32,1152]{1,0:T(8,128)(2,1)S(1)} collective-permute-done((bf16[32,1152]{1,0:T(8,128)(2,1)S(1)}, bf16[32,1152]{1,0:T(8,128)(2,1)S(1)}, u32[]{:S(2)}, u32[]{:S(2)}) %collective-permute-start.2) | collective-permute-done | bytes 73760 | tf_op jit(solution)/shard_map/ppermute | solution.py:22
  10.0 1.7 %collective-permute-done.1 = bf16[32,1152]{1,0:T(8,128)(2,1)S(1)} collective-permute-done((bf16[32,1152]{1,0:T(8,128)(2,1)S(1)}, bf16[32,1152]{1,0:T(8,128)(2,1)S(1)}, u32[]{:S(2)}, u32[]{:S(2)}) %collective-permute-start.1) | collective-permute-done | bytes 73760 | tf_op jit(solution)/shard_map/ppermute | solution.py:22
  12.2 2.7 %collective-permute-start.3 = (bf16[128,1152]{1,0:T(8,128)(2,1)S(1)}, bf16[128,1152]{1,0:T(8,128)(2,1)S(1)}, u32[]{:S(2)}, u32[]{:S(2)}) collective-permute-start(bf16[128,1152]{1,0:T(8,128)(2,1)S(1)} %pad_maximum_fusion.7), channel_id=1, source_target_pairs={{0,4},{1,5},{2,6},{3,7},{4,0},{5,1},{6,2},{7,3},{8,12},{9,13},{10,... | collective-permute-start | bytes 884744 | tf_op jit(solution)/shard_map/ppermute | solution.py:22
  14.9 12.4 %collective-permute-done.3 = bf16[128,1152]{1,0:T(8,128)(2,1)S(1)} collective-permute-done((bf16[128,1152]{1,0:T(8,128)(2,1)S(1)}, bf16[128,1152]{1,0:T(8,128)(2,1)S(1)}, u32[]{:S(2)}, u32[]{:S(2)}) %collective-permute-start.3) | collective-permute-done | bytes 294944 | tf_op jit(solution)/shard_map/ppermute | solution.py:22
  29.0 1.6 collective-permute-start.5
  32.0 6.2 %collective-permute-done.6 = bf16[128,1024]{1,0:T(8,128)(2,1)S(1)} collective-permute-done((bf16[128,1024]{1,0:T(8,128)(2,1)S(1)}, bf16[128,1024]{1,0:T(8,128)(2,1)S(1)}, u32[]{:S(2)}, u32[]{:S(2)}) %collective-permute-start.6) | collective-permute-done | bytes 262176 | tf_op jit(solution)/shard_map/ppermute | solution.py:22
  38.2 3.5 %collective-permute-done.5 = bf16[128,1024]{1,0:T(8,128)(2,1)S(1)} collective-permute-done((bf16[128,1024]{1,0:T(8,128)(2,1)S(1)}, bf16[128,1024]{1,0:T(8,128)(2,1)S(1)}, u32[]{:S(2)}, u32[]{:S(2)}) %collective-permute-start.5) | collective-permute-done | bytes 262176 | tf_op jit(solution)/shard_map/ppermute | solution.py:22
  42.3 1.6 %copy-done.1 = bf16[4096,512]{1,0:T(8,128)(2,1)S(1)} copy-done((bf16[4096,512]{1,0:T(8,128)(2,1)S(1)}, bf16[4096,512]{1,0:T(8,128)(2,1)}, u32[]{:S(2)}) %copy-start.1) | copy-done | bytes 4194328
  44.8 2.3 %fusion.18 = bf16[256,128]{1,0:T(8,128)(2,1)S(1)} fusion(bf16[4096,128]{1,0:T(8,128)(2,1)} %param.18, bf16[4096,128]{1,0:T(8,128)(2,1)} %param.17, f32[4096]{0:T(1024)S(1)} %copy-done.2, f32[128]{0:T(128)S(1)} %add_rsqrt_fusion.1, bf16[128,1024]{1,0:T(8,128)(2,1)S(1)} %get-tuple-element.26, bf16[128,1024]{1,0:T(8,128)(2,1)S(1)} %get-tuple-element.27, ...), kind=kOutput, calls=%fused_computation.32 | convolution fusion | flops 278429696 | bytes 3228160 | tf_op jit(solution)/shard_map/pd,dc->cp/dot_general | solution.py:118
  47.4 2.0 %collective-permute-start.9 = (bf16[2,32,128]{2,1,0:T(8,128)(2,1)S(1)}, bf16[2,32,128]{2,1,0:T(8,128)(2,1)S(1)}, u32[]{:S(2)}, u32[]{:S(2)}) collective-permute-start(bf16[2,32,128]{2,1,0:T(8,128)(2,1)S(1)} %get-tuple-element.63), channel_id=1, source_target_pairs={{0,3},{1,2},{2,1},{3,0},{4,7},{5,6},{6,5},{7,4},{8,11},{9,10},{10,... | collective-permute-start | bytes 49160 | tf_op jit(solution)/shard_map/ppermute | solution.py:22
  54.2 2.6 %collective-permute-start.10 = (bf16[4,32,128]{2,1,0:T(8,128)(2,1)S(1)}, bf16[4,32,128]{2,1,0:T(8,128)(2,1)S(1)}, u32[]{:S(2)}, u32[]{:S(2)}) collective-permute-start(bf16[4,32,128]{2,1,0:T(8,128)(2,1)S(1)} %get-tuple-element.60), channel_id=1, source_target_pairs={{0,4},{1,5},{2,6},{3,7},{4,0},{5,1},{6,2},{7,3},{8,12},{9,13},{10,... | collective-permute-start | bytes 98312 | tf_op jit(solution)/shard_map/ppermute | solution.py:22
  56.8 2.2 %collective-permute-done.10 = bf16[4,32,128]{2,1,0:T(8,128)(2,1)S(1)} collective-permute-done((bf16[4,32,128]{2,1,0:T(8,128)(2,1)S(1)}, bf16[4,32,128]{2,1,0:T(8,128)(2,1)S(1)}, u32[]{:S(2)}, u32[]{:S(2)}) %collective-permute-start.10) | collective-permute-done | bytes 32800 | tf_op jit(solution)/shard_map/ppermute | solution.py:22
  60.3 2.9 %convolution_convert_fusion.1 = bf16[128,4096]{1,0:T(8,128)(2,1)S(1)} fusion(bf16[128,512]{0,1:T(8,128)(2,1)S(1)} %bitcast.216, bf16[512,4096]{1,0:T(8,128)(2,1)} %param.19), kind=kOutput, calls=%fused_computation.4 | convolution fusion | flops 537395200 | bytes 5373952 | tf_op jit(solution)/shard_map/dot_general | solution.py:30
  63.6 2.3 %collective-permute-start.11 = (bf16[128,1024]{1,0:T(8,128)(2,1)S(1)}, bf16[128,1024]{1,0:T(8,128)(2,1)S(1)}, u32[]{:S(2)}, u32[]{:S(2)}) collective-permute-start(bf16[128,1024]{1,0:T(8,128)(2,1)S(1)} %get-tuple-element.18), channel_id=1, source_target_pairs={{0,3},{1,2},{2,1},{3,0},{4,7},{5,6},{6,5},{7,4},{8,11},{9,10},{10,... | collective-permute-start | bytes 786440 | tf_op jit(solution)/shard_map/ppermute | solution.py:22
  67.1 5.8 %collective-permute-done.11 = bf16[128,1024]{1,0:T(8,128)(2,1)S(1)} collective-permute-done((bf16[128,1024]{1,0:T(8,128)(2,1)S(1)}, bf16[128,1024]{1,0:T(8,128)(2,1)S(1)}, u32[]{:S(2)}, u32[]{:S(2)}) %collective-permute-start.11) | collective-permute-done | bytes 262176 | tf_op jit(solution)/shard_map/ppermute | solution.py:22
  72.9 2.5 %collective-permute-done.13 = bf16[128,1024]{1,0:T(8,128)(2,1)S(1)} collective-permute-done((bf16[128,1024]{1,0:T(8,128)(2,1)S(1)}, bf16[128,1024]{1,0:T(8,128)(2,1)S(1)}, u32[]{:S(2)}, u32[]{:S(2)}) %collective-permute-start.13) | collective-permute-done | bytes 262176 | tf_op jit(solution)/shard_map/ppermute | solution.py:22
  75.8 2.7 %collective-permute-start.14 = (bf16[128,1024]{1,0:T(8,128)(2,1)S(1)}, bf16[128,1024]{1,0:T(8,128)(2,1)S(1)}, u32[]{:S(2)}, u32[]{:S(2)}) collective-permute-start(bf16[128,1024]{1,0:T(8,128)(2,1)S(1)} %fusion.29), channel_id=1, source_target_pairs={{0,4},{1,5},{2,6},{3,7},{4,0},{5,1},{6,2},{7,3},{8,12},{9,13},{10,... | collective-permute-start | bytes 786440 | tf_op jit(solution)/shard_map/ppermute | solution.py:22
  78.5 10.5 %collective-permute-done.14 = bf16[128,1024]{1,0:T(8,128)(2,1)S(1)} collective-permute-done((bf16[128,1024]{1,0:T(8,128)(2,1)S(1)}, bf16[128,1024]{1,0:T(8,128)(2,1)S(1)}, u32[]{:S(2)}, u32[]{:S(2)}) %collective-permute-start.14) | collective-permute-done | bytes 262176 | tf_op jit(solution)/shard_map/ppermute | solution.py:22
  89.1 1.7 %collective-permute-start.17 = (bf16[128,1024]{1,0:T(8,128)(2,1)S(1)}, bf16[128,1024]{1,0:T(8,128)(2,1)S(1)}, u32[]{:S(2)}, u32[]{:S(2)}) collective-permute-start(bf16[128,1024]{1,0:T(8,128)(2,1)S(1)} %add_convert_fusion), channel_id=1, source_target_pairs={{0,3},{1,2},{2,1},{3,0},{4,7},{5,6},{6,5},{7,4},{8,11},{9,10},{10,... | collective-permute-start | bytes 786440 | tf_op jit(solution)/shard_map/ppermute | solution.py:22
  92.7 6.7 %collective-permute-done.17 = bf16[128,1024]{1,0:T(8,128)(2,1)S(1)} collective-permute-done((bf16[128,1024]{1,0:T(8,128)(2,1)S(1)}, bf16[128,1024]{1,0:T(8,128)(2,1)S(1)}, u32[]{:S(2)}, u32[]{:S(2)}) %collective-permute-start.17) | collective-permute-done | bytes 262176 | tf_op jit(solution)/shard_map/ppermute | solution.py:22
  99.4 3.4 %collective-permute-done.16 = bf16[128,1024]{1,0:T(8,128)(2,1)S(1)} collective-permute-done((bf16[128,1024]{1,0:T(8,128)(2,1)S(1)}, bf16[128,1024]{1,0:T(8,128)(2,1)S(1)}, u32[]{:S(2)}, u32[]{:S(2)}) %collective-permute-start.16) | collective-permute-done | bytes 262176 | tf_op jit(solution)/shard_map/ppermute | solution.py:22
  103.8 7.0 %fusion.34 = f32[128,1408]{1,0:T(8,128)} fusion(bf16[4096,1408]{1,0:T(8,128)(2,1)} %param.21, f32[4096]{0:T(1024)S(1)} %copy-done.3, f32[128]{0:T(128)S(1)} %add_rsqrt_fusion, bf16[128,1024]{1,0:T(8,128)(2,1)S(1)} %get-tuple-element.15, bf16[128,1024]{1,0:T(8,128)(2,1)S(1)} %get-tuple-element.16, bf16[128,1024]{1,0:T(8,128)(2,1)S(1)} %get-tuple-element.17, ...), kind=kOutput, calls=%fused_computation.55 | convolution fusion | flops 1482162176 | bytes 13320704 | tf_op jit(solution)/shard_map/dot_general | solution.py:30
  110.8 11.6 %convolution_convert_fusion = bf16[128,4096]{1,0:T(8,128)(2,1)S(1)} fusion(bf16[1408,4096]{1,0:T(8,128)(2,1)} %param.23, bf16[4096,1408]{1,0:T(8,128)(2,1)} %param.22, f32[128,1408]{1,0:T(8,128)} %fusion.34, f32[4096]{0:T(1024)S(1)} %copy-done.3, f32[128]{0:T(128)S(1)} %add_rsqrt_fusion, bf16[128,1024]{1,0:T(8,128)(2,1)S(1)} %get-tuple-element.15, ...), kind=kOutput, calls=%fused_computation.3 | convolution fusion | flops 2960162816 | bytes 25903616 | tf_op jit(solution)/shard_map/dot_general | solution.py:30
  122.7 2.7 %collective-permute-start.18 = (bf16[128,1024]{1,0:T(8,128)(2,1)S(1)}, bf16[128,1024]{1,0:T(8,128)(2,1)S(1)}, u32[]{:S(2)}, u32[]{:S(2)}) collective-permute-start(bf16[128,1024]{1,0:T(8,128)(2,1)S(1)} %get-tuple-element.7), channel_id=1, source_target_pairs={{0,3},{1,2},{2,1},{3,0},{4,7},{5,6},{6,5},{7,4},{8,11},{9,10},{10,... | collective-permute-start | bytes 786440 | tf_op jit(solution)/shard_map/ppermute | solution.py:22
  126.4 6.5 %collective-permute-done.18 = bf16[128,1024]{1,0:T(8,128)(2,1)S(1)} collective-permute-done((bf16[128,1024]{1,0:T(8,128)(2,1)S(1)}, bf16[128,1024]{1,0:T(8,128)(2,1)S(1)}, u32[]{:S(2)}, u32[]{:S(2)}) %collective-permute-start.18) | collective-permute-done | bytes 262176 | tf_op jit(solution)/shard_map/ppermute | solution.py:22
  132.9 4.5 %collective-permute-done.20 = bf16[128,1024]{1,0:T(8,128)(2,1)S(1)} collective-permute-done((bf16[128,1024]{1,0:T(8,128)(2,1)S(1)}, bf16[128,1024]{1,0:T(8,128)(2,1)S(1)}, u32[]{:S(2)}, u32[]{:S(2)}) %collective-permute-start.20) | collective-permute-done | bytes 262176 | tf_op jit(solution)/shard_map/ppermute | solution.py:22
  138.0 3.4 %collective-permute-start.21 = (bf16[128,1024]{1,0:T(8,128)(2,1)S(1)}, bf16[128,1024]{1,0:T(8,128)(2,1)S(1)}, u32[]{:S(2)}, u32[]{:S(2)}) collective-permute-start(bf16[128,1024]{1,0:T(8,128)(2,1)S(1)} %convolution_convert_fusion.3), channel_id=1, source_target_pairs={{0,4},{1,5},{2,6},{3,7},{4,0},{5,1},{6,2},{7,3},{8,12},{9,13},{10,... | collective-permute-start | bytes 786440 | tf_op jit(solution)/shard_map/ppermute | solution.py:22
  141.7 11.8 %collective-permute-done.21 = bf16[128,1024]{1,0:T(8,128)(2,1)S(1)} collective-permute-done((bf16[128,1024]{1,0:T(8,128)(2,1)S(1)}, bf16[128,1024]{1,0:T(8,128)(2,1)S(1)}, u32[]{:S(2)}, u32[]{:S(2)}) %collective-permute-start.21) | collective-permute-done | bytes 262176 | tf_op jit(solution)/shard_map/ppermute | solution.py:22
  157.4 1.9 %collective-permute-done.24 = bf16[32,1024]{1,0:T(8,128)(2,1)S(1)} collective-permute-done((bf16[32,1024]{1,0:T(8,128)(2,1)S(1)}, bf16[32,1024]{1,0:T(8,128)(2,1)S(1)}, u32[]{:S(2)}, u32[]{:S(2)}) %collective-permute-start.24) | collective-permute-done | bytes 65568 | tf_op jit(solution)/shard_map/ppermute | solution.py:22
  160.3 1.5 fusion.2
  (124 shorter events, 25.4 us)
Async XLA Ops:
  3.3 6.7 %collective-permute-start.2 = (bf16[32,1152]{1,0:T(8,128)(2,1)S(1)}, bf16[32,1152]{1,0:T(8,128)(2,1)S(1)}, u32[]{:S(2)}, u32[]{:S(2)}) collective-permute-start(bf16[32,1152]{1,0:T(8,128)(2,1)S(1)} %get-tuple-element.31), channel_id=1, source_target_pairs={{0,3},{1,2},{2,1},{3,0},{4,7},{5,6},{6,5},{7,4},{8,11},{9,10},{10,... | collective-permute-start | bytes 221192 | tf_op jit(solution)/shard_map/ppermute | solution.py:22
  7.4 4.4 %collective-permute-start.1 = (bf16[32,1152]{1,0:T(8,128)(2,1)S(1)}, bf16[32,1152]{1,0:T(8,128)(2,1)S(1)}, u32[]{:S(2)}, u32[]{:S(2)}) collective-permute-start(bf16[32,1152]{1,0:T(8,128)(2,1)S(1)} %get-tuple-element.32), channel_id=1, source_target_pairs={{0,2},{1,3},{2,0},{3,1},{4,6},{5,7},{6,4},{7,5},{8,10},{9,11},{10,... | collective-permute-start | bytes 221192 | tf_op jit(solution)/shard_map/ppermute | solution.py:22
  7.8 4.4 %collective-permute-start = (bf16[32,1152]{1,0:T(8,128)(2,1)S(1)}, bf16[32,1152]{1,0:T(8,128)(2,1)S(1)}, u32[]{:S(2)}, u32[]{:S(2)}) collective-permute-start(bf16[32,1152]{1,0:T(8,128)(2,1)S(1)} %get-tuple-element.33), channel_id=1, source_target_pairs={{0,1},{1,0},{2,3},{3,2},{4,5},{5,4},{6,7},{7,6},{8,9},{9,8},{10,11... | collective-permute-start | bytes 221192 | tf_op jit(solution)/shard_map/ppermute | solution.py:22
  12.2 15.1 %collective-permute-start.3 = (bf16[128,1152]{1,0:T(8,128)(2,1)S(1)}, bf16[128,1152]{1,0:T(8,128)(2,1)S(1)}, u32[]{:S(2)}, u32[]{:S(2)}) collective-permute-start(bf16[128,1152]{1,0:T(8,128)(2,1)S(1)} %pad_maximum_fusion.7), channel_id=1, source_target_pairs={{0,4},{1,5},{2,6},{3,7},{4,0},{5,1},{6,2},{7,3},{8,12},{9,13},{10,... | collective-permute-start | bytes 884744 | tf_op jit(solution)/shard_map/ppermute | solution.py:22
  28.0 10.2 %collective-permute-start.6 = (bf16[128,1024]{1,0:T(8,128)(2,1)S(1)}, bf16[128,1024]{1,0:T(8,128)(2,1)S(1)}, u32[]{:S(2)}, u32[]{:S(2)}) collective-permute-start(bf16[128,1024]{1,0:T(8,128)(2,1)S(1)} %convolution_convert_fusion.4), channel_id=1, source_target_pairs={{0,3},{1,2},{2,1},{3,0},{4,7},{5,6},{6,5},{7,4},{8,11},{9,10},{10,... | collective-permute-start | bytes 786440 | tf_op jit(solution)/shard_map/ppermute | solution.py:22
  29.0 12.7 %collective-permute-start.5 = (bf16[128,1024]{1,0:T(8,128)(2,1)S(1)}, bf16[128,1024]{1,0:T(8,128)(2,1)S(1)}, u32[]{:S(2)}, u32[]{:S(2)}) collective-permute-start(bf16[128,1024]{1,0:T(8,128)(2,1)S(1)} %convolution_convert_fusion.4), channel_id=1, source_target_pairs={{0,2},{1,3},{2,0},{3,1},{4,6},{5,7},{6,4},{7,5},{8,10},{9,11},{10,... | collective-permute-start | bytes 786440 | tf_op jit(solution)/shard_map/ppermute | solution.py:22
  30.6 11.1 %collective-permute-start.4 = (bf16[128,1024]{1,0:T(8,128)(2,1)S(1)}, bf16[128,1024]{1,0:T(8,128)(2,1)S(1)}, u32[]{:S(2)}, u32[]{:S(2)}) collective-permute-start(bf16[128,1024]{1,0:T(8,128)(2,1)S(1)} %convolution_convert_fusion.4), channel_id=1, source_target_pairs={{0,1},{1,0},{2,3},{3,2},{4,5},{5,4},{6,7},{7,6},{8,9},{9,8},{10,11... | collective-permute-start | bytes 786440 | tf_op jit(solution)/shard_map/ppermute | solution.py:22
  41.8 2.2 %copy-start.1 = (bf16[4096,512]{1,0:T(8,128)(2,1)S(1)}, bf16[4096,512]{1,0:T(8,128)(2,1)}, u32[]{:S(2)}) copy-start(bf16[4096,512]{1,0:T(8,128)(2,1)} %param.16) | copy-start | bytes 12582916
  41.9 2.1 %copy-start.2 = (f32[4096]{0:T(1024)S(1)}, f32[4096]{0:T(1024)}, u32[]{:S(2)}) copy-start(f32[4096]{0:T(1024)} %param.15) | copy-start | bytes 49156
  47.4 4.7 %collective-permute-start.9 = (bf16[2,32,128]{2,1,0:T(8,128)(2,1)S(1)}, bf16[2,32,128]{2,1,0:T(8,128)(2,1)S(1)}, u32[]{:S(2)}, u32[]{:S(2)}) collective-permute-start(bf16[2,32,128]{2,1,0:T(8,128)(2,1)S(1)} %get-tuple-element.63), channel_id=1, source_target_pairs={{0,3},{1,2},{2,1},{3,0},{4,7},{5,6},{6,5},{7,4},{8,11},{9,10},{10,... | collective-permute-start | bytes 49160 | tf_op jit(solution)/shard_map/ppermute | solution.py:22
  49.4 3.7 %collective-permute-start.8 = (bf16[2,32,128]{2,1,0:T(8,128)(2,1)S(1)}, bf16[2,32,128]{2,1,0:T(8,128)(2,1)S(1)}, u32[]{:S(2)}, u32[]{:S(2)}) collective-permute-start(bf16[2,32,128]{2,1,0:T(8,128)(2,1)S(1)} %get-tuple-element.64), channel_id=1, source_target_pairs={{0,2},{1,3},{2,0},{3,1},{4,6},{5,7},{6,4},{7,5},{8,10},{9,11},{10,... | collective-permute-start | bytes 49160 | tf_op jit(solution)/shard_map/ppermute | solution.py:22
  50.4 3.7 %collective-permute-start.7 = (bf16[2,32,128]{2,1,0:T(8,128)(2,1)S(1)}, bf16[2,32,128]{2,1,0:T(8,128)(2,1)S(1)}, u32[]{:S(2)}, u32[]{:S(2)}) collective-permute-start(bf16[2,32,128]{2,1,0:T(8,128)(2,1)S(1)} %get-tuple-element.65), channel_id=1, source_target_pairs={{0,1},{1,0},{2,3},{3,2},{4,5},{5,4},{6,7},{7,6},{8,9},{9,8},{10,11... | collective-permute-start | bytes 49160 | tf_op jit(solution)/shard_map/ppermute | solution.py:22
  54.2 4.9 %collective-permute-start.10 = (bf16[4,32,128]{2,1,0:T(8,128)(2,1)S(1)}, bf16[4,32,128]{2,1,0:T(8,128)(2,1)S(1)}, u32[]{:S(2)}, u32[]{:S(2)}) collective-permute-start(bf16[4,32,128]{2,1,0:T(8,128)(2,1)S(1)} %get-tuple-element.60), channel_id=1, source_target_pairs={{0,4},{1,5},{2,6},{3,7},{4,0},{5,1},{6,2},{7,3},{8,12},{9,13},{10,... | collective-permute-start | bytes 98312 | tf_op jit(solution)/shard_map/ppermute | solution.py:22
  63.6 9.3 %collective-permute-start.11 = (bf16[128,1024]{1,0:T(8,128)(2,1)S(1)}, bf16[128,1024]{1,0:T(8,128)(2,1)S(1)}, u32[]{:S(2)}, u32[]{:S(2)}) collective-permute-start(bf16[128,1024]{1,0:T(8,128)(2,1)S(1)} %get-tuple-element.18), channel_id=1, source_target_pairs={{0,3},{1,2},{2,1},{3,0},{4,7},{5,6},{6,5},{7,4},{8,11},{9,10},{10,... | collective-permute-start | bytes 786440 | tf_op jit(solution)/shard_map/ppermute | solution.py:22
  65.9 9.6 %collective-permute-start.13 = (bf16[128,1024]{1,0:T(8,128)(2,1)S(1)}, bf16[128,1024]{1,0:T(8,128)(2,1)S(1)}, u32[]{:S(2)}, u32[]{:S(2)}) collective-permute-start(bf16[128,1024]{1,0:T(8,128)(2,1)S(1)} %get-tuple-element.19), channel_id=1, source_target_pairs={{0,2},{1,3},{2,0},{3,1},{4,6},{5,7},{6,4},{7,5},{8,10},{9,11},{10,... | collective-permute-start | bytes 786440 | tf_op jit(solution)/shard_map/ppermute | solution.py:22
  65.9 9.7 %collective-permute-start.12 = (bf16[128,1024]{1,0:T(8,128)(2,1)S(1)}, bf16[128,1024]{1,0:T(8,128)(2,1)S(1)}, u32[]{:S(2)}, u32[]{:S(2)}) collective-permute-start(bf16[128,1024]{1,0:T(8,128)(2,1)S(1)} %get-tuple-element.20), channel_id=1, source_target_pairs={{0,1},{1,0},{2,3},{3,2},{4,5},{5,4},{6,7},{7,6},{8,9},{9,8},{10,11... | collective-permute-start | bytes 786440 | tf_op jit(solution)/shard_map/ppermute | solution.py:22
  75.8 13.2 %collective-permute-start.14 = (bf16[128,1024]{1,0:T(8,128)(2,1)S(1)}, bf16[128,1024]{1,0:T(8,128)(2,1)S(1)}, u32[]{:S(2)}, u32[]{:S(2)}) collective-permute-start(bf16[128,1024]{1,0:T(8,128)(2,1)S(1)} %fusion.29), channel_id=1, source_target_pairs={{0,4},{1,5},{2,6},{3,7},{4,0},{5,1},{6,2},{7,3},{8,12},{9,13},{10,... | collective-permute-start | bytes 786440 | tf_op jit(solution)/shard_map/ppermute | solution.py:22
  89.1 10.3 %collective-permute-start.17 = (bf16[128,1024]{1,0:T(8,128)(2,1)S(1)}, bf16[128,1024]{1,0:T(8,128)(2,1)S(1)}, u32[]{:S(2)}, u32[]{:S(2)}) collective-permute-start(bf16[128,1024]{1,0:T(8,128)(2,1)S(1)} %add_convert_fusion), channel_id=1, source_target_pairs={{0,3},{1,2},{2,1},{3,0},{4,7},{5,6},{6,5},{7,4},{8,11},{9,10},{10,... | collective-permute-start | bytes 786440 | tf_op jit(solution)/shard_map/ppermute | solution.py:22
  90.8 12.0 %collective-permute-start.16 = (bf16[128,1024]{1,0:T(8,128)(2,1)S(1)}, bf16[128,1024]{1,0:T(8,128)(2,1)S(1)}, u32[]{:S(2)}, u32[]{:S(2)}) collective-permute-start(bf16[128,1024]{1,0:T(8,128)(2,1)S(1)} %add_convert_fusion), channel_id=1, source_target_pairs={{0,2},{1,3},{2,0},{3,1},{4,6},{5,7},{6,4},{7,5},{8,10},{9,11},{10,... | collective-permute-start | bytes 786440 | tf_op jit(solution)/shard_map/ppermute | solution.py:22
  92.2 10.7 %collective-permute-start.15 = (bf16[128,1024]{1,0:T(8,128)(2,1)S(1)}, bf16[128,1024]{1,0:T(8,128)(2,1)S(1)}, u32[]{:S(2)}, u32[]{:S(2)}) collective-permute-start(bf16[128,1024]{1,0:T(8,128)(2,1)S(1)} %add_convert_fusion), channel_id=1, source_target_pairs={{0,1},{1,0},{2,3},{3,2},{4,5},{5,4},{6,7},{7,6},{8,9},{9,8},{10,11... | collective-permute-start | bytes 786440 | tf_op jit(solution)/shard_map/ppermute | solution.py:22
  103.0 0.7 copy-start.3
  122.7 10.2 %collective-permute-start.18 = (bf16[128,1024]{1,0:T(8,128)(2,1)S(1)}, bf16[128,1024]{1,0:T(8,128)(2,1)S(1)}, u32[]{:S(2)}, u32[]{:S(2)}) collective-permute-start(bf16[128,1024]{1,0:T(8,128)(2,1)S(1)} %get-tuple-element.7), channel_id=1, source_target_pairs={{0,3},{1,2},{2,1},{3,0},{4,7},{5,6},{6,5},{7,4},{8,11},{9,10},{10,... | collective-permute-start | bytes 786440 | tf_op jit(solution)/shard_map/ppermute | solution.py:22
  125.4 12.0 %collective-permute-start.20 = (bf16[128,1024]{1,0:T(8,128)(2,1)S(1)}, bf16[128,1024]{1,0:T(8,128)(2,1)S(1)}, u32[]{:S(2)}, u32[]{:S(2)}) collective-permute-start(bf16[128,1024]{1,0:T(8,128)(2,1)S(1)} %get-tuple-element.8), channel_id=1, source_target_pairs={{0,2},{1,3},{2,0},{3,1},{4,6},{5,7},{6,4},{7,5},{8,10},{9,11},{10,... | collective-permute-start | bytes 786440 | tf_op jit(solution)/shard_map/ppermute | solution.py:22
  125.6 11.9 %collective-permute-start.19 = (bf16[128,1024]{1,0:T(8,128)(2,1)S(1)}, bf16[128,1024]{1,0:T(8,128)(2,1)S(1)}, u32[]{:S(2)}, u32[]{:S(2)}) collective-permute-start(bf16[128,1024]{1,0:T(8,128)(2,1)S(1)} %get-tuple-element.9), channel_id=1, source_target_pairs={{0,1},{1,0},{2,3},{3,2},{4,5},{5,4},{6,7},{7,6},{8,9},{9,8},{10,11... | collective-permute-start | bytes 786440 | tf_op jit(solution)/shard_map/ppermute | solution.py:22
  126.4 31.0 %copy-start.4 = (bf16[128]{0:T(256)(128)(2,1)S(1)}, bf16[128]{0:T(256)(128)(2,1)}, u32[]{:S(2)}) copy-start(bf16[128]{0:T(256)(128)(2,1)} %param.14) | copy-start | bytes 772
  138.0 22.3 %copy-start = (bf16[128,4096]{1,0:T(8,128)(2,1)S(1)}, bf16[128,4096]{1,0:T(8,128)(2,1)}, u32[]{:S(2)}) copy-start(bf16[128,4096]{1,0:T(8,128)(2,1)} %param.12) | copy-start | bytes 3145732
  138.0 15.5 %collective-permute-start.21 = (bf16[128,1024]{1,0:T(8,128)(2,1)S(1)}, bf16[128,1024]{1,0:T(8,128)(2,1)S(1)}, u32[]{:S(2)}, u32[]{:S(2)}) collective-permute-start(bf16[128,1024]{1,0:T(8,128)(2,1)S(1)} %convolution_convert_fusion.3), channel_id=1, source_target_pairs={{0,4},{1,5},{2,6},{3,7},{4,0},{5,1},{6,2},{7,3},{8,12},{9,13},{10,... | collective-permute-start | bytes 786440 | tf_op jit(solution)/shard_map/ppermute | solution.py:22
  153.9 5.4 %collective-permute-start.24 = (bf16[32,1024]{1,0:T(8,128)(2,1)S(1)}, bf16[32,1024]{1,0:T(8,128)(2,1)S(1)}, u32[]{:S(2)}, u32[]{:S(2)}) collective-permute-start(bf16[32,1024]{1,0:T(8,128)(2,1)S(1)} %get-tuple-element.39), channel_id=1, source_target_pairs={{0,3},{1,2},{2,1},{3,0},{4,7},{5,6},{6,5},{7,4},{8,11},{9,10},{10,... | collective-permute-start | bytes 196616 | tf_op jit(solution)/shard_map/ppermute | solution.py:22
  154.6 4.7 %collective-permute-start.23 = (bf16[32,1024]{1,0:T(8,128)(2,1)S(1)}, bf16[32,1024]{1,0:T(8,128)(2,1)S(1)}, u32[]{:S(2)}, u32[]{:S(2)}) collective-permute-start(bf16[32,1024]{1,0:T(8,128)(2,1)S(1)} %get-tuple-element.40), channel_id=1, source_target_pairs={{0,2},{1,3},{2,0},{3,1},{4,6},{5,7},{6,4},{7,5},{8,10},{9,11},{10,... | collective-permute-start | bytes 196616 | tf_op jit(solution)/shard_map/ppermute | solution.py:22
  156.0 4.3 %collective-permute-start.22 = (bf16[32,1024]{1,0:T(8,128)(2,1)S(1)}, bf16[32,1024]{1,0:T(8,128)(2,1)S(1)}, u32[]{:S(2)}, u32[]{:S(2)}) collective-permute-start(bf16[32,1024]{1,0:T(8,128)(2,1)S(1)} %get-tuple-element.41), channel_id=1, source_target_pairs={{0,1},{1,0},{2,3},{3,2},{4,5},{5,4},{6,7},{7,6},{8,9},{9,8},{10,11... | collective-permute-start | bytes 196616 | tf_op jit(solution)/shard_map/ppermute | solution.py:22

commit v2 on v1

--- a/solution.py
+++ b/solution.py
@@ -22,6 +22,14 @@
     return lax.ppermute(value, "ctx", [(i, i ^ mask) for i in range(size)])
 
 
+def far_mask(k):
+    return NEAR * k ^ (k & 1) * 2
+
+
+def quarter_of(device):
+    return (device & 3) ^ ((device // NEAR & 1) * 2)
+
+
 def at(stack, index):
     return lax.dynamic_index_in_dim(stack, index, 0, keepdims=False)
 
@@ -57,7 +65,7 @@
     sent = block.astype(bf16)
     total = sent.astype(f32)
     for k in range(1, far_size):
-        total = total + swap(sent, NEAR * k).astype(f32)
+        total = total + swap(sent, far_mask(k)).astype(f32)
     return total
 
 
@@ -79,8 +87,8 @@
     size = lax.axis_size("ctx")
     far_size = size // NEAR
     me = lax.axis_index("ctx")
-    near = me % NEAR
     far = me // NEAR
+    near = quarter_of(me)
     picked_count = PICK_DEV * size
     quarter = width // NEAR
 
@@ -95,11 +103,12 @@
     parts = jnp.stack([jnp.concatenate((part, meta), axis=1) for part in quarters(rows_here)])
 
     near_rows = jnp.concatenate([at(parts, near)] + [swap(at(parts, near ^ k), k) for k in (1, 2, 3)], axis=0)
-    all_rows = jnp.concatenate([near_rows] + [swap(near_rows, NEAR * k) for k in range(1, far_size)], axis=0)
+    all_rows = jnp.concatenate([near_rows] + [swap(near_rows, far_mask(k)) for k in range(1, far_size)], axis=0)
     slots = size * MOST
     all_index = all_rows[:, quarter].astype(jnp.int32)
     order = jnp.arange(slots, dtype=jnp.int32)
-    device_of = (far ^ (order // (NEAR * MOST))) * NEAR + (near ^ (order // MOST % NEAR))
+    far_of = far ^ (order // (NEAR * MOST))
+    device_of = far_of * NEAR + (near ^ (order // MOST % NEAR) ^ (far_of & 1) * 2)
     taken = (all_index >= 0).astype(f32)
     earlier = (device_of[:, None] < device_of[None, :]).astype(f32)
     rank_of = jnp.sum(earlier * taken[:, None], axis=0).astype(jnp.int32) + order % MOST
@@ -119,16 +128,17 @@
     comps = key_weight.shape[1] // KEY_VALUE_HEADS
     kv_cols = kv_cols.reshape(2, comps, KEY_VALUE_HEADS, picked_count)
     sends = []
-    for target in range(size):
-        first = target * heads_here // group_width
-        sends.append(kv_cols[:, :, first : first + kv_here])
-    sends = jnp.stack(sends).reshape(far_size, NEAR, 2 * comps * kv_here, picked_count)
-    sends = jnp.transpose(sends, (1, 0, 2, 3))
+    for label in range(NEAR):
+        for group in range(far_size):
+            target = group * NEAR + (label ^ (group & 1) * 2)
+            first = target * heads_here // group_width
+            sends.append(kv_cols[:, :, first : first + kv_here])
+    sends = jnp.stack(sends).reshape(NEAR, far_size, 2 * comps * kv_here, picked_count)
     got = jnp.stack([at(sends, near)] + [swap(at(sends, near ^ k), k) for k in (1, 2, 3)])
     got = jnp.transpose(got, (1, 0, 2, 3))
-    got = jnp.stack([at(got, far)] + [swap(at(got, far ^ k), NEAR * k) for k in range(1, far_size)])
+    got = jnp.stack([at(got, far)] + [swap(at(got, far ^ k), far_mask(k)) for k in range(1, far_size)])
     ordered = jnp.stack(
-        [at(at(got, far ^ (d // NEAR)), near ^ (d % NEAR)) for d in range(size)]
+        [at(at(got, far ^ (d // NEAR)), near ^ quarter_of(d)) for d in range(size)]
     ).reshape(size, 2, comps, kv_here, picked_count)
     ordered = jnp.transpose(ordered, (1, 3, 0, 2, 4)).reshape(2, kv_here, HEAD_SIZE, picked_count)
 
@@ -175,7 +185,7 @@
     spread = select.reshape(picked_count, far_size, NEAR * MOST)
     delta = dot(spread[:, 0].T, ffn_part) + dot(spread[:, 0].T, attn_quarter.astype(bf16))
     for k in range(1, far_size):
-        delta = delta + swap(dot(spread[:, k].T, ffn_part).astype(bf16), NEAR * k).astype(f32)
+        delta = delta + swap(dot(spread[:, k].T, ffn_part).astype(bf16), far_mask(k)).astype(f32)
     delta = delta.astype(bf16).reshape(NEAR, MOST, quarter)
     back = jnp.stack([delta[0]] + [swap(delta[k], k) for k in (1, 2, 3)])
     back = jnp.concatenate([at(back, near ^ a) for a in range(NEAR)], axis=1)

time: 162 us -> 155 us (0.957)
  waiting for transfers between devices: 86.3 us -> 70.2 us
  starting transfers between devices: 37.4 us -> 45.9 us
    ppermute x25, waiting for transfers between devices: 86.3 us -> 70.2 us  [swap(): return lax.ppermute(value, 'ctx', [(i, i ^ mask) for i in range(size)])]
    ppermute x25, starting transfers between devices: 37.4 us -> 45.9 us  [swap(): return lax.ppermute(value, 'ctx', [(i, i ^ mask) for i in range(size)])]
  transfers between devices with their start and end apart: 25 -> 25, of which waited for: 23 -> 21; matrix products, arithmetic and copies ran while one was open for 1% -> 1% of each run, Pallas kernels for 0% -> 0%
where the time goes in v2:
time: 155 us; the launch traced here: 154 us
  waiting for transfers between devices  70.2 us (45%)
  starting transfers between devices  45.9 us (30%)
  matrix products  30 us (19%)
  other arithmetic  4.11 us (3%)
  local copies, waits for them, and re-layouts  3.45 us (2%)
    ppermute x25, waiting for transfers between devices, swap(): return lax.ppermute(value, 'ctx', [(i, i ^ mask) for i in range(size)])  70.2 us
    ppermute x25, starting transfers between devices, swap(): return lax.ppermute(value, 'ctx', [(i, i ^ mask) for i in range(size)])  45.9 us
    dot_general x11, matrix products, dot(): return jnp.dot(a, b, preferred_element_type=f32)  27.2 us
  transfers between devices with their start and end apart: 25, of which 21 were waited for; matrix products, arithmetic and copies ran while one was open for 1% of the time, Pallas kernels for 0%

profile of v2, /device:TPU:0, one launch (start us, length us, event | category | flops | bytes accessed | tf_op | source)
XLA Modules:
  0.0 154.3 jit_solution(8992815871886080004)
XLA Ops:
  3.3 4.0 %collective-permute-start.2 = (bf16[32,1152]{1,0:T(8,128)(2,1)S(1)}, bf16[32,1152]{1,0:T(8,128)(2,1)S(1)}, u32[]{:S(2)}, u32[]{:S(2)}) collective-permute-start(bf16[32,1152]{1,0:T(8,128)(2,1)S(1)} %get-tuple-element.31), channel_id=1, source_target_pairs={{0,3},{1,2},{2,1},{3,0},{4,7},{5,6},{6,5},{7,4},{8,11},{9,10},{10,... | collective-permute-start | bytes 221192 | tf_op jit(solution)/shard_map/ppermute | solution.py:22
  8.1 1.9 %collective-permute-done.2 = bf16[32,1152]{1,0:T(8,128)(2,1)S(1)} collective-permute-done((bf16[32,1152]{1,0:T(8,128)(2,1)S(1)}, bf16[32,1152]{1,0:T(8,128)(2,1)S(1)}, u32[]{:S(2)}, u32[]{:S(2)}) %collective-permute-start.2) | collective-permute-done | bytes 73760 | tf_op jit(solution)/shard_map/ppermute | solution.py:22
  10.0 1.7 %collective-permute-done.1 = bf16[32,1152]{1,0:T(8,128)(2,1)S(1)} collective-permute-done((bf16[32,1152]{1,0:T(8,128)(2,1)S(1)}, bf16[32,1152]{1,0:T(8,128)(2,1)S(1)}, u32[]{:S(2)}, u32[]{:S(2)}) %collective-permute-start.1) | collective-permute-done | bytes 73760 | tf_op jit(solution)/shard_map/ppermute | solution.py:22
  12.2 3.7 %collective-permute-start.3 = (bf16[128,1152]{1,0:T(8,128)(2,1)S(1)}, bf16[128,1152]{1,0:T(8,128)(2,1)S(1)}, u32[]{:S(2)}, u32[]{:S(2)}) collective-permute-start(bf16[128,1152]{1,0:T(8,128)(2,1)S(1)} %pad_maximum_fusion.7), channel_id=1, source_target_pairs={{0,6},{1,7},{2,4},{3,5},{4,2},{5,3},{6,0},{7,1},{8,14},{9,15},{10,... | collective-permute-start | bytes 884744 | tf_op jit(solution)/shard_map/ppermute | solution.py:22
  15.9 6.3 %collective-permute-done.3 = bf16[128,1152]{1,0:T(8,128)(2,1)S(1)} collective-permute-done((bf16[128,1152]{1,0:T(8,128)(2,1)S(1)}, bf16[128,1152]{1,0:T(8,128)(2,1)S(1)}, u32[]{:S(2)}, u32[]{:S(2)}) %collective-permute-start.3) | collective-permute-done | bytes 294944 | tf_op jit(solution)/shard_map/ppermute | solution.py:22
  22.9 6.1 %collective-permute-start.6 = (bf16[128,1024]{1,0:T(8,128)(2,1)S(1)}, bf16[128,1024]{1,0:T(8,128)(2,1)S(1)}, u32[]{:S(2)}, u32[]{:S(2)}) collective-permute-start(bf16[128,1024]{1,0:T(8,128)(2,1)S(1)} %convolution_convert_fusion.4), channel_id=1, source_target_pairs={{0,3},{1,2},{2,1},{3,0},{4,7},{5,6},{6,5},{7,4},{8,11},{9,10},{10,... | collective-permute-start | bytes 786440 | tf_op jit(solution)/shard_map/ppermute | solution.py:22
  30.8 5.4 %collective-permute-done.6 = bf16[128,1024]{1,0:T(8,128)(2,1)S(1)} collective-permute-done((bf16[128,1024]{1,0:T(8,128)(2,1)S(1)}, bf16[128,1024]{1,0:T(8,128)(2,1)S(1)}, u32[]{:S(2)}, u32[]{:S(2)}) %collective-permute-start.6) | collective-permute-done | bytes 262176 | tf_op jit(solution)/shard_map/ppermute | solution.py:22
  36.2 3.9 %collective-permute-done.5 = bf16[128,1024]{1,0:T(8,128)(2,1)S(1)} collective-permute-done((bf16[128,1024]{1,0:T(8,128)(2,1)S(1)}, bf16[128,1024]{1,0:T(8,128)(2,1)S(1)}, u32[]{:S(2)}, u32[]{:S(2)}) %collective-permute-start.5) | collective-permute-done | bytes 262176 | tf_op jit(solution)/shard_map/ppermute | solution.py:22
  40.7 1.6 %copy-done.1 = bf16[4096,512]{1,0:T(8,128)(2,1)S(1)} copy-done((bf16[4096,512]{1,0:T(8,128)(2,1)S(1)}, bf16[4096,512]{1,0:T(8,128)(2,1)}, u32[]{:S(2)}) %copy-start.1) | copy-done | bytes 4194328
  43.2 2.3 %fusion.18 = bf16[256,128]{1,0:T(8,128)(2,1)S(1)} fusion(bf16[4096,128]{1,0:T(8,128)(2,1)} %param.18, bf16[4096,128]{1,0:T(8,128)(2,1)} %param.17, f32[4096]{0:T(1024)S(1)} %copy-done.2, f32[128]{0:T(128)S(1)} %add_rsqrt_fusion.1, bf16[128,1024]{1,0:T(8,128)(2,1)S(1)} %get-tuple-element.26, bf16[128,1024]{1,0:T(8,128)(2,1)S(1)} %get-tuple-element.27, ...), kind=kOutput, calls=%fused_computation.32 | convolution fusion | flops 278429696 | bytes 3228160 | tf_op jit(solution)/shard_map/pd,dc->cp/dot_general | solution.py:127
  45.8 2.7 %collective-permute-start.9 = (bf16[2,32,128]{2,1,0:T(8,128)(2,1)S(1)}, bf16[2,32,128]{2,1,0:T(8,128)(2,1)S(1)}, u32[]{:S(2)}, u32[]{:S(2)}) collective-permute-start(bf16[2,32,128]{2,1,0:T(8,128)(2,1)S(1)} %get-tuple-element.63), channel_id=1, source_target_pairs={{0,3},{1,2},{2,1},{3,0},{4,7},{5,6},{6,5},{7,4},{8,11},{9,10},{10,... | collective-permute-start | bytes 49160 | tf_op jit(solution)/shard_map/ppermute | solution.py:22
  50.5 1.7 %collective-permute-done.8 = bf16[2,32,128]{2,1,0:T(8,128)(2,1)S(1)} collective-permute-done((bf16[2,32,128]{2,1,0:T(8,128)(2,1)S(1)}, bf16[2,32,128]{2,1,0:T(8,128)(2,1)S(1)}, u32[]{:S(2)}, u32[]{:S(2)}) %collective-permute-start.8) | collective-permute-done | bytes 16416 | tf_op jit(solution)/shard_map/ppermute | solution.py:22
  52.5 1.6 %collective-permute-start.10 = (bf16[4,32,128]{2,1,0:T(8,128)(2,1)S(1)}, bf16[4,32,128]{2,1,0:T(8,128)(2,1)S(1)}, u32[]{:S(2)}, u32[]{:S(2)}) collective-permute-start(bf16[4,32,128]{2,1,0:T(8,128)(2,1)S(1)} %get-tuple-element.60), channel_id=1, source_target_pairs={{0,6},{1,7},{2,4},{3,5},{4,2},{5,3},{6,0},{7,1},{8,14},{9,15},{10,... | collective-permute-start | bytes 98312 | tf_op jit(solution)/shard_map/ppermute | solution.py:22
  54.2 4.1 %collective-permute-done.10 = bf16[4,32,128]{2,1,0:T(8,128)(2,1)S(1)} collective-permute-done((bf16[4,32,128]{2,1,0:T(8,128)(2,1)S(1)}, bf16[4,32,128]{2,1,0:T(8,128)(2,1)S(1)}, u32[]{:S(2)}, u32[]{:S(2)}) %collective-permute-start.10) | collective-permute-done | bytes 32800 | tf_op jit(solution)/shard_map/ppermute | solution.py:22
  59.6 2.9 %convolution_convert_fusion.1 = bf16[128,4096]{1,0:T(8,128)(2,1)S(1)} fusion(bf16[128,512]{0,1:T(8,128)(2,1)S(1)} %bitcast.214, bf16[512,4096]{1,0:T(8,128)(2,1)} %param.19), kind=kOutput, calls=%fused_computation.4 | convolution fusion | flops 537395200 | bytes 5373952 | tf_op jit(solution)/shard_map/dot_general | solution.py:38
  63.7 1.8 %collective-permute-start.13 = (bf16[128,1024]{1,0:T(8,128)(2,1)S(1)}, bf16[128,1024]{1,0:T(8,128)(2,1)S(1)}, u32[]{:S(2)}, u32[]{:S(2)}) collective-permute-start(bf16[128,1024]{1,0:T(8,128)(2,1)S(1)} %get-tuple-element.19), channel_id=1, source_target_pairs={{0,2},{1,3},{2,0},{3,1},{4,6},{5,7},{6,4},{7,5},{8,10},{9,11},{10,... | collective-permute-start | bytes 786440 | tf_op jit(solution)/shard_map/ppermute | solution.py:22
  66.4 5.8 %collective-permute-done.11 = bf16[128,1024]{1,0:T(8,128)(2,1)S(1)} collective-permute-done((bf16[128,1024]{1,0:T(8,128)(2,1)S(1)}, bf16[128,1024]{1,0:T(8,128)(2,1)S(1)}, u32[]{:S(2)}, u32[]{:S(2)}) %collective-permute-start.11) | collective-permute-done | bytes 262176 | tf_op jit(solution)/shard_map/ppermute | solution.py:22
  72.1 2.7 %collective-permute-done.13 = bf16[128,1024]{1,0:T(8,128)(2,1)S(1)} collective-permute-done((bf16[128,1024]{1,0:T(8,128)(2,1)S(1)}, bf16[128,1024]{1,0:T(8,128)(2,1)S(1)}, u32[]{:S(2)}, u32[]{:S(2)}) %collective-permute-start.13) | collective-permute-done | bytes 262176 | tf_op jit(solution)/shard_map/ppermute | solution.py:22
  76.3 7.1 %collective-permute-done.14 = bf16[128,1024]{1,0:T(8,128)(2,1)S(1)} collective-permute-done((bf16[128,1024]{1,0:T(8,128)(2,1)S(1)}, bf16[128,1024]{1,0:T(8,128)(2,1)S(1)}, u32[]{:S(2)}, u32[]{:S(2)}) %collective-permute-start.14) | collective-permute-done | bytes 262176 | tf_op jit(solution)/shard_map/ppermute | solution.py:22
  83.5 4.8 %collective-permute-start.17 = (bf16[128,1024]{1,0:T(8,128)(2,1)S(1)}, bf16[128,1024]{1,0:T(8,128)(2,1)S(1)}, u32[]{:S(2)}, u32[]{:S(2)}) collective-permute-start(bf16[128,1024]{1,0:T(8,128)(2,1)S(1)} %add_convert_fusion), channel_id=1, source_target_pairs={{0,3},{1,2},{2,1},{3,0},{4,7},{5,6},{6,5},{7,4},{8,11},{9,10},{10,... | collective-permute-start | bytes 786440 | tf_op jit(solution)/shard_map/ppermute | solution.py:22
  89.1 6.0 %collective-permute-done.17 = bf16[128,1024]{1,0:T(8,128)(2,1)S(1)} collective-permute-done((bf16[128,1024]{1,0:T(8,128)(2,1)S(1)}, bf16[128,1024]{1,0:T(8,128)(2,1)S(1)}, u32[]{:S(2)}, u32[]{:S(2)}) %collective-permute-start.17) | collective-permute-done | bytes 262176 | tf_op jit(solution)/shard_map/ppermute | solution.py:22
  95.1 2.5 %collective-permute-done.16 = bf16[128,1024]{1,0:T(8,128)(2,1)S(1)} collective-permute-done((bf16[128,1024]{1,0:T(8,128)(2,1)S(1)}, bf16[128,1024]{1,0:T(8,128)(2,1)S(1)}, u32[]{:S(2)}, u32[]{:S(2)}) %collective-permute-start.16) | collective-permute-done | bytes 262176 | tf_op jit(solution)/shard_map/ppermute | solution.py:22
  98.7 7.0 %fusion.34 = f32[128,1408]{1,0:T(8,128)} fusion(bf16[4096,1408]{1,0:T(8,128)(2,1)} %param.21, f32[4096]{0:T(1024)S(1)} %copy-done.3, f32[128]{0:T(128)S(1)} %add_rsqrt_fusion, bf16[128,1024]{1,0:T(8,128)(2,1)S(1)} %get-tuple-element.15, bf16[128,1024]{1,0:T(8,128)(2,1)S(1)} %get-tuple-element.16, bf16[128,1024]{1,0:T(8,128)(2,1)S(1)} %get-tuple-element.17, ...), kind=kOutput, calls=%fused_computation.55 | convolution fusion | flops 1482162176 | bytes 13320704 | tf_op jit(solution)/shard_map/dot_general | solution.py:38
  105.7 11.6 %convolution_convert_fusion = bf16[128,4096]{1,0:T(8,128)(2,1)S(1)} fusion(bf16[1408,4096]{1,0:T(8,128)(2,1)} %param.23, bf16[4096,1408]{1,0:T(8,128)(2,1)} %param.22, f32[128,1408]{1,0:T(8,128)} %fusion.34, f32[4096]{0:T(1024)S(1)} %copy-done.3, f32[128]{0:T(128)S(1)} %add_rsqrt_fusion, bf16[128,1024]{1,0:T(8,128)(2,1)S(1)} %get-tuple-element.15, ...), kind=kOutput, calls=%fused_computation.3 | convolution fusion | flops 2960162816 | bytes 25903616 | tf_op jit(solution)/shard_map/dot_general | solution.py:38
  117.7 2.7 %collective-permute-start.18 = (bf16[128,1024]{1,0:T(8,128)(2,1)S(1)}, bf16[128,1024]{1,0:T(8,128)(2,1)S(1)}, u32[]{:S(2)}, u32[]{:S(2)}) collective-permute-start(bf16[128,1024]{1,0:T(8,128)(2,1)S(1)} %get-tuple-element.7), channel_id=1, source_target_pairs={{0,3},{1,2},{2,1},{3,0},{4,7},{5,6},{6,5},{7,4},{8,11},{9,10},{10,... | collective-permute-start | bytes 786440 | tf_op jit(solution)/shard_map/ppermute | solution.py:22
  121.8 6.1 %collective-permute-done.18 = bf16[128,1024]{1,0:T(8,128)(2,1)S(1)} collective-permute-done((bf16[128,1024]{1,0:T(8,128)(2,1)S(1)}, bf16[128,1024]{1,0:T(8,128)(2,1)S(1)}, u32[]{:S(2)}, u32[]{:S(2)}) %collective-permute-start.18) | collective-permute-done | bytes 262176 | tf_op jit(solution)/shard_map/ppermute | solution.py:22
  127.9 3.4 %collective-permute-done.20 = bf16[128,1024]{1,0:T(8,128)(2,1)S(1)} collective-permute-done((bf16[128,1024]{1,0:T(8,128)(2,1)S(1)}, bf16[128,1024]{1,0:T(8,128)(2,1)S(1)}, u32[]{:S(2)}, u32[]{:S(2)}) %collective-permute-start.20) | collective-permute-done | bytes 262176 | tf_op jit(solution)/shard_map/ppermute | solution.py:22
  131.8 2.4 %collective-permute-start.21 = (bf16[128,1024]{1,0:T(8,128)(2,1)S(1)}, bf16[128,1024]{1,0:T(8,128)(2,1)S(1)}, u32[]{:S(2)}, u32[]{:S(2)}) collective-permute-start(bf16[128,1024]{1,0:T(8,128)(2,1)S(1)} %convolution_convert_fusion.3), channel_id=1, source_target_pairs={{0,6},{1,7},{2,4},{3,5},{4,2},{5,3},{6,0},{7,1},{8,14},{9,15},{10,... | collective-permute-start | bytes 786440 | tf_op jit(solution)/shard_map/ppermute | solution.py:22
  134.4 6.9 %collective-permute-done.21 = bf16[128,1024]{1,0:T(8,128)(2,1)S(1)} collective-permute-done((bf16[128,1024]{1,0:T(8,128)(2,1)S(1)}, bf16[128,1024]{1,0:T(8,128)(2,1)S(1)}, u32[]{:S(2)}, u32[]{:S(2)}) %collective-permute-start.21) | collective-permute-done | bytes 262176 | tf_op jit(solution)/shard_map/ppermute | solution.py:22
  141.7 6.7 %collective-permute-start.24 = (bf16[32,1024]{1,0:T(8,128)(2,1)S(1)}, bf16[32,1024]{1,0:T(8,128)(2,1)S(1)}, u32[]{:S(2)}, u32[]{:S(2)}) collective-permute-start(bf16[32,1024]{1,0:T(8,128)(2,1)S(1)} %get-tuple-element.39), channel_id=1, source_target_pairs={{0,3},{1,2},{2,1},{3,0},{4,7},{5,6},{6,5},{7,4},{8,11},{9,10},{10,... | collective-permute-start | bytes 196616 | tf_op jit(solution)/shard_map/ppermute | solution.py:22
  150.7 2.0 %collective-permute-done.23 = bf16[32,1024]{1,0:T(8,128)(2,1)S(1)} collective-permute-done((bf16[32,1024]{1,0:T(8,128)(2,1)S(1)}, bf16[32,1024]{1,0:T(8,128)(2,1)S(1)}, u32[]{:S(2)}, u32[]{:S(2)}) %collective-permute-start.23) | collective-permute-done | bytes 65568 | tf_op jit(solution)/shard_map/ppermute | solution.py:22
  152.7 1.5 fusion.2
  (124 shorter events, 22.7 us)
Async XLA Ops:
  3.3 6.7 %collective-permute-start.2 = (bf16[32,1152]{1,0:T(8,128)(2,1)S(1)}, bf16[32,1152]{1,0:T(8,128)(2,1)S(1)}, u32[]{:S(2)}, u32[]{:S(2)}) collective-permute-start(bf16[32,1152]{1,0:T(8,128)(2,1)S(1)} %get-tuple-element.31), channel_id=1, source_target_pairs={{0,3},{1,2},{2,1},{3,0},{4,7},{5,6},{6,5},{7,4},{8,11},{9,10},{10,... | collective-permute-start | bytes 221192 | tf_op jit(solution)/shard_map/ppermute | solution.py:22
  7.4 4.4 %collective-permute-start.1 = (bf16[32,1152]{1,0:T(8,128)(2,1)S(1)}, bf16[32,1152]{1,0:T(8,128)(2,1)S(1)}, u32[]{:S(2)}, u32[]{:S(2)}) collective-permute-start(bf16[32,1152]{1,0:T(8,128)(2,1)S(1)} %get-tuple-element.32), channel_id=1, source_target_pairs={{0,2},{1,3},{2,0},{3,1},{4,6},{5,7},{6,4},{7,5},{8,10},{9,11},{10,... | collective-permute-start | bytes 221192 | tf_op jit(solution)/shard_map/ppermute | solution.py:22
  7.8 4.4 %collective-permute-start = (bf16[32,1152]{1,0:T(8,128)(2,1)S(1)}, bf16[32,1152]{1,0:T(8,128)(2,1)S(1)}, u32[]{:S(2)}, u32[]{:S(2)}) collective-permute-start(bf16[32,1152]{1,0:T(8,128)(2,1)S(1)} %get-tuple-element.33), channel_id=1, source_target_pairs={{0,1},{1,0},{2,3},{3,2},{4,5},{5,4},{6,7},{7,6},{8,9},{9,8},{10,11... | collective-permute-start | bytes 221192 | tf_op jit(solution)/shard_map/ppermute | solution.py:22
  12.2 10.0 %collective-permute-start.3 = (bf16[128,1152]{1,0:T(8,128)(2,1)S(1)}, bf16[128,1152]{1,0:T(8,128)(2,1)S(1)}, u32[]{:S(2)}, u32[]{:S(2)}) collective-permute-start(bf16[128,1152]{1,0:T(8,128)(2,1)S(1)} %pad_maximum_fusion.7), channel_id=1, source_target_pairs={{0,6},{1,7},{2,4},{3,5},{4,2},{5,3},{6,0},{7,1},{8,14},{9,15},{10,... | collective-permute-start | bytes 884744 | tf_op jit(solution)/shard_map/ppermute | solution.py:22
  22.9 13.3 %collective-permute-start.6 = (bf16[128,1024]{1,0:T(8,128)(2,1)S(1)}, bf16[128,1024]{1,0:T(8,128)(2,1)S(1)}, u32[]{:S(2)}, u32[]{:S(2)}) collective-permute-start(bf16[128,1024]{1,0:T(8,128)(2,1)S(1)} %convolution_convert_fusion.4), channel_id=1, source_target_pairs={{0,3},{1,2},{2,1},{3,0},{4,7},{5,6},{6,5},{7,4},{8,11},{9,10},{10,... | collective-permute-start | bytes 786440 | tf_op jit(solution)/shard_map/ppermute | solution.py:22
  28.9 11.2 %collective-permute-start.5 = (bf16[128,1024]{1,0:T(8,128)(2,1)S(1)}, bf16[128,1024]{1,0:T(8,128)(2,1)S(1)}, u32[]{:S(2)}, u32[]{:S(2)}) collective-permute-start(bf16[128,1024]{1,0:T(8,128)(2,1)S(1)} %convolution_convert_fusion.4), channel_id=1, source_target_pairs={{0,2},{1,3},{2,0},{3,1},{4,6},{5,7},{6,4},{7,5},{8,10},{9,11},{10,... | collective-permute-start | bytes 786440 | tf_op jit(solution)/shard_map/ppermute | solution.py:22
  28.9 11.2 %collective-permute-start.4 = (bf16[128,1024]{1,0:T(8,128)(2,1)S(1)}, bf16[128,1024]{1,0:T(8,128)(2,1)S(1)}, u32[]{:S(2)}, u32[]{:S(2)}) collective-permute-start(bf16[128,1024]{1,0:T(8,128)(2,1)S(1)} %convolution_convert_fusion.4), channel_id=1, source_target_pairs={{0,1},{1,0},{2,3},{3,2},{4,5},{5,4},{6,7},{7,6},{8,9},{9,8},{10,11... | collective-permute-start | bytes 786440 | tf_op jit(solution)/shard_map/ppermute | solution.py:22
  40.1 2.2 %copy-start.1 = (bf16[4096,512]{1,0:T(8,128)(2,1)S(1)}, bf16[4096,512]{1,0:T(8,128)(2,1)}, u32[]{:S(2)}) copy-start(bf16[4096,512]{1,0:T(8,128)(2,1)} %param.16) | copy-start | bytes 12582916
  40.2 2.1 %copy-start.2 = (f32[4096]{0:T(1024)S(1)}, f32[4096]{0:T(1024)}, u32[]{:S(2)}) copy-start(f32[4096]{0:T(1024)} %param.15) | copy-start | bytes 49156
  45.8 4.7 %collective-permute-start.9 = (bf16[2,32,128]{2,1,0:T(8,128)(2,1)S(1)}, bf16[2,32,128]{2,1,0:T(8,128)(2,1)S(1)}, u32[]{:S(2)}, u32[]{:S(2)}) collective-permute-start(bf16[2,32,128]{2,1,0:T(8,128)(2,1)S(1)} %get-tuple-element.63), channel_id=1, source_target_pairs={{0,3},{1,2},{2,1},{3,0},{4,7},{5,6},{6,5},{7,4},{8,11},{9,10},{10,... | collective-permute-start | bytes 49160 | tf_op jit(solution)/shard_map/ppermute | solution.py:22
  48.5 3.7 %collective-permute-start.8 = (bf16[2,32,128]{2,1,0:T(8,128)(2,1)S(1)}, bf16[2,32,128]{2,1,0:T(8,128)(2,1)S(1)}, u32[]{:S(2)}, u32[]{:S(2)}) collective-permute-start(bf16[2,32,128]{2,1,0:T(8,128)(2,1)S(1)} %get-tuple-element.64), channel_id=1, source_target_pairs={{0,2},{1,3},{2,0},{3,1},{4,6},{5,7},{6,4},{7,5},{8,10},{9,11},{10,... | collective-permute-start | bytes 49160 | tf_op jit(solution)/shard_map/ppermute | solution.py:22
  48.7 3.7 %collective-permute-start.7 = (bf16[2,32,128]{2,1,0:T(8,128)(2,1)S(1)}, bf16[2,32,128]{2,1,0:T(8,128)(2,1)S(1)}, u32[]{:S(2)}, u32[]{:S(2)}) collective-permute-start(bf16[2,32,128]{2,1,0:T(8,128)(2,1)S(1)} %get-tuple-element.65), channel_id=1, source_target_pairs={{0,1},{1,0},{2,3},{3,2},{4,5},{5,4},{6,7},{7,6},{8,9},{9,8},{10,11... | collective-permute-start | bytes 49160 | tf_op jit(solution)/shard_map/ppermute | solution.py:22
  52.5 5.8 %collective-permute-start.10 = (bf16[4,32,128]{2,1,0:T(8,128)(2,1)S(1)}, bf16[4,32,128]{2,1,0:T(8,128)(2,1)S(1)}, u32[]{:S(2)}, u32[]{:S(2)}) collective-permute-start(bf16[4,32,128]{2,1,0:T(8,128)(2,1)S(1)} %get-tuple-element.60), channel_id=1, source_target_pairs={{0,6},{1,7},{2,4},{3,5},{4,2},{5,3},{6,0},{7,1},{8,14},{9,15},{10,... | collective-permute-start | bytes 98312 | tf_op jit(solution)/shard_map/ppermute | solution.py:22
  62.8 9.3 %collective-permute-start.11 = (bf16[128,1024]{1,0:T(8,128)(2,1)S(1)}, bf16[128,1024]{1,0:T(8,128)(2,1)S(1)}, u32[]{:S(2)}, u32[]{:S(2)}) collective-permute-start(bf16[128,1024]{1,0:T(8,128)(2,1)S(1)} %get-tuple-element.18), channel_id=1, source_target_pairs={{0,3},{1,2},{2,1},{3,0},{4,7},{5,6},{6,5},{7,4},{8,11},{9,10},{10,... | collective-permute-start | bytes 786440 | tf_op jit(solution)/shard_map/ppermute | solution.py:22
  63.7 11.1 %collective-permute-start.13 = (bf16[128,1024]{1,0:T(8,128)(2,1)S(1)}, bf16[128,1024]{1,0:T(8,128)(2,1)S(1)}, u32[]{:S(2)}, u32[]{:S(2)}) collective-permute-start(bf16[128,1024]{1,0:T(8,128)(2,1)S(1)} %get-tuple-element.19), channel_id=1, source_target_pairs={{0,2},{1,3},{2,0},{3,1},{4,6},{5,7},{6,4},{7,5},{8,10},{9,11},{10,... | collective-permute-start | bytes 786440 | tf_op jit(solution)/shard_map/ppermute | solution.py:22
  65.5 9.3 %collective-permute-start.12 = (bf16[128,1024]{1,0:T(8,128)(2,1)S(1)}, bf16[128,1024]{1,0:T(8,128)(2,1)S(1)}, u32[]{:S(2)}, u32[]{:S(2)}) collective-permute-start(bf16[128,1024]{1,0:T(8,128)(2,1)S(1)} %get-tuple-element.20), channel_id=1, source_target_pairs={{0,1},{1,0},{2,3},{3,2},{4,5},{5,4},{6,7},{7,6},{8,9},{9,8},{10,11... | collective-permute-start | bytes 786440 | tf_op jit(solution)/shard_map/ppermute | solution.py:22
  75.0 8.4 %collective-permute-start.14 = (bf16[128,1024]{1,0:T(8,128)(2,1)S(1)}, bf16[128,1024]{1,0:T(8,128)(2,1)S(1)}, u32[]{:S(2)}, u32[]{:S(2)}) collective-permute-start(bf16[128,1024]{1,0:T(8,128)(2,1)S(1)} %fusion.29), channel_id=1, source_target_pairs={{0,6},{1,7},{2,4},{3,5},{4,2},{5,3},{6,0},{7,1},{8,14},{9,15},{10,... | collective-permute-start | bytes 786440 | tf_op jit(solution)/shard_map/ppermute | solution.py:22
  83.5 11.6 %collective-permute-start.17 = (bf16[128,1024]{1,0:T(8,128)(2,1)S(1)}, bf16[128,1024]{1,0:T(8,128)(2,1)S(1)}, u32[]{:S(2)}, u32[]{:S(2)}) collective-permute-start(bf16[128,1024]{1,0:T(8,128)(2,1)S(1)} %add_convert_fusion), channel_id=1, source_target_pairs={{0,3},{1,2},{2,1},{3,0},{4,7},{5,6},{6,5},{7,4},{8,11},{9,10},{10,... | collective-permute-start | bytes 786440 | tf_op jit(solution)/shard_map/ppermute | solution.py:22
  88.3 9.3 %collective-permute-start.16 = (bf16[128,1024]{1,0:T(8,128)(2,1)S(1)}, bf16[128,1024]{1,0:T(8,128)(2,1)S(1)}, u32[]{:S(2)}, u32[]{:S(2)}) collective-permute-start(bf16[128,1024]{1,0:T(8,128)(2,1)S(1)} %add_convert_fusion), channel_id=1, source_target_pairs={{0,2},{1,3},{2,0},{3,1},{4,6},{5,7},{6,4},{7,5},{8,10},{9,11},{10,... | collective-permute-start | bytes 786440 | tf_op jit(solution)/shard_map/ppermute | solution.py:22
  88.3 9.6 %collective-permute-start.15 = (bf16[128,1024]{1,0:T(8,128)(2,1)S(1)}, bf16[128,1024]{1,0:T(8,128)(2,1)S(1)}, u32[]{:S(2)}, u32[]{:S(2)}) collective-permute-start(bf16[128,1024]{1,0:T(8,128)(2,1)S(1)} %add_convert_fusion), channel_id=1, source_target_pairs={{0,1},{1,0},{2,3},{3,2},{4,5},{5,4},{6,7},{7,6},{8,9},{9,8},{10,11... | collective-permute-start | bytes 786440 | tf_op jit(solution)/shard_map/ppermute | solution.py:22
  98.0 0.7 copy-start.3
  117.7 10.2 %collective-permute-start.18 = (bf16[128,1024]{1,0:T(8,128)(2,1)S(1)}, bf16[128,1024]{1,0:T(8,128)(2,1)S(1)}, u32[]{:S(2)}, u32[]{:S(2)}) collective-permute-start(bf16[128,1024]{1,0:T(8,128)(2,1)S(1)} %get-tuple-element.7), channel_id=1, source_target_pairs={{0,3},{1,2},{2,1},{3,0},{4,7},{5,6},{6,5},{7,4},{8,11},{9,10},{10,... | collective-permute-start | bytes 786440 | tf_op jit(solution)/shard_map/ppermute | solution.py:22
  120.4 11.0 %collective-permute-start.20 = (bf16[128,1024]{1,0:T(8,128)(2,1)S(1)}, bf16[128,1024]{1,0:T(8,128)(2,1)S(1)}, u32[]{:S(2)}, u32[]{:S(2)}) collective-permute-start(bf16[128,1024]{1,0:T(8,128)(2,1)S(1)} %get-tuple-element.8), channel_id=1, source_target_pairs={{0,2},{1,3},{2,0},{3,1},{4,6},{5,7},{6,4},{7,5},{8,10},{9,11},{10,... | collective-permute-start | bytes 786440 | tf_op jit(solution)/shard_map/ppermute | solution.py:22
  120.4 10.9 %collective-permute-start.19 = (bf16[128,1024]{1,0:T(8,128)(2,1)S(1)}, bf16[128,1024]{1,0:T(8,128)(2,1)S(1)}, u32[]{:S(2)}, u32[]{:S(2)}) collective-permute-start(bf16[128,1024]{1,0:T(8,128)(2,1)S(1)} %get-tuple-element.9), channel_id=1, source_target_pairs={{0,1},{1,0},{2,3},{3,2},{4,5},{5,4},{6,7},{7,6},{8,9},{9,8},{10,11... | collective-permute-start | bytes 786440 | tf_op jit(solution)/shard_map/ppermute | solution.py:22
  121.8 27.5 %copy-start.4 = (bf16[128]{0:T(256)(128)(2,1)S(1)}, bf16[128]{0:T(256)(128)(2,1)}, u32[]{:S(2)}) copy-start(bf16[128]{0:T(256)(128)(2,1)} %param.14) | copy-start | bytes 772
  131.8 20.9 %copy-start = (bf16[128,4096]{1,0:T(8,128)(2,1)S(1)}, bf16[128,4096]{1,0:T(8,128)(2,1)}, u32[]{:S(2)}) copy-start(bf16[128,4096]{1,0:T(8,128)(2,1)} %param.12) | copy-start | bytes 3145732
  131.8 9.6 %collective-permute-start.21 = (bf16[128,1024]{1,0:T(8,128)(2,1)S(1)}, bf16[128,1024]{1,0:T(8,128)(2,1)S(1)}, u32[]{:S(2)}, u32[]{:S(2)}) collective-permute-start(bf16[128,1024]{1,0:T(8,128)(2,1)S(1)} %convolution_convert_fusion.3), channel_id=1, source_target_pairs={{0,6},{1,7},{2,4},{3,5},{4,2},{5,3},{6,0},{7,1},{8,14},{9,15},{10,... | collective-permute-start | bytes 786440 | tf_op jit(solution)/shard_map/ppermute | solution.py:22
  141.7 9.0 %collective-permute-start.24 = (bf16[32,1024]{1,0:T(8,128)(2,1)S(1)}, bf16[32,1024]{1,0:T(8,128)(2,1)S(1)}, u32[]{:S(2)}, u32[]{:S(2)}) collective-permute-start(bf16[32,1024]{1,0:T(8,128)(2,1)S(1)} %get-tuple-element.39), channel_id=1, source_target_pairs={{0,3},{1,2},{2,1},{3,0},{4,7},{5,6},{6,5},{7,4},{8,11},{9,10},{10,... | collective-permute-start | bytes 196616 | tf_op jit(solution)/shard_map/ppermute | solution.py:22
  148.4 4.3 %collective-permute-start.23 = (bf16[32,1024]{1,0:T(8,128)(2,1)S(1)}, bf16[32,1024]{1,0:T(8,128)(2,1)S(1)}, u32[]{:S(2)}, u32[]{:S(2)}) collective-permute-start(bf16[32,1024]{1,0:T(8,128)(2,1)S(1)} %get-tuple-element.40), channel_id=1, source_target_pairs={{0,2},{1,3},{2,0},{3,1},{4,6},{5,7},{6,4},{7,5},{8,10},{9,11},{10,... | collective-permute-start | bytes 196616 | tf_op jit(solution)/shard_map/ppermute | solution.py:22
  148.4 4.3 %collective-permute-start.22 = (bf16[32,1024]{1,0:T(8,128)(2,1)S(1)}, bf16[32,1024]{1,0:T(8,128)(2,1)S(1)}, u32[]{:S(2)}, u32[]{:S(2)}) collective-permute-start(bf16[32,1024]{1,0:T(8,128)(2,1)S(1)} %get-tuple-element.41), channel_id=1, source_target_pairs={{0,1},{1,0},{2,3},{3,2},{4,5},{5,4},{6,7},{7,6},{8,9},{9,8},{10,11... | collective-permute-start | bytes 196616 | tf_op jit(solution)/shard_map/ppermute | solution.py:22

commit v3 on v2

v3 whole, which is shorter than its diff:
```python
import functools

import jax
import jax.numpy as jnp
from jax import lax
from jax.experimental import pallas as pl
from jax.experimental.pallas import tpu as pltpu
from jax.sharding import PartitionSpec as P

QUERY_HEADS = 32
KEY_VALUE_HEADS = 8
HEAD_SIZE = 128
PICK_DEV = 16
MOST = 32
NEAR = 4
META = 128

norm_eps = 1e-05
rope_base = 500000.0

f32 = jnp.float32
bf16 = jnp.bfloat16
i32 = jnp.int32

VMEM = pl.BlockSpec(memory_space=pltpu.VMEM)
SMEM = pl.BlockSpec(memory_space=pltpu.SMEM)
ANY = pl.BlockSpec(memory_space=pl.ANY)
HBM = pl.BlockSpec(memory_space=pltpu.HBM)
MIB = 1024 * 1024


def swap(value, mask):
    size = lax.axis_size("ctx")
    return lax.ppermute(value, "ctx", [(i, i ^ mask) for i in range(size)])


def far_mask(k):
    return NEAR * k ^ (k & 1) * 2


def quarter_of(device):
    return (device & 3) ^ ((device // NEAR & 1) * 2)


def dot(a, b):
    return jnp.dot(a, b, preferred_element_type=f32)


def dot_nt(a, b):
    return lax.dot_general(a, b, (((1,), (1,)), ((), ())), preferred_element_type=f32)


def dot_tn(a, b):
    return lax.dot_general(a, b, (((0,), (0,)), ((), ())), preferred_element_type=f32)


def span(index, width):
    return pl.ds(pl.multiple_of(index * width, width), width)


def shape(dims, dtype=bf16):
    return jax.ShapeDtypeStruct(dims, dtype)


def run(kernel, name, out_shape, specs, *args, scratch=(), limit=8):
    outs = jax.tree.map(lambda _: VMEM, out_shape)
    return pl.pallas_call(
        kernel,
        in_specs=specs,
        out_specs=outs,
        out_shape=out_shape,
        scratch_shapes=scratch,
        compiler_params=pltpu.CompilerParams(vmem_limit_bytes=limit * MIB),
        name=name,
    )(*args)


def load(weights, after, name):
    count = len(weights)

    def kernel(*refs):
        sources, targets, done, sems = refs[:count], refs[count + 1 : -2], refs[-2], refs[-1]
        copies = [
            pltpu.make_async_copy(source, target, sems.at[i])
            for i, (source, target) in enumerate(zip(sources, targets))
        ]
        for copy in copies:
            copy.start()
        for copy in copies:
            copy.wait()
        done[...] = jnp.zeros_like(done)

    return pl.pallas_call(
        kernel,
        in_specs=[HBM] * count + [ANY],
        out_specs=[VMEM] * (count + 1),
        out_shape=[pltpu.VMEM(w.shape, w.dtype) for w in weights] + [pltpu.VMEM((8, 128), i32)],
        scratch_shapes=[pltpu.SemaphoreType.DMA((count,))],
        compiler_params=pltpu.CompilerParams(vmem_limit_bytes=MIB),
        name=name,
    )(*[pltpu.with_memory_space_constraint(w, pltpu.HBM) for w in weights], after)


def slots_of(flags):
    tokens = flags.shape[1]
    flag = jnp.broadcast_to(flags.astype(f32), (MOST, tokens))
    upto = lax.broadcasted_iota(i32, (tokens, tokens), 0) <= lax.broadcasted_iota(i32, (tokens, tokens), 1)
    place = dot(flag.astype(bf16), upto.astype(f32).astype(bf16))
    slot = lax.broadcasted_iota(i32, (MOST, tokens), 0).astype(f32) + 1.0
    return jnp.where((place == slot) & (flag > 0.5), 1.0, 0.0)


def pick_kernel(near, flags, tokens, *outs):
    hot = slots_of(flags[...])
    number = lax.broadcasted_iota(i32, hot.shape, 1).astype(f32) + 1.0
    index = jnp.sum(hot * number, axis=1, keepdims=True) - 1.0
    meta = jnp.broadcast_to(index, (MOST, META)).astype(bf16)
    hot = hot.astype(bf16)
    for k in range(NEAR):
        width = outs[k].shape[1] - META
        outs[k][:, :width] = dot(hot, tokens[:, span(near[0] ^ k, width)]).astype(bf16)
        outs[k][:, width:] = meta


def put_kernel(near, flags, scales, tokens, *refs):
    blocks, out = refs[:NEAR], refs[NEAR]
    hot = (slots_of(flags[...]) * scales[...].astype(f32)).astype(bf16)
    for k in range(NEAR):
        cols = span(near[0] ^ k, blocks[k].shape[1])
        out[:, cols] = (tokens[:, cols].astype(f32) + dot_tn(hot, blocks[k][...])).astype(bf16)


def normed(near, blocks, gain, out):
    width = out.shape[1]
    total = 0.0
    for block in blocks:
        value = block[...].astype(f32)
        total += jnp.sum(value * value, axis=1, keepdims=True)
    scale = lax.rsqrt(total * (1.0 / width) + norm_eps)
    for k, block in enumerate(blocks):
        cols = span(near[0] ^ k, block.shape[1])
        out[:, cols] = (block[...].astype(f32) * scale * gain[:, cols]).astype(bf16)


def kv_kernel(near, b0, b1, b2, b3, gain, key_weight, value_weight, place_k, place_v, done, rows, s0, s1, s2, s3):
    normed(near, (b0, b1, b2, b3), gain, rows)
    keys = dot(rows[...], key_weight[...]).astype(bf16)
    values = dot(rows[...], value_weight[...]).astype(bf16)
    sends = (dot_nt(place_k[...], keys) + dot_nt(place_v[...], values)).astype(bf16)
    height = s0.shape[0]
    for k, out in enumerate((s0, s1, s2, s3)):
        out[...] = sends[k * height : (k + 1) * height]


def matmul_kernel(left, right, out):
    out[...] = dot(left[...], right[...]).astype(out.dtype)


def attention_kernel(raw_q, raw_kv, order_k, order_v, cos_row, sin_row, cos_col, sin_col, out):
    half = HEAD_SIZE // 2
    keys = dot(order_k[...], raw_kv[...])
    values = dot(order_v[...], raw_kv[...]).astype(bf16)
    low, high = keys[:half], keys[half:]
    cosine, sine = cos_col[...], sin_col[...]
    keys = jnp.concatenate((low * cosine - high * sine, high * cosine + low * sine), axis=0).astype(bf16)
    count = raw_q.shape[0]
    allowed = lax.broadcasted_iota(i32, (count, count), 1) <= lax.broadcasted_iota(i32, (count, count), 0)
    for head in range(raw_q.shape[1] // HEAD_SIZE):
        cols = slice(head * HEAD_SIZE, (head + 1) * HEAD_SIZE)
        query = raw_q[:, cols]
        query = (query * cos_row[...] + pltpu.roll(query, half, 1) * sin_row[...]).astype(bf16)
        scores = dot(query, keys) * (1.0 / HEAD_SIZE**0.5)
        scores = jnp.where(allowed, scores, -jnp.inf)
        terms = jnp.exp(scores - jnp.max(scores, axis=1, keepdims=True))
        probs = (terms / jnp.sum(terms, axis=1, keepdims=True)).astype(bf16)
        out[:, cols] = dot_nt(probs, values).astype(bf16)


def block_kernel(k, near, left, right, out):
    out[...] = dot(left[...], right[:, span(near[0] ^ k, out.shape[1])]).astype(bf16)


def hidden_kernel(near, b0, b1, b2, b3, gain, gate, up, out, rows):
    normed(near, (b0, b1, b2, b3), gain, rows)
    gate_proj = dot(rows[...], gate[...])
    up_proj = dot(rows[...], up[...])
    out[...] = (jax.nn.silu(gate_proj) * up_proj).astype(bf16)


def column_blocks(near_arr, left, right, name):
    count, quarter = left.shape[0], right.shape[1] // NEAR
    outs = {}
    for k in (3, 1, 2, 0):
        outs[k] = run(
            functools.partial(block_kernel, k), name, shape((count, quarter)), [SMEM, VMEM, VMEM], near_arr, left, right
        )
    return outs


def near_scatter(blocks):
    total = blocks[0].astype(f32)
    for k in (3, 1, 2):
        total = total + swap(blocks[k], k).astype(f32)
    return total


def far_sum(block, far_size):
    sent = block.astype(bf16)
    total = sent.astype(f32)
    for k in range(1, far_size):
        total = total + swap(sent, far_mask(k)).astype(f32)
    return total


def body(
    tokens,
    pick_flags,
    gate_scales,
    attn_gain,
    query_weight,
    key_weight,
    value_matrix,
    output_weight,
    ffn_gain,
    gate_weight,
    up_weight,
    down_weight,
):
    tok_local, width = tokens.shape
    size = lax.axis_size("ctx")
    far_size = size // NEAR
    me = lax.axis_index("ctx")
    far = me // NEAR
    near = quarter_of(me)
    near_arr = near.astype(i32).reshape(1)
    count = PICK_DEV * size
    quarter = width // NEAR
    kernel_mib = 8 if count <= 128 else 24
    flags_row = pick_flags.reshape(1, tok_local)
    attn_gain, ffn_gain = attn_gain.reshape(1, width), ffn_gain.reshape(1, width)

    parts = run(
        pick_kernel, "pick", [shape((MOST, quarter + META))] * NEAR, [SMEM, VMEM, VMEM], near_arr, flags_row, tokens
    )
    key_w, value_w, query_w, done = load((key_weight, value_matrix, query_weight), parts[0], "load_qkv")

    near_rows = jnp.concatenate([parts[0]] + [swap(parts[k], k) for k in (1, 2, 3)], axis=0)
    gate_w, done = load((gate_weight,), near_rows, "load_gate")
    all_rows = jnp.concatenate([near_rows] + [swap(near_rows, far_mask(k)) for k in range(1, far_size)], axis=0)
    slots = size * MOST
    all_index = all_rows[:, quarter].astype(i32)
    order = jnp.arange(slots, dtype=i32)
    far_of = far ^ (order // (NEAR * MOST))
    device_of = far_of * NEAR + (near ^ (order // MOST % NEAR) ^ (far_of & 1) * 2)
    taken = (all_index >= 0).astype(f32)
    earlier = (device_of[:, None] < device_of[None, :]).astype(f32)
    rank_of = jnp.sum(earlier * taken[:, None], axis=0).astype(i32) + order % MOST + done[0, 0]
    pick_ids = jnp.arange(count, dtype=i32)
    select = (pick_ids[:, None] == rank_of[None, :]) & (all_index >= 0)[None, :]
    token_positions = jnp.sum(jnp.where(select, (device_of * tok_local + all_index)[None, :], 0), axis=1)
    select = select.astype(bf16)
    rows_quarter = dot(select, all_rows[:, :quarter]).astype(bf16)
    output_w, done = load((output_weight,), rows_quarter, "load_out")
    row_blocks = [rows_quarter] + [swap(rows_quarter, k) for k in (1, 2, 3)]

    half_dim = HEAD_SIZE // 2
    frequency = rope_base ** (-(jnp.arange(half_dim, dtype=f32) * 2.0) / HEAD_SIZE)
    angles = token_positions.astype(f32)[:, None] * frequency[None, :]
    cosine, sine = jnp.cos(angles), jnp.sin(angles)
    cos_row = jnp.concatenate((cosine, cosine), axis=1)
    sin_row = jnp.concatenate((-sine, sine), axis=1)

    comps = key_weight.shape[1] // KEY_VALUE_HEADS
    heads_here = query_weight.shape[1] // HEAD_SIZE
    group_width = QUERY_HEADS // KEY_VALUE_HEADS
    block_rows = 2 * comps
    total_rows = size * block_rows
    row_id = jnp.arange(total_rows, dtype=i32)
    comp_id, is_value = row_id % comps, row_id // comps % 2
    to_far = far ^ (row_id // block_rows % far_size)
    target = to_far * NEAR + (near ^ (row_id // (block_rows * far_size)) ^ (to_far & 1) * 2)
    column = comp_id * KEY_VALUE_HEADS + target * heads_here // group_width
    col_id = jnp.arange(key_weight.shape[1], dtype=i32)
    place = column[:, None] == col_id[None, :]
    place_k = (place & (is_value == 0)[:, None]).astype(bf16)
    place_v = (place & (is_value == 1)[:, None]).astype(bf16)
    rows_normed, *sends = run(
        kv_kernel,
        "keys_values",
        [shape((count, width))] + [shape((total_rows // NEAR, count))] * NEAR,
        [SMEM] + [VMEM] * 9 + [ANY],
        near_arr,
        *row_blocks,
        attn_gain,
        key_w,
        value_w,
        place_k,
        place_v,
        done,
        limit=kernel_mib,
    )
    got = [sends[0]] + [swap(sends[k], k) for k in (1, 2, 3)]
    raw_q = run(
        matmul_kernel, "query", shape((count, heads_here * HEAD_SIZE), f32), [VMEM, VMEM], rows_normed, query_w
    )
    pieces = []
    for k in range(far_size):
        piece = jnp.concatenate([g[k * block_rows : (k + 1) * block_rows] for g in got], axis=0)
        pieces.append(swap(piece, far_mask(k)) if k else piece)
    raw_kv = jnp.concatenate(pieces, axis=0)
    from_far = far ^ (row_id // (block_rows * NEAR))
    origin = from_far * NEAR + (near ^ (row_id // block_rows % NEAR) ^ (from_far & 1) * 2)
    ordered = jnp.arange(HEAD_SIZE, dtype=i32)[:, None] == (origin * comps + comp_id)[None, :]
    order_k = (ordered & (is_value == 0)[None, :]).astype(bf16)
    order_v = (ordered & (is_value == 1)[None, :]).astype(bf16)
    heads = run(
        attention_kernel,
        "attention",
        shape((count, heads_here * HEAD_SIZE)),
        [VMEM] * 8,
        raw_q,
        raw_kv,
        order_k,
        order_v,
        cos_row,
        sin_row,
        cosine.T,
        sine.T,
        limit=kernel_mib,
    )

    out_blocks = column_blocks(near_arr, heads, output_w, "attn_out")
    attn_near = near_scatter(out_blocks).astype(bf16)
    down_w, done = load((down_weight,), attn_near, "load_down")
    attn_quarter = far_sum(attn_near, far_size) + done[0, 0].astype(f32)
    mixed_quarter = (rows_quarter.astype(f32) + attn_quarter).astype(bf16)
    up_w, done = load((up_weight,), mixed_quarter, "load_up")
    mixed_blocks = [mixed_quarter] + [swap(mixed_quarter, k) for k in (1, 2, 3)]
    hidden = run(
        hidden_kernel,
        "hidden",
        shape((count, gate_weight.shape[1])),
        [SMEM] + [VMEM] * 7,
        near_arr,
        *mixed_blocks,
        ffn_gain,
        gate_w,
        up_w,
        scratch=[pltpu.VMEM((count, width), bf16)],
        limit=kernel_mib,
    )
    ffn_part = near_scatter(column_blocks(near_arr, hidden, down_w, "ffn_out")).astype(bf16)

    spread = select.reshape(count, far_size, NEAR * MOST)
    delta = dot_tn(spread[:, 0], ffn_part) + dot_tn(spread[:, 0], attn_quarter.astype(bf16))
    for k in range(1, far_size):
        delta = delta + swap(dot_tn(spread[:, k], ffn_part).astype(bf16), far_mask(k)).astype(f32)
    delta = delta.astype(bf16).reshape(NEAR, MOST, quarter)
    back = [delta[0]] + [swap(delta[k], k) for k in (1, 2, 3)]
    return run(
        put_kernel,
        "put",
        shape((tok_local, width)),
        [SMEM] + [VMEM] * 7,
        near_arr,
        flags_row,
        gate_scales.reshape(1, tok_local),
        tokens,
        *back,
    )


def solution(mesh):
    in_specs = (
        P(("dp", "ctx"), None),
        P(("dp", "ctx")),
        P(("dp", "ctx")),
        P(),
        P(None, "ctx"),
        P(None, "ctx"),
        P(None, "ctx"),
        P("ctx", None),
        P(),
        P(None, "ctx"),
        P(None, "ctx"),
        P("ctx", None),
    )
    out_specs = P(("dp", "ctx"), None)
    return jax.shard_map(body, mesh=mesh, in_specs=in_specs, out_specs=out_specs, check_vma=False)
```

time: 155 us -> 135 us (0.87)
  Pallas kernels: 0 us -> 32.1 us
  matrix products: 30 us -> 1.04 us
  waiting for transfers between devices: 70.2 us -> 53.1 us
  starting transfers between devices: 45.9 us -> 40.7 us
    pallas_call x0 -> x19, Pallas kernels: none -> 32.1 us  [the longest x5 19.1 us: load(): pl.pallas_call(kernel, in_specs=[HBM] * count + [ANY], out_specs=[VMEM] *...]
    dot_general x11 -> x1, matrix products: 27.2 us -> 0.23 us  [dot(): return jnp.dot(a, b, preferred_element_type=f32)]
    ppermute x25, waiting for transfers between devices: 70.2 us -> 53.1 us  [swap(): return lax.ppermute(value, 'ctx', [(i, i ^ mask) for i in range(size)])]
    ppermute x25, starting transfers between devices: 45.9 us -> 40.7 us  [swap(): return lax.ppermute(value, 'ctx', [(i, i ^ mask) for i in range(size)])]
    dot_general x3, matrix products: 2.84 us -> 0.82 us  [dot_tn(): lax.dot_general(a, b, (((0,), (0,)), ((), ())), preferred_element_type=f32)]
  transfers between devices with their start and end apart: 25 -> 25, of which waited for: 21 -> 20; matrix products, arithmetic and copies ran while one was open for 1% -> 2% of each run, Pallas kernels for 0% -> 15%
where the time goes in v3:
time: 135 us; the launch traced here: 134 us
  waiting for transfers between devices  53.1 us (39%)
  starting transfers between devices  40.7 us (30%)
  Pallas kernels  32.1 us (24%)
  other arithmetic  3.31 us (2%)
  local copies, waits for them, and re-layouts  3.12 us (2%)
    ppermute x25, waiting for transfers between devices, swap(): return lax.ppermute(value, 'ctx', [(i, i ^ mask) for i in range(size)])  53.1 us
    ppermute x25, starting transfers between devices, swap(): return lax.ppermute(value, 'ctx', [(i, i ^ mask) for i in range(size)])  40.7 us
    pallas_call x5, Pallas kernels, load(): pl.pallas_call(kernel, in_specs=[HBM] * count + [ANY], out_specs=[VMEM] *...  19.1 us
    pallas_call x14, Pallas kernels, run(): pl.pallas_call(kernel, in_specs=specs, out_specs=outs, out_shape=out_shap...  13 us
  transfers between devices with their start and end apart: 25, of which 20 were waited for; matrix products, arithmetic and copies ran while one was open for 2% of the time, Pallas kernels for 15%

profile of v3, /device:TPU:0, one launch (start us, length us, event | category | flops | bytes accessed | tf_op | source)
XLA Modules:
  0.0 134.5 jit_solution(4694366976936529142)
XLA Ops:
  2.3 3.0 %collective-permute-start = (bf16[32,1152]{1,0:T(8,128)(2,1)S(1)}, bf16[32,1152]{1,0:T(8,128)(2,1)S(1)}, u32[]{:S(2)}, u32[]{:S(2)}) collective-permute-start(bf16[32,1152]{1,0:T(8,128)(2,1)S(1)} %get-tuple-element.25), channel_id=1, source_target_pairs={{0,1},{1,0},{2,3},{3,2},{4,5},{5,4},{6,7},{7,6},{8,9},{9,8},{10,11... | collective-permute-start | bytes 221192 | tf_op jit(solution)/shard_map/ppermute | solution.py:34
  5.3 1.6 %collective-permute-start.1 = (bf16[32,1152]{1,0:T(8,128)(2,1)S(1)}, bf16[32,1152]{1,0:T(8,128)(2,1)S(1)}, u32[]{:S(2)}, u32[]{:S(2)}) collective-permute-start(bf16[32,1152]{1,0:T(8,128)(2,1)S(1)} %get-tuple-element.26), channel_id=1, source_target_pairs={{0,2},{1,3},{2,0},{3,1},{4,6},{5,7},{6,4},{7,5},{8,10},{9,11},{10,... | collective-permute-start | bytes 221192 | tf_op jit(solution)/shard_map/ppermute | solution.py:34
  7.0 3.5 %load_qkv.1 = (bf16[4096,128]{1,0:T(8,128)(2,1)S(1)}, bf16[4096,128]{1,0:T(8,128)(2,1)S(1)}, bf16[4096,512]{1,0:T(8,128)(2,1)S(1)}, s32[8,128]{1,0:T(8,128)}) custom-call(bf16[4096,128]{1,0:T(8,128)(2,1)} %refs_0_.6, bf16[4096,128]{1,0:T(8,128)(2,1)} %refs_1_.1, bf16[4096,512]{1,0:T(8,128)(2,1)} %refs_2_.1, bf16[32,1152]{1,0:T(8,128)(2,1)S(1)} %get-tuple-element.24.refs_3_), custom_call_target="tpu_custom_call" | custom-call | tf_op jit(solution)/shard_map/load_qkv/pallas_call | solution.py:93
  10.6 1.6 %collective-permute-done.2 = bf16[32,1152]{1,0:T(8,128)(2,1)S(1)} collective-permute-done((bf16[32,1152]{1,0:T(8,128)(2,1)S(1)}, bf16[32,1152]{1,0:T(8,128)(2,1)S(1)}, u32[]{:S(2)}, u32[]{:S(2)}) %collective-permute-start.2) | collective-permute-done | bytes 73760 | tf_op jit(solution)/shard_map/ppermute | solution.py:34
  12.2 2.5 %collective-permute-start.3 = (bf16[128,1152]{1,0:T(8,128)(2,1)S(1)}, bf16[128,1152]{1,0:T(8,128)(2,1)S(1)}, u32[]{:S(2)}, u32[]{:S(2)}) collective-permute-start(bf16[128,1152]{1,0:T(8,128)(2,1)S(1)} %get-tuple-element.47.refs_1_), channel_id=1, source_target_pairs={{0,6},{1,7},{2,4},{3,5},{4,2},{5,3},{6,0},{7,1},{8,14},{9,15},{10,... | collective-permute-start | bytes 884744 | tf_op jit(solution)/shard_map/ppermute | solution.py:34
  14.9 4.3 %load_gate.1 = (bf16[4096,1408]{1,0:T(8,128)(2,1)S(1)}, s32[8,128]{1,0:T(8,128)S(1)}) custom-call(bf16[4096,1408]{1,0:T(8,128)(2,1)} %refs_0_.5, bf16[128,1152]{1,0:T(8,128)(2,1)S(1)} %get-tuple-element.47.refs_1_), custom_call_target="tpu_custom_call" | custom-call | tf_op jit(solution)/shard_map/load_gate/pallas_call | solution.py:93
  22.5 6.7 %collective-permute-start.6 = (bf16[128,1024]{1,0:T(8,128)(2,1)S(1)}, bf16[128,1024]{1,0:T(8,128)(2,1)S(1)}, u32[]{:S(2)}, u32[]{:S(2)}) collective-permute-start(bf16[128,1024]{1,0:T(8,128)(2,1)S(1)} %convolution_convert_fusion.1.refs_1_.b0), channel_id=1, source_target_pairs={{0,3},{1,2},{2,1},{3,0},{4,7},{5,6},{6,5},{7,4},{8,11},{9,10},{10,... | collective-permute-start | bytes 786440 | tf_op jit(solution)/shard_map/ppermute | solution.py:34
  30.2 2.2 %load_out.1 = (bf16[512,4096]{1,0:T(8,128)(2,1)S(1)}, s32[8,128]{1,0:T(8,128)S(1)}) custom-call(bf16[512,4096]{1,0:T(8,128)(2,1)} %refs_0_.7, bf16[128,1024]{1,0:T(8,128)(2,1)S(1)} %convolution_convert_fusion.1.refs_1_.b0), custom_call_target="tpu_custom_call" | custom-call | tf_op jit(solution)/shard_map/load_out/pallas_call | solution.py:93
  32.7 3.7 %collective-permute-done.6.b3 = bf16[128,1024]{1,0:T(8,128)(2,1)S(1)} collective-permute-done((bf16[128,1024]{1,0:T(8,128)(2,1)S(1)}, bf16[128,1024]{1,0:T(8,128)(2,1)S(1)}, u32[]{:S(2)}, u32[]{:S(2)}) %collective-permute-start.6) | collective-permute-done | bytes 262176 | tf_op jit(solution)/shard_map/ppermute | solution.py:34
  36.5 3.2 %collective-permute-done.5.b2 = bf16[128,1024]{1,0:T(8,128)(2,1)S(1)} collective-permute-done((bf16[128,1024]{1,0:T(8,128)(2,1)S(1)}, bf16[128,1024]{1,0:T(8,128)(2,1)S(1)}, u32[]{:S(2)}, u32[]{:S(2)}) %collective-permute-start.5) | collective-permute-done | bytes 262176 | tf_op jit(solution)/shard_map/ppermute | solution.py:34
  40.4 1.5 %keys_values.1 = (bf16[128,4096]{1,0:T(8,128)(2,1)S(1)}, bf16[64,128]{1,0:T(8,128)(2,1)S(1)}, bf16[64,128]{1,0:T(8,128)(2,1)S(1)}, bf16[64,128]{1,0:T(8,128)(2,1)S(1)}, bf16[64,128]{1,0:T(8,128)(2,1)S(1)}) custom-call(s32[1]{0:T(128)} %bitcast.near, bf16[128,1024]{1,0:T(8,128)(2,1)S(1)} %convolution_convert_fusion.1.refs_1_.b0, ...), custom_call_target="tpu_custom_call" | custom-call | tf_op jit(solution)/shard_map/keys_values/pallas_call | solution.py:67
  42.6 2.6 %collective-permute-start.8 = (bf16[64,128]{1,0:T(8,128)(2,1)S(1)}, bf16[64,128]{1,0:T(8,128)(2,1)S(1)}, u32[]{:S(2)}, u32[]{:S(2)}) collective-permute-start(bf16[64,128]{1,0:T(8,128)(2,1)S(1)} %get-tuple-element.36), channel_id=1, source_target_pairs={{0,2},{1,3},{2,0},{3,1},{4,6},{5,7},{6,4},{7,5},{8,10},{9,11},{10,... | collective-permute-start | bytes 49160 | tf_op jit(solution)/shard_map/ppermute | solution.py:34
  46.9 2.9 %collective-permute-done.9 = bf16[64,128]{1,0:T(8,128)(2,1)S(1)} collective-permute-done((bf16[64,128]{1,0:T(8,128)(2,1)S(1)}, bf16[64,128]{1,0:T(8,128)(2,1)S(1)}, u32[]{:S(2)}, u32[]{:S(2)}) %collective-permute-start.9) | collective-permute-done | bytes 16416 | tf_op jit(solution)/shard_map/ppermute | solution.py:34
  52.1 3.5 %collective-permute-done.10 = bf16[128,128]{1,0:T(8,128)(2,1)S(1)} collective-permute-done((bf16[128,128]{1,0:T(8,128)(2,1)S(1)}, bf16[128,128]{1,0:T(8,128)(2,1)S(1)}, u32[]{:S(2)}, u32[]{:S(2)}) %collective-permute-start.10) | collective-permute-done | bytes 32800 | tf_op jit(solution)/shard_map/ppermute | solution.py:34
  58.3 2.8 %collective-permute-start.13 = (bf16[128,1024]{1,0:T(8,128)(2,1)S(1)}, bf16[128,1024]{1,0:T(8,128)(2,1)S(1)}, u32[]{:S(2)}, u32[]{:S(2)}) collective-permute-start(bf16[128,1024]{1,0:T(8,128)(2,1)S(1)} %attn_out.7), channel_id=1, source_target_pairs={{0,2},{1,3},{2,0},{3,1},{4,6},{5,7},{6,4},{7,5},{8,10},{9,11},{10,... | collective-permute-start | bytes 786440 | tf_op jit(solution)/shard_map/ppermute | solution.py:34
  61.5 5.4 %collective-permute-done.11 = bf16[128,1024]{1,0:T(8,128)(2,1)S(1)} collective-permute-done((bf16[128,1024]{1,0:T(8,128)(2,1)S(1)}, bf16[128,1024]{1,0:T(8,128)(2,1)S(1)}, u32[]{:S(2)}, u32[]{:S(2)}) %collective-permute-start.11) | collective-permute-done | bytes 262176 | tf_op jit(solution)/shard_map/ppermute | solution.py:34
  66.9 1.8 %collective-permute-done.12 = bf16[128,1024]{1,0:T(8,128)(2,1)S(1)} collective-permute-done((bf16[128,1024]{1,0:T(8,128)(2,1)S(1)}, bf16[128,1024]{1,0:T(8,128)(2,1)S(1)}, u32[]{:S(2)}, u32[]{:S(2)}) %collective-permute-start.12) | collective-permute-done | bytes 262176 | tf_op jit(solution)/shard_map/ppermute | solution.py:34
  70.3 4.3 %load_down.1 = (bf16[1408,4096]{1,0:T(8,128)(2,1)S(1)}, s32[8,128]{1,0:T(8,128)S(1)}) custom-call(bf16[1408,4096]{1,0:T(8,128)(2,1)} %refs_0_.8, bf16[128,1024]{1,0:T(8,128)(2,1)S(1)} %add_convert_fusion.2.refs_1_), custom_call_target="tpu_custom_call" | custom-call | tf_op jit(solution)/shard_map/load_down/pallas_call | solution.py:93
  75.8 2.4 %collective-permute-done.14 = bf16[128,1024]{1,0:T(8,128)(2,1)S(1)} collective-permute-done((bf16[128,1024]{1,0:T(8,128)(2,1)S(1)}, bf16[128,1024]{1,0:T(8,128)(2,1)S(1)}, u32[]{:S(2)}, u32[]{:S(2)}) %collective-permute-start.14) | collective-permute-done | bytes 262176 | tf_op jit(solution)/shard_map/ppermute | solution.py:34
  78.3 4.1 %collective-permute-start.17 = (bf16[128,1024]{1,0:T(8,128)(2,1)S(1)}, bf16[128,1024]{1,0:T(8,128)(2,1)S(1)}, u32[]{:S(2)}, u32[]{:S(2)}) collective-permute-start(bf16[128,1024]{1,0:T(8,128)(2,1)S(1)} %add_convert_fusion.1.refs_1_.b0), channel_id=1, source_target_pairs={{0,3},{1,2},{2,1},{3,0},{4,7},{5,6},{6,5},{7,4},{8,11},{9,10},{10,... | collective-permute-start | bytes 786440 | tf_op jit(solution)/shard_map/ppermute | solution.py:34
  83.7 4.9 %load_up.1 = (bf16[4096,1408]{1,0:T(8,128)(2,1)S(1)}, s32[8,128]{1,0:T(8,128)}) custom-call(bf16[4096,1408]{1,0:T(8,128)(2,1)} %refs_0_.9, bf16[128,1024]{1,0:T(8,128)(2,1)S(1)} %add_convert_fusion.1.refs_1_.b0), custom_call_target="tpu_custom_call" | custom-call | tf_op jit(solution)/shard_map/load_up/pallas_call | solution.py:93
  89.6 2.3 %collective-permute-done.16.b2 = bf16[128,1024]{1,0:T(8,128)(2,1)S(1)} collective-permute-done((bf16[128,1024]{1,0:T(8,128)(2,1)S(1)}, bf16[128,1024]{1,0:T(8,128)(2,1)S(1)}, u32[]{:S(2)}, u32[]{:S(2)}) %collective-permute-start.16) | collective-permute-done | bytes 262176 | tf_op jit(solution)/shard_map/ppermute | solution.py:34
  92.6 4.2 %hidden.1.left = bf16[128,1408]{1,0:T(8,128)(2,1)S(1)} custom-call(s32[1]{0:T(128)} %bitcast.near, bf16[128,1024]{1,0:T(8,128)(2,1)S(1)} %add_convert_fusion.1.refs_1_.b0, bf16[128,1024]{1,0:T(8,128)(2,1)S(1)} %collective-permute-done.15.b1, bf16[128,1024]{1,0:T(8,128)(2,1)S(1)} %collective-permute-done.16.b2, ...), custom_call_target="tpu_custom_call" | custom-call | tf_op jit(solution)/shard_map/hidden/pallas_call | solution.py:67
  98.7 2.7 %collective-permute-start.18 = (bf16[128,1024]{1,0:T(8,128)(2,1)S(1)}, bf16[128,1024]{1,0:T(8,128)(2,1)S(1)}, u32[]{:S(2)}, u32[]{:S(2)}) collective-permute-start(bf16[128,1024]{1,0:T(8,128)(2,1)S(1)} %ffn_out.5), channel_id=1, source_target_pairs={{0,3},{1,2},{2,1},{3,0},{4,7},{5,6},{6,5},{7,4},{8,11},{9,10},{10,... | collective-permute-start | bytes 786440 | tf_op jit(solution)/shard_map/ppermute | solution.py:34
  103.0 5.9 %collective-permute-done.18 = bf16[128,1024]{1,0:T(8,128)(2,1)S(1)} collective-permute-done((bf16[128,1024]{1,0:T(8,128)(2,1)S(1)}, bf16[128,1024]{1,0:T(8,128)(2,1)S(1)}, u32[]{:S(2)}, u32[]{:S(2)}) %collective-permute-start.18) | collective-permute-done | bytes 262176 | tf_op jit(solution)/shard_map/ppermute | solution.py:34
  108.9 4.0 %collective-permute-done.19 = bf16[128,1024]{1,0:T(8,128)(2,1)S(1)} collective-permute-done((bf16[128,1024]{1,0:T(8,128)(2,1)S(1)}, bf16[128,1024]{1,0:T(8,128)(2,1)S(1)}, u32[]{:S(2)}, u32[]{:S(2)}) %collective-permute-start.19) | collective-permute-done | bytes 262176 | tf_op jit(solution)/shard_map/ppermute | solution.py:34
  113.4 2.1 %collective-permute-start.21 = (bf16[128,1024]{1,0:T(8,128)(2,1)S(1)}, bf16[128,1024]{1,0:T(8,128)(2,1)S(1)}, u32[]{:S(2)}, u32[]{:S(2)}) collective-permute-start(bf16[128,1024]{1,0:T(8,128)(2,1)S(1)} %convolution_convert_fusion), channel_id=1, source_target_pairs={{0,6},{1,7},{2,4},{3,5},{4,2},{5,3},{6,0},{7,1},{8,14},{9,15},{10,... | collective-permute-start | bytes 786440 | tf_op jit(solution)/shard_map/ppermute | solution.py:34
  115.8 7.8 %collective-permute-done.21 = bf16[128,1024]{1,0:T(8,128)(2,1)S(1)} collective-permute-done((bf16[128,1024]{1,0:T(8,128)(2,1)S(1)}, bf16[128,1024]{1,0:T(8,128)(2,1)S(1)}, u32[]{:S(2)}, u32[]{:S(2)}) %collective-permute-start.21) | collective-permute-done | bytes 262176 | tf_op jit(solution)/shard_map/ppermute | solution.py:34
  123.9 4.7 %collective-permute-start.24 = (bf16[32,1024]{1,0:T(8,128)(2,1)S(1)}, bf16[32,1024]{1,0:T(8,128)(2,1)S(1)}, u32[]{:S(2)}, u32[]{:S(2)}) collective-permute-start(bf16[32,1024]{1,0:T(8,128)(2,1)S(1)} %get-tuple-element.43), channel_id=1, source_target_pairs={{0,3},{1,2},{2,1},{3,0},{4,7},{5,6},{6,5},{7,4},{8,11},{9,10},{10,... | collective-permute-start | bytes 196616 | tf_op jit(solution)/shard_map/ppermute | solution.py:34
  129.7 1.5 %collective-permute-done.24.refs_3_ = bf16[32,1024]{1,0:T(8,128)(2,1)S(1)} collective-permute-done((bf16[32,1024]{1,0:T(8,128)(2,1)S(1)}, bf16[32,1024]{1,0:T(8,128)(2,1)S(1)}, u32[]{:S(2)}, u32[]{:S(2)}) %collective-permute-start.24) | collective-permute-done | bytes 65568 | tf_op jit(solution)/shard_map/ppermute | solution.py:34
  131.2 1.7 %collective-permute-done.23.refs_2_ = bf16[32,1024]{1,0:T(8,128)(2,1)S(1)} collective-permute-done((bf16[32,1024]{1,0:T(8,128)(2,1)S(1)}, bf16[32,1024]{1,0:T(8,128)(2,1)S(1)}, u32[]{:S(2)}, u32[]{:S(2)}) %collective-permute-start.23) | collective-permute-done | bytes 65568 | tf_op jit(solution)/shard_map/ppermute | solution.py:34
  132.9 1.6 %put.1 = bf16[128,4096]{1,0:T(8,128)(2,1)} custom-call(s32[1]{0:T(128)} %bitcast.near, s32[1,128]{1,0:T(1,128)S(1)} %bitcast.24, bf16[1,128]{1,0:T(2,128)(2,1)S(1)} %bitcast.25, bf16[128,4096]{1,0:T(8,128)(2,1)S(1)} %copy-done.1, bf16[32,1024]{1,0:T(8,128)(2,1)S(1)} %get-tuple-element.46.refs_0_, bf16[32,1024]{1,0:T(8,128)(2,1)S(1)} %collective-permute-done.22.refs_1_, ...), custom_call_target="tpu_custom_call" | custom-call | tf_op jit(solution)/shard_map/put/pallas_call | solution.py:67
  (92 shorter events, 26.3 us)
Async XLA Ops:
  0.0 1.2 copy-start
  1.2 0.7 copy-start.4
  2.3 8.2 %collective-permute-start = (bf16[32,1152]{1,0:T(8,128)(2,1)S(1)}, bf16[32,1152]{1,0:T(8,128)(2,1)S(1)}, u32[]{:S(2)}, u32[]{:S(2)}) collective-permute-start(bf16[32,1152]{1,0:T(8,128)(2,1)S(1)} %get-tuple-element.25), channel_id=1, source_target_pairs={{0,1},{1,0},{2,3},{3,2},{4,5},{5,4},{6,7},{7,6},{8,9},{9,8},{10,11... | collective-permute-start | bytes 221192 | tf_op jit(solution)/shard_map/ppermute | solution.py:34
  5.3 5.2 %collective-permute-start.1 = (bf16[32,1152]{1,0:T(8,128)(2,1)S(1)}, bf16[32,1152]{1,0:T(8,128)(2,1)S(1)}, u32[]{:S(2)}, u32[]{:S(2)}) collective-permute-start(bf16[32,1152]{1,0:T(8,128)(2,1)S(1)} %get-tuple-element.26), channel_id=1, source_target_pairs={{0,2},{1,3},{2,0},{3,1},{4,6},{5,7},{6,4},{7,5},{8,10},{9,11},{10,... | collective-permute-start | bytes 221192 | tf_op jit(solution)/shard_map/ppermute | solution.py:34
  6.9 5.3 %collective-permute-start.2 = (bf16[32,1152]{1,0:T(8,128)(2,1)S(1)}, bf16[32,1152]{1,0:T(8,128)(2,1)S(1)}, u32[]{:S(2)}, u32[]{:S(2)}) collective-permute-start(bf16[32,1152]{1,0:T(8,128)(2,1)S(1)} %get-tuple-element.27), channel_id=1, source_target_pairs={{0,3},{1,2},{2,1},{3,0},{4,7},{5,6},{6,5},{7,4},{8,11},{9,10},{10,... | collective-permute-start | bytes 221192 | tf_op jit(solution)/shard_map/ppermute | solution.py:34
  7.0 33.4 %copy-start.2 = (f32[4096]{0:T(1024)S(1)}, f32[4096]{0:T(1024)}, u32[]{:S(2)}) copy-start(f32[4096]{0:T(1024)} %param.15) | copy-start | bytes 49156
  12.2 9.0 %collective-permute-start.3 = (bf16[128,1152]{1,0:T(8,128)(2,1)S(1)}, bf16[128,1152]{1,0:T(8,128)(2,1)S(1)}, u32[]{:S(2)}, u32[]{:S(2)}) collective-permute-start(bf16[128,1152]{1,0:T(8,128)(2,1)S(1)} %get-tuple-element.47.refs_1_), channel_id=1, source_target_pairs={{0,6},{1,7},{2,4},{3,5},{4,2},{5,3},{6,0},{7,1},{8,14},{9,15},{10,... | collective-permute-start | bytes 884744 | tf_op jit(solution)/shard_map/ppermute | solution.py:34
  22.5 14.0 %collective-permute-start.6 = (bf16[128,1024]{1,0:T(8,128)(2,1)S(1)}, bf16[128,1024]{1,0:T(8,128)(2,1)S(1)}, u32[]{:S(2)}, u32[]{:S(2)}) collective-permute-start(bf16[128,1024]{1,0:T(8,128)(2,1)S(1)} %convolution_convert_fusion.1.refs_1_.b0), channel_id=1, source_target_pairs={{0,3},{1,2},{2,1},{3,0},{4,7},{5,6},{6,5},{7,4},{8,11},{9,10},{10,... | collective-permute-start | bytes 786440 | tf_op jit(solution)/shard_map/ppermute | solution.py:34
  29.2 10.5 %collective-permute-start.5 = (bf16[128,1024]{1,0:T(8,128)(2,1)S(1)}, bf16[128,1024]{1,0:T(8,128)(2,1)S(1)}, u32[]{:S(2)}, u32[]{:S(2)}) collective-permute-start(bf16[128,1024]{1,0:T(8,128)(2,1)S(1)} %convolution_convert_fusion.1.refs_1_.b0), channel_id=1, source_target_pairs={{0,2},{1,3},{2,0},{3,1},{4,6},{5,7},{6,4},{7,5},{8,10},{9,11},{10,... | collective-permute-start | bytes 786440 | tf_op jit(solution)/shard_map/ppermute | solution.py:34
  29.2 11.2 %collective-permute-start.4 = (bf16[128,1024]{1,0:T(8,128)(2,1)S(1)}, bf16[128,1024]{1,0:T(8,128)(2,1)S(1)}, u32[]{:S(2)}, u32[]{:S(2)}) collective-permute-start(bf16[128,1024]{1,0:T(8,128)(2,1)S(1)} %convolution_convert_fusion.1.refs_1_.b0), channel_id=1, source_target_pairs={{0,1},{1,0},{2,3},{3,2},{4,5},{5,4},{6,7},{7,6},{8,9},{9,8},{10,11... | collective-permute-start | bytes 786440 | tf_op jit(solution)/shard_map/ppermute | solution.py:34
  41.9 3.8 %collective-permute-start.7 = (bf16[64,128]{1,0:T(8,128)(2,1)S(1)}, bf16[64,128]{1,0:T(8,128)(2,1)S(1)}, u32[]{:S(2)}, u32[]{:S(2)}) collective-permute-start(bf16[64,128]{1,0:T(8,128)(2,1)S(1)} %get-tuple-element.35), channel_id=1, source_target_pairs={{0,1},{1,0},{2,3},{3,2},{4,5},{5,4},{6,7},{7,6},{8,9},{9,8},{10,11... | collective-permute-start | bytes 49160 | tf_op jit(solution)/shard_map/ppermute | solution.py:34
  42.6 4.3 %collective-permute-start.8 = (bf16[64,128]{1,0:T(8,128)(2,1)S(1)}, bf16[64,128]{1,0:T(8,128)(2,1)S(1)}, u32[]{:S(2)}, u32[]{:S(2)}) collective-permute-start(bf16[64,128]{1,0:T(8,128)(2,1)S(1)} %get-tuple-element.36), channel_id=1, source_target_pairs={{0,2},{1,3},{2,0},{3,1},{4,6},{5,7},{6,4},{7,5},{8,10},{9,11},{10,... | collective-permute-start | bytes 49160 | tf_op jit(solution)/shard_map/ppermute | solution.py:34
  45.2 4.6 %collective-permute-start.9 = (bf16[64,128]{1,0:T(8,128)(2,1)S(1)}, bf16[64,128]{1,0:T(8,128)(2,1)S(1)}, u32[]{:S(2)}, u32[]{:S(2)}) collective-permute-start(bf16[64,128]{1,0:T(8,128)(2,1)S(1)} %get-tuple-element.37), channel_id=1, source_target_pairs={{0,3},{1,2},{2,1},{3,0},{4,7},{5,6},{6,5},{7,4},{8,11},{9,10},{10,... | collective-permute-start | bytes 49160 | tf_op jit(solution)/shard_map/ppermute | solution.py:34
  49.8 5.8 %collective-permute-start.10 = (bf16[128,128]{1,0:T(8,128)(2,1)S(1)}, bf16[128,128]{1,0:T(8,128)(2,1)S(1)}, u32[]{:S(2)}, u32[]{:S(2)}) collective-permute-start(bf16[128,128]{1,0:T(8,128)(2,1)S(1)} %pad_maximum_fusion.2), channel_id=1, source_target_pairs={{0,6},{1,7},{2,4},{3,5},{4,2},{5,3},{6,0},{7,1},{8,14},{9,15},{10,... | collective-permute-start | bytes 98312 | tf_op jit(solution)/shard_map/ppermute | solution.py:34
  57.6 9.3 %collective-permute-start.11 = (bf16[128,1024]{1,0:T(8,128)(2,1)S(1)}, bf16[128,1024]{1,0:T(8,128)(2,1)S(1)}, u32[]{:S(2)}, u32[]{:S(2)}) collective-permute-start(bf16[128,1024]{1,0:T(8,128)(2,1)S(1)} %attn_out.5), channel_id=1, source_target_pairs={{0,3},{1,2},{2,1},{3,0},{4,7},{5,6},{6,5},{7,4},{8,11},{9,10},{10,... | collective-permute-start | bytes 786440 | tf_op jit(solution)/shard_map/ppermute | solution.py:34
  57.7 11.1 %collective-permute-start.12 = (bf16[128,1024]{1,0:T(8,128)(2,1)S(1)}, bf16[128,1024]{1,0:T(8,128)(2,1)S(1)}, u32[]{:S(2)}, u32[]{:S(2)}) collective-permute-start(bf16[128,1024]{1,0:T(8,128)(2,1)S(1)} %attn_out.6), channel_id=1, source_target_pairs={{0,1},{1,0},{2,3},{3,2},{4,5},{5,4},{6,7},{7,6},{8,9},{9,8},{10,11... | collective-permute-start | bytes 786440 | tf_op jit(solution)/shard_map/ppermute | solution.py:34
  58.3 10.4 %collective-permute-start.13 = (bf16[128,1024]{1,0:T(8,128)(2,1)S(1)}, bf16[128,1024]{1,0:T(8,128)(2,1)S(1)}, u32[]{:S(2)}, u32[]{:S(2)}) collective-permute-start(bf16[128,1024]{1,0:T(8,128)(2,1)S(1)} %attn_out.7), channel_id=1, source_target_pairs={{0,2},{1,3},{2,0},{3,1},{4,6},{5,7},{6,4},{7,5},{8,10},{9,11},{10,... | collective-permute-start | bytes 786440 | tf_op jit(solution)/shard_map/ppermute | solution.py:34
  68.9 23.7 %copy-start.3 = (f32[4096]{0:T(1024)S(1)}, f32[4096]{0:T(1024)}, u32[]{:S(2)}) copy-start(f32[4096]{0:T(1024)} %param.20) | copy-start | bytes 49156
  68.9 9.3 %collective-permute-start.14 = (bf16[128,1024]{1,0:T(8,128)(2,1)S(1)}, bf16[128,1024]{1,0:T(8,128)(2,1)S(1)}, u32[]{:S(2)}, u32[]{:S(2)}) collective-permute-start(bf16[128,1024]{1,0:T(8,128)(2,1)S(1)} %add_convert_fusion.2.refs_1_), channel_id=1, source_target_pairs={{0,6},{1,7},{2,4},{3,5},{4,2},{5,3},{6,0},{7,1},{8,14},{9,15},{10,... | collective-permute-start | bytes 786440 | tf_op jit(solution)/shard_map/ppermute | solution.py:34
  78.3 11.3 %collective-permute-start.17 = (bf16[128,1024]{1,0:T(8,128)(2,1)S(1)}, bf16[128,1024]{1,0:T(8,128)(2,1)S(1)}, u32[]{:S(2)}, u32[]{:S(2)}) collective-permute-start(bf16[128,1024]{1,0:T(8,128)(2,1)S(1)} %add_convert_fusion.1.refs_1_.b0), channel_id=1, source_target_pairs={{0,3},{1,2},{2,1},{3,0},{4,7},{5,6},{6,5},{7,4},{8,11},{9,10},{10,... | collective-permute-start | bytes 786440 | tf_op jit(solution)/shard_map/ppermute | solution.py:34
  82.4 9.5 %collective-permute-start.16 = (bf16[128,1024]{1,0:T(8,128)(2,1)S(1)}, bf16[128,1024]{1,0:T(8,128)(2,1)S(1)}, u32[]{:S(2)}, u32[]{:S(2)}) collective-permute-start(bf16[128,1024]{1,0:T(8,128)(2,1)S(1)} %add_convert_fusion.1.refs_1_.b0), channel_id=1, source_target_pairs={{0,2},{1,3},{2,0},{3,1},{4,6},{5,7},{6,4},{7,5},{8,10},{9,11},{10,... | collective-permute-start | bytes 786440 | tf_op jit(solution)/shard_map/ppermute | solution.py:34
  82.4 10.2 %collective-permute-start.15 = (bf16[128,1024]{1,0:T(8,128)(2,1)S(1)}, bf16[128,1024]{1,0:T(8,128)(2,1)S(1)}, u32[]{:S(2)}, u32[]{:S(2)}) collective-permute-start(bf16[128,1024]{1,0:T(8,128)(2,1)S(1)} %add_convert_fusion.1.refs_1_.b0), channel_id=1, source_target_pairs={{0,1},{1,0},{2,3},{3,2},{4,5},{5,4},{6,7},{7,6},{8,9},{9,8},{10,11... | collective-permute-start | bytes 786440 | tf_op jit(solution)/shard_map/ppermute | solution.py:34
  98.6 34.3 %copy-start.1 = (bf16[128,4096]{1,0:T(8,128)(2,1)S(1)}, bf16[128,4096]{1,0:T(8,128)(2,1)}, u32[]{:S(2)}) copy-start(bf16[128,4096]{1,0:T(8,128)(2,1)} %tokens.3) | copy-start | bytes 3145732
  98.6 34.2 %copy-start.5 = (s32[128]{0:T(128)S(1)}, s32[128]{0:T(128)}, u32[]{:S(2)}) copy-start(s32[128]{0:T(128)} %param.13) | copy-start | bytes 1540
  98.6 34.2 %copy-start.6 = (bf16[128]{0:T(256)(128)(2,1)S(1)}, bf16[128]{0:T(256)(128)(2,1)}, u32[]{:S(2)}) copy-start(bf16[128]{0:T(256)(128)(2,1)} %param.14) | copy-start | bytes 772
  98.7 10.3 %collective-permute-start.18 = (bf16[128,1024]{1,0:T(8,128)(2,1)S(1)}, bf16[128,1024]{1,0:T(8,128)(2,1)S(1)}, u32[]{:S(2)}, u32[]{:S(2)}) collective-permute-start(bf16[128,1024]{1,0:T(8,128)(2,1)S(1)} %ffn_out.5), channel_id=1, source_target_pairs={{0,3},{1,2},{2,1},{3,0},{4,7},{5,6},{6,5},{7,4},{8,11},{9,10},{10,... | collective-permute-start | bytes 786440 | tf_op jit(solution)/shard_map/ppermute | solution.py:34
  101.4 11.6 %collective-permute-start.19 = (bf16[128,1024]{1,0:T(8,128)(2,1)S(1)}, bf16[128,1024]{1,0:T(8,128)(2,1)S(1)}, u32[]{:S(2)}, u32[]{:S(2)}) collective-permute-start(bf16[128,1024]{1,0:T(8,128)(2,1)S(1)} %ffn_out.6), channel_id=1, source_target_pairs={{0,1},{1,0},{2,3},{3,2},{4,5},{5,4},{6,7},{7,6},{8,9},{9,8},{10,11... | collective-permute-start | bytes 786440 | tf_op jit(solution)/shard_map/ppermute | solution.py:34
  102.0 10.9 %collective-permute-start.20 = (bf16[128,1024]{1,0:T(8,128)(2,1)S(1)}, bf16[128,1024]{1,0:T(8,128)(2,1)S(1)}, u32[]{:S(2)}, u32[]{:S(2)}) collective-permute-start(bf16[128,1024]{1,0:T(8,128)(2,1)S(1)} %ffn_out.7), channel_id=1, source_target_pairs={{0,2},{1,3},{2,0},{3,1},{4,6},{5,7},{6,4},{7,5},{8,10},{9,11},{10,... | collective-permute-start | bytes 786440 | tf_op jit(solution)/shard_map/ppermute | solution.py:34
  113.4 10.2 %collective-permute-start.21 = (bf16[128,1024]{1,0:T(8,128)(2,1)S(1)}, bf16[128,1024]{1,0:T(8,128)(2,1)S(1)}, u32[]{:S(2)}, u32[]{:S(2)}) collective-permute-start(bf16[128,1024]{1,0:T(8,128)(2,1)S(1)} %convolution_convert_fusion), channel_id=1, source_target_pairs={{0,6},{1,7},{2,4},{3,5},{4,2},{5,3},{6,0},{7,1},{8,14},{9,15},{10,... | collective-permute-start | bytes 786440 | tf_op jit(solution)/shard_map/ppermute | solution.py:34
  123.9 7.3 %collective-permute-start.24 = (bf16[32,1024]{1,0:T(8,128)(2,1)S(1)}, bf16[32,1024]{1,0:T(8,128)(2,1)S(1)}, u32[]{:S(2)}, u32[]{:S(2)}) collective-permute-start(bf16[32,1024]{1,0:T(8,128)(2,1)S(1)} %get-tuple-element.43), channel_id=1, source_target_pairs={{0,3},{1,2},{2,1},{3,0},{4,7},{5,6},{6,5},{7,4},{8,11},{9,10},{10,... | collective-permute-start | bytes 196616 | tf_op jit(solution)/shard_map/ppermute | solution.py:34
  128.6 4.3 %collective-permute-start.23 = (bf16[32,1024]{1,0:T(8,128)(2,1)S(1)}, bf16[32,1024]{1,0:T(8,128)(2,1)S(1)}, u32[]{:S(2)}, u32[]{:S(2)}) collective-permute-start(bf16[32,1024]{1,0:T(8,128)(2,1)S(1)} %get-tuple-element.44), channel_id=1, source_target_pairs={{0,2},{1,3},{2,0},{3,1},{4,6},{5,7},{6,4},{7,5},{8,10},{9,11},{10,... | collective-permute-start | bytes 196616 | tf_op jit(solution)/shard_map/ppermute | solution.py:34
  128.6 4.3 %collective-permute-start.22 = (bf16[32,1024]{1,0:T(8,128)(2,1)S(1)}, bf16[32,1024]{1,0:T(8,128)(2,1)S(1)}, u32[]{:S(2)}, u32[]{:S(2)}) collective-permute-start(bf16[32,1024]{1,0:T(8,128)(2,1)S(1)} %get-tuple-element.45), channel_id=1, source_target_pairs={{0,1},{1,0},{2,3},{3,2},{4,5},{5,4},{6,7},{7,6},{8,9},{9,8},{10,11... | collective-permute-start | bytes 196616 | tf_op jit(solution)/shard_map/ppermute | solution.py:34

commit v4 on v3

--- a/solution.py
+++ b/solution.py
@@ -14,6 +14,9 @@
 MOST = 32
 NEAR = 4
 META = 128
+FRONT_CUTS = 2
+ATTN_CUTS = 2
+BACK_CUTS = 2
 
 norm_eps = 1e-05
 rope_base = 500000.0
@@ -62,7 +65,7 @@
     return jax.ShapeDtypeStruct(dims, dtype)
 
 
-def run(kernel, name, out_shape, specs, *args, scratch=(), limit=8):
+def run(kernel, name, out_shape, specs, *args, scratch=(), limit=4):
     outs = jax.tree.map(lambda _: VMEM, out_shape)
     return pl.pallas_call(
         kernel,
@@ -75,11 +78,13 @@
     )(*args)
 
 
-def load(weights, after, name):
+def load(weights, after, name, rows=None, zeros=(8, 128)):
     count = len(weights)
 
     def kernel(*refs):
         sources, targets, done, sems = refs[:count], refs[count + 1 : -2], refs[-2], refs[-1]
+        if rows:
+            sources = [source.at[pl.ds(*rows)] for source in sources]
         copies = [
             pltpu.make_async_copy(source, target, sems.at[i])
             for i, (source, target) in enumerate(zip(sources, targets))
@@ -94,11 +99,15 @@
         kernel,
         in_specs=[HBM] * count + [ANY],
         out_specs=[VMEM] * (count + 1),
-        out_shape=[pltpu.VMEM(w.shape, w.dtype) for w in weights] + [pltpu.VMEM((8, 128), i32)],
+        out_shape=[pltpu.VMEM((rows[1] if rows else w.shape[0], w.shape[1]), w.dtype) for w in weights] + [pltpu.VMEM(zeros, i32)],
         scratch_shapes=[pltpu.SemaphoreType.DMA((count,))],
         compiler_params=pltpu.CompilerParams(vmem_limit_bytes=MIB),
         name=name,
     )(*[pltpu.with_memory_space_constraint(w, pltpu.HBM) for w in weights], after)
+
+
+def in_vmem(value):
+    return pltpu.with_memory_space_constraint(value, pltpu.VMEM)
 
 
 def slots_of(flags):
@@ -110,24 +119,51 @@
     return jnp.where((place == slot) & (flag > 0.5), 1.0, 0.0)
 
 
-def pick_kernel(near, flags, tokens, *outs):
+def pick_kernel(near, flags_hbm, tokens_hbm, *refs):
+    outs, (flags, tokens, sems) = refs[:NEAR], refs[NEAR:]
+    copies = [
+        pltpu.make_async_copy(flags_hbm, flags, sems.at[0]),
+        pltpu.make_async_copy(tokens_hbm, tokens, sems.at[1]),
+    ]
+    for copy in copies:
+        copy.start()
+    copies[0].wait()
     hot = slots_of(flags[...])
     number = lax.broadcasted_iota(i32, hot.shape, 1).astype(f32) + 1.0
     index = jnp.sum(hot * number, axis=1, keepdims=True) - 1.0
     meta = jnp.broadcast_to(index, (MOST, META)).astype(bf16)
     hot = hot.astype(bf16)
+    copies[1].wait()
     for k in range(NEAR):
         width = outs[k].shape[1] - META
-        outs[k][:, :width] = dot(hot, tokens[:, span(near[0] ^ k, width)]).astype(bf16)
-        outs[k][:, width:] = meta
+        outs[k][:, META:] = dot(hot, tokens[:, span(near[0] ^ k, width)]).astype(bf16)
+        outs[k][:, :META] = meta
+
+
+def pack_kernel(done, *refs):
+    blocks, outs = refs[:NEAR], refs[NEAR:]
+    start = 0
+    for out in outs:
+        for k, block in enumerate(blocks):
+            out[k * MOST : (k + 1) * MOST] = block[:, start : start + out.shape[1]]
+        start += out.shape[1]
 
 
 def put_kernel(near, flags, scales, tokens, *refs):
-    blocks, out = refs[:NEAR], refs[NEAR]
+    blocks, (out, held, sems) = refs[:NEAR], refs[NEAR:]
     hot = (slots_of(flags[...]) * scales[...].astype(f32)).astype(bf16)
-    for k in range(NEAR):
-        cols = span(near[0] ^ k, blocks[k].shape[1])
-        out[:, cols] = (tokens[:, cols].astype(f32) + dot_tn(hot, blocks[k][...])).astype(bf16)
+    copies = []
+    for k, block in enumerate(blocks):
+        cols = span(near[0] ^ k, block.shape[1])
+        held[:, cols] = (tokens[:, cols].astype(f32) + dot_tn(hot, block[...])).astype(bf16)
+        copies.append(pltpu.make_async_copy(held.at[:, cols], out.at[:, cols], sems.at[k]))
+        copies[-1].start()
+    for copy in copies:
+        copy.wait()
+
+
+def part_cols(near, index, cuts, width):
+    return span((near[0] ^ index // cuts) * cuts + index % cuts, width)
 
 
 def normed(near, blocks, gain, out):
@@ -137,18 +173,19 @@
         value = block[...].astype(f32)
         total += jnp.sum(value * value, axis=1, keepdims=True)
     scale = lax.rsqrt(total * (1.0 / width) + norm_eps)
-    for k, block in enumerate(blocks):
-        cols = span(near[0] ^ k, block.shape[1])
+    for i, block in enumerate(blocks):
+        cols = part_cols(near, i, len(blocks) // NEAR, block.shape[1])
         out[:, cols] = (block[...].astype(f32) * scale * gain[:, cols]).astype(bf16)
 
 
-def kv_kernel(near, b0, b1, b2, b3, gain, key_weight, value_weight, place_k, place_v, done, rows, s0, s1, s2, s3):
-    normed(near, (b0, b1, b2, b3), gain, rows)
+def kv_kernel(near, gain, key_weight, value_weight, place_k, place_v, done, *refs):
+    blocks, (rows, *outs) = refs[: -1 - NEAR], refs[-1 - NEAR :]
+    normed(near, blocks, gain, rows)
     keys = dot(rows[...], key_weight[...]).astype(bf16)
     values = dot(rows[...], value_weight[...]).astype(bf16)
     sends = (dot_nt(place_k[...], keys) + dot_nt(place_v[...], values)).astype(bf16)
-    height = s0.shape[0]
-    for k, out in enumerate((s0, s1, s2, s3)):
+    height = outs[0].shape[0]
+    for k, out in enumerate(outs):
         out[...] = sends[k * height : (k + 1) * height]
 
 
@@ -156,7 +193,7 @@
     out[...] = dot(left[...], right[...]).astype(out.dtype)
 
 
-def attention_kernel(raw_q, raw_kv, order_k, order_v, cos_row, sin_row, cos_col, sin_col, out):
+def attention_kernel(raw_q, raw_kv, order_k, order_v, cos_row, sin_row, cos_col, sin_col, done_a, done_b, out):
     half = HEAD_SIZE // 2
     keys = dot(order_k[...], raw_kv[...])
     values = dot(order_v[...], raw_kv[...]).astype(bf16)
@@ -176,25 +213,71 @@
         out[:, cols] = dot_nt(probs, values).astype(bf16)
 
 
-def block_kernel(k, near, left, right, out):
-    out[...] = dot(left[...], right[:, span(near[0] ^ k, out.shape[1])]).astype(bf16)
-
-
-def hidden_kernel(near, b0, b1, b2, b3, gain, gate, up, out, rows):
-    normed(near, (b0, b1, b2, b3), gain, rows)
-    gate_proj = dot(rows[...], gate[...])
-    up_proj = dot(rows[...], up[...])
-    out[...] = (jax.nn.silu(gate_proj) * up_proj).astype(bf16)
-
-
-def column_blocks(near_arr, left, right, name):
-    count, quarter = left.shape[0], right.shape[1] // NEAR
-    outs = {}
+def block_kernel(cuts, cut, near, left, *refs):
+    rights, outs = refs[:-NEAR], refs[-NEAR:]
+    depth = rights[0].shape[0]
     for k in (3, 1, 2, 0):
-        outs[k] = run(
-            functools.partial(block_kernel, k), name, shape((count, quarter)), [SMEM, VMEM, VMEM], near_arr, left, right
-        )
-    return outs
+        cols = part_cols(near, k * cuts + cut, cuts, outs[k].shape[1])
+        total = 0.0
+        for i, right in enumerate(rights):
+            total += dot(left[:, i * depth : (i + 1) * depth], right[:, cols])
+        outs[k][...] = total.astype(bf16)
+
+
+def gained(near, blocks, gain, out, cuts, cut):
+    total = 0.0
+    for k, block in enumerate(blocks):
+        width = block.shape[1]
+        value = block[...].astype(f32)
+        total += jnp.sum(value * value, axis=1, keepdims=True)
+        out[:, k * width : (k + 1) * width] = (value * gain[:, part_cols(near, k * cuts + cut, cuts, width)]).astype(bf16)
+    return total
+
+
+def cut_dot(near, rows, weight, cuts, cut):
+    width = rows.shape[1] // NEAR
+    total = 0.0
+    for k in range(NEAR):
+        depth = part_cols(near, k * cuts + cut, cuts, width)
+        total += dot(rows[:, k * width : (k + 1) * width], weight[depth, :])
+    return total
+
+
+def hidden_part_kernel(cuts, cut, near, gain, gate, up, *refs):
+    blocks, (gate_sum, up_sum, square_sum, rows) = refs[:NEAR], refs[NEAR:]
+    total = gained(near, blocks, gain, rows, cuts, cut)
+    square_sum[...] = jnp.broadcast_to(total, square_sum.shape)
+    gate_sum[...] = cut_dot(near, rows, gate, cuts, cut)
+    up_sum[...] = cut_dot(near, rows, up, cuts, cut)
+
+
+def hidden_kernel(cuts, near, gain, gate, up, *refs):
+    blocks, sums, (out, rows) = refs[:NEAR], refs[NEAR:-2], refs[-2:]
+    total = gained(near, blocks, gain, rows, cuts, cuts - 1)
+    gate_sum = cut_dot(near, rows, gate, cuts, cuts - 1)
+    up_sum = cut_dot(near, rows, up, cuts, cuts - 1)
+    for gate_part, up_part, square_part in zip(sums[::3], sums[1::3], sums[2::3]):
+        gate_sum += gate_part[...]
+        up_sum += up_part[...]
+        total += square_part[:, :1]
+    scale = lax.rsqrt(total * (1.0 / gate.shape[0]) + norm_eps)
+    out[...] = (jax.nn.silu(gate_sum * scale) * (up_sum * scale)).astype(bf16)
+
+
+def column_blocks(near_arr, left, rights, cuts, cut, name):
+    dims = (left.shape[0], rights[0].shape[1] // NEAR // cuts)
+    kernel = functools.partial(block_kernel, cuts, cut)
+    return run(kernel, name, [shape(dims)] * NEAR, [SMEM, VMEM] + [VMEM] * len(rights), near_arr, left, *rights)
+
+
+def near_gather(parts):
+    got = [[part] + [swap(part, k) for k in (1, 2, 3)] for part in parts]
+    return [cut[k] for k in range(NEAR) for cut in got]
+
+
+def cut_cols(matrix, cuts):
+    width = matrix.shape[1] // cuts
+    return [matrix[:, i * width : (i + 1) * width] for i in range(cuts)]
 
 
 def near_scatter(blocks):
@@ -235,33 +318,57 @@
     near_arr = near.astype(i32).reshape(1)
     count = PICK_DEV * size
     quarter = width // NEAR
-    kernel_mib = 8 if count <= 128 else 24
+    kernel_mib = 6 if count <= 128 else 24
     flags_row = pick_flags.reshape(1, tok_local)
     attn_gain, ffn_gain = attn_gain.reshape(1, width), ffn_gain.reshape(1, width)
 
     parts = run(
-        pick_kernel, "pick", [shape((MOST, quarter + META))] * NEAR, [SMEM, VMEM, VMEM], near_arr, flags_row, tokens
+        pick_kernel,
+        "pick",
+        [shape((MOST, quarter + META))] * NEAR,
+        [SMEM, HBM, HBM],
+        near_arr,
+        pltpu.with_memory_space_constraint(flags_row, pltpu.HBM),
+        pltpu.with_memory_space_constraint(tokens, pltpu.HBM),
+        scratch=[
+            pltpu.VMEM((1, tok_local), i32),
+            pltpu.VMEM((tok_local, width), bf16),
+            pltpu.SemaphoreType.DMA((2,)),
+        ],
     )
     key_w, value_w, query_w, done = load((key_weight, value_matrix, query_weight), parts[0], "load_qkv")
 
-    near_rows = jnp.concatenate([parts[0]] + [swap(parts[k], k) for k in (1, 2, 3)], axis=0)
-    gate_w, done = load((gate_weight,), near_rows, "load_gate")
-    all_rows = jnp.concatenate([near_rows] + [swap(near_rows, far_mask(k)) for k in range(1, far_size)], axis=0)
+    cuts = FRONT_CUTS
+    wide = quarter // cuts
+    pieces = run(
+        pack_kernel,
+        "pack",
+        [shape((NEAR * MOST, wide + (0 if cut else META))) for cut in range(cuts)],
+        [ANY] + [VMEM] * NEAR,
+        done,
+        *([parts[0]] + [swap(parts[k], k) for k in (1, 2, 3)]),
+    )
+    gate_w, done = load((gate_weight,), pieces[0], "load_gate", zeros=(1, size * MOST))
+    all_rows = [
+        jnp.concatenate([piece] + [swap(piece, far_mask(k)) for k in range(1, far_size)], axis=0) for piece in pieces
+    ]
     slots = size * MOST
-    all_index = all_rows[:, quarter].astype(i32)
+    all_index = all_rows[0][:, 0].astype(i32)
     order = jnp.arange(slots, dtype=i32)
     far_of = far ^ (order // (NEAR * MOST))
     device_of = far_of * NEAR + (near ^ (order // MOST % NEAR) ^ (far_of & 1) * 2)
     taken = (all_index >= 0).astype(f32)
     earlier = (device_of[:, None] < device_of[None, :]).astype(f32)
-    rank_of = jnp.sum(earlier * taken[:, None], axis=0).astype(i32) + order % MOST + done[0, 0]
+    rank_of = jnp.sum(earlier * taken[:, None], axis=0).astype(i32) + order % MOST + done[0]
     pick_ids = jnp.arange(count, dtype=i32)
     select = (pick_ids[:, None] == rank_of[None, :]) & (all_index >= 0)[None, :]
     token_positions = jnp.sum(jnp.where(select, (device_of * tok_local + all_index)[None, :], 0), axis=1)
     select = select.astype(bf16)
-    rows_quarter = dot(select, all_rows[:, :quarter]).astype(bf16)
-    output_w, done = load((output_weight,), rows_quarter, "load_out")
-    row_blocks = [rows_quarter] + [swap(rows_quarter, k) for k in (1, 2, 3)]
+    all_rows[0] = all_rows[0][:, META:]
+    row_parts = [dot(select, piece).astype(bf16) for piece in all_rows]
+    output_w, up_w, done = load((output_weight, up_weight), row_parts[0], "load_out_up")
+    row_blocks = near_gather(row_parts)
+    rows_quarter = jnp.concatenate(row_parts, axis=1)
 
     half_dim = HEAD_SIZE // 2
     frequency = rope_base ** (-(jnp.arange(half_dim, dtype=f32) * 2.0) / HEAD_SIZE)
@@ -288,17 +395,19 @@
         kv_kernel,
         "keys_values",
         [shape((count, width))] + [shape((total_rows // NEAR, count))] * NEAR,
-        [SMEM] + [VMEM] * 9 + [ANY],
+        [SMEM] + [VMEM] * 5 + [ANY] + [VMEM] * len(row_blocks),
         near_arr,
-        *row_blocks,
         attn_gain,
         key_w,
         value_w,
         place_k,
         place_v,
         done,
+        *row_blocks,
         limit=kernel_mib,
     )
+    down_half = down_weight.shape[0] // 2
+    down_a, done_a = load((down_weight,), sends[0], "load_down", (0, down_half))
     got = [sends[0]] + [swap(sends[k], k) for k in (1, 2, 3)]
     raw_q = run(
         matmul_kernel, "query", shape((count, heads_here * HEAD_SIZE), f32), [VMEM, VMEM], rows_normed, query_w
@@ -307,6 +416,7 @@
     for k in range(far_size):
         piece = jnp.concatenate([g[k * block_rows : (k + 1) * block_rows] for g in got], axis=0)
         pieces.append(swap(piece, far_mask(k)) if k else piece)
+    down_b, done_b = load((down_weight,), pieces[0], "load_down", (down_half, down_half))
     raw_kv = jnp.concatenate(pieces, axis=0)
     from_far = far ^ (row_id // (block_rows * NEAR))
     origin = from_far * NEAR + (near ^ (row_id // block_rows % NEAR) ^ (from_far & 1) * 2)
@@ -317,7 +427,7 @@
         attention_kernel,
         "attention",
         shape((count, heads_here * HEAD_SIZE)),
-        [VMEM] * 8,
+        [VMEM] * 8 + [ANY] * 2,
         raw_q,
         raw_kv,
         order_k,
@@ -326,48 +436,56 @@
         sin_row,
         cosine.T,
         sine.T,
+        done_a,
+        done_b,
         limit=kernel_mib,
     )
 
-    out_blocks = column_blocks(near_arr, heads, output_w, "attn_out")
-    attn_near = near_scatter(out_blocks).astype(bf16)
-    down_w, done = load((down_weight,), attn_near, "load_down")
-    attn_quarter = far_sum(attn_near, far_size) + done[0, 0].astype(f32)
-    mixed_quarter = (rows_quarter.astype(f32) + attn_quarter).astype(bf16)
-    up_w, done = load((up_weight,), mixed_quarter, "load_up")
-    mixed_blocks = [mixed_quarter] + [swap(mixed_quarter, k) for k in (1, 2, 3)]
-    hidden = run(
-        hidden_kernel,
-        "hidden",
-        shape((count, gate_weight.shape[1])),
-        [SMEM] + [VMEM] * 7,
-        near_arr,
-        *mixed_blocks,
-        ffn_gain,
-        gate_w,
-        up_w,
-        scratch=[pltpu.VMEM((count, width), bf16)],
-        limit=kernel_mib,
-    )
-    ffn_part = near_scatter(column_blocks(near_arr, hidden, down_w, "ffn_out")).astype(bf16)
-
+    cuts = ATTN_CUTS
+    attn_near = [
+        near_scatter(column_blocks(near_arr, heads, (output_w,), cuts, cut, "attn_out")).astype(bf16) for cut in range(cuts)
+    ]
+    attn_parts = [far_sum(part, far_size) for part in attn_near]
+    mixed_parts = [
+        (rows.astype(f32) + part).astype(bf16) for rows, part in zip(cut_cols(rows_quarter, cuts), attn_parts)
+    ]
+    attn_quarter = jnp.concatenate(attn_parts, axis=1).astype(bf16)
+    units = gate_weight.shape[1]
+    sums = []
+    for cut, part in enumerate(mixed_parts):
+        blocks = near_gather([part])
+        last = cut == cuts - 1
+        common = dict(scratch=[pltpu.VMEM((count, width // cuts), bf16)], limit=kernel_mib)
+        operands = (near_arr, ffn_gain, in_vmem(gate_w), in_vmem(up_w), *blocks)
+        specs = [SMEM] + [VMEM] * (3 + NEAR)
+        if not last:
+            outs = [shape((count, units), f32)] * 2 + [shape((count, 128), f32)]
+            kernel = functools.partial(hidden_part_kernel, cuts, cut)
+            sums += run(kernel, "hidden_part", outs, specs, *operands, **common)
+    kernel = functools.partial(hidden_kernel, cuts)
+    hidden = run(kernel, "hidden", shape((count, units)), specs + [VMEM] * len(sums), *operands, *sums, **common)
+
+    cuts = BACK_CUTS
     spread = select.reshape(count, far_size, NEAR * MOST)
-    delta = dot_tn(spread[:, 0], ffn_part) + dot_tn(spread[:, 0], attn_quarter.astype(bf16))
-    for k in range(1, far_size):
-        delta = delta + swap(dot_tn(spread[:, k], ffn_part).astype(bf16), far_mask(k)).astype(f32)
-    delta = delta.astype(bf16).reshape(NEAR, MOST, quarter)
+    deltas = []
+    for cut, attn_part in enumerate(cut_cols(attn_quarter, cuts)):
+        blocks = column_blocks(near_arr, hidden, (in_vmem(down_a), in_vmem(down_b)), cuts, cut, "ffn_out")
+        ffn_part = near_scatter(blocks).astype(bf16)
+        delta = dot_tn(spread[:, 0], ffn_part) + dot_tn(spread[:, 0], attn_part)
+        for k in range(1, far_size):
+            delta = delta + swap(dot_tn(spread[:, k], ffn_part).astype(bf16), far_mask(k)).astype(f32)
+        deltas.append(delta.astype(bf16))
+    delta = jnp.concatenate(deltas, axis=1).reshape(NEAR, MOST, quarter)
     back = [delta[0]] + [swap(delta[k], k) for k in (1, 2, 3)]
-    return run(
+    return pl.pallas_call(
         put_kernel,
-        "put",
-        shape((tok_local, width)),
-        [SMEM] + [VMEM] * 7,
-        near_arr,
-        flags_row,
-        gate_scales.reshape(1, tok_local),
-        tokens,
-        *back,
-    )
+        in_specs=[SMEM] + [VMEM] * (3 + NEAR),
+        out_specs=HBM,
+        out_shape=shape((tok_local, width)),
+        scratch_shapes=[pltpu.VMEM((tok_local, width), bf16), pltpu.SemaphoreType.DMA((NEAR,))],
+        compiler_params=pltpu.CompilerParams(vmem_limit_bytes=4 * MIB),
+        name="put",
+    )(near_arr, flags_row, gate_scales.reshape(1, tok_local), tokens, *back)
 
 
 def solution(mesh):

time: 135 us -> 119 us (0.88)
  waiting for transfers between devices: 53.1 us -> 27.7 us
  starting transfers between devices: 40.7 us -> 55.3 us
  local copies, waits for them, and re-layouts: 3.12 us -> 0.11 us
  other arithmetic: 3.31 us -> 1.95 us
    ppermute x25 -> x40, waiting for transfers between devices: 53.1 us -> 27.7 us  [swap(): return lax.ppermute(value, 'ctx', [(i, i ^ mask) for i in range(size)])]
    ppermute x25 -> x40, starting transfers between devices: 40.7 us -> 55.3 us  [swap(): return lax.ppermute(value, 'ctx', [(i, i ^ mask) for i in range(size)])]
    unnamed x17 -> x11, local copies, waits for them, and re-layouts: 1.96 us -> 0.05 us
    pallas_call x0 -> x1, Pallas kernels: none -> 1.4 us  [body(): pl.pallas_call(put_kernel, in_specs=[SMEM] + [VMEM] * (3 + NEAR), out_spe...]
    pallas_call x14 -> x11, Pallas kernels: 13 us -> 11.6 us  [run(): pl.pallas_call(kernel, in_specs=specs, out_specs=outs, out_shape=out_shap...]
  transfers between devices with their start and end apart: 25 -> 40, of which waited for: 20 -> 26; matrix products, arithmetic and copies ran while one was open for 2% -> 3% of each run, Pallas kernels for 15% -> 19%
where the time goes in v4:
time: 119 us
  starting transfers between devices  55.3 us (46%)
  Pallas kernels  31.1 us (26%)
  waiting for transfers between devices  27.7 us (23%)
  other arithmetic  1.95 us (2%)
  matrix products  1.76 us (1%)
    ppermute x40, starting transfers between devices, swap(): return lax.ppermute(value, 'ctx', [(i, i ^ mask) for i in range(size)])  55.3 us
    ppermute x40, waiting for transfers between devices, swap(): return lax.ppermute(value, 'ctx', [(i, i ^ mask) for i in range(size)])  27.7 us
    pallas_call x5, Pallas kernels, load(): pl.pallas_call(kernel, in_specs=[HBM] * count + [ANY], out_specs=[VMEM] *...  18 us
    pallas_call x11, Pallas kernels, run(): pl.pallas_call(kernel, in_specs=specs, out_specs=outs, out_shape=out_shap...  11.6 us
  transfers between devices with their start and end apart: 40, of which 26 were waited for; matrix products, arithmetic and copies ran while one was open for 3% of the time, Pallas kernels for 19%

profile of v4, /device:TPU:0, one launch (start us, length us, event | category | flops | bytes accessed | tf_op | source)
XLA Modules:
  0.0 118.5 jit_solution(11170036764857301208)
XLA Ops:
  0.0 1.6 %pick.1 = (bf16[32,1152]{1,0:T(8,128)(2,1)S(1)}, bf16[32,1152]{1,0:T(8,128)(2,1)S(1)}, bf16[32,1152]{1,0:T(8,128)(2,1)S(1)}, bf16[32,1152]{1,0:T(8,128)(2,1)S(1)}) custom-call(s32[1]{0:T(128)} %bitcast.near, s32[1,128]{1,0:T(1,128)} %bitcast.26, bf16[128,4096]{1,0:T(8,128)(2,1)} %tokens.1), custom_call_target="tpu_custom_call" | custom-call | tf_op jit(solution)/shard_map/pick/pallas_call | solution.py:70
  1.6 3.0 %collective-permute-start = (bf16[32,1152]{1,0:T(8,128)(2,1)S(1)}, bf16[32,1152]{1,0:T(8,128)(2,1)S(1)}, u32[]{:S(2)}, u32[]{:S(2)}) collective-permute-start(bf16[32,1152]{1,0:T(8,128)(2,1)S(1)} %get-tuple-element.50), channel_id=1, source_target_pairs={{0,1},{1,0},{2,3},{3,2},{4,5},{5,4},{6,7},{7,6},{8,9},{9,8},{10,11... | collective-permute-start | bytes 221192 | tf_op jit(solution)/shard_map/ppermute | solution.py:37
  4.6 1.6 %collective-permute-start.1 = (bf16[32,1152]{1,0:T(8,128)(2,1)S(1)}, bf16[32,1152]{1,0:T(8,128)(2,1)S(1)}, u32[]{:S(2)}, u32[]{:S(2)}) collective-permute-start(bf16[32,1152]{1,0:T(8,128)(2,1)S(1)} %get-tuple-element.51), channel_id=1, source_target_pairs={{0,2},{1,3},{2,0},{3,1},{4,6},{5,7},{6,4},{7,5},{8,10},{9,11},{10,... | collective-permute-start | bytes 221192 | tf_op jit(solution)/shard_map/ppermute | solution.py:37
  6.4 2.9 %load_qkv.1 = (bf16[4096,128]{1,0:T(8,128)(2,1)S(1)}, bf16[4096,128]{1,0:T(8,128)(2,1)S(1)}, bf16[4096,512]{1,0:T(8,128)(2,1)S(1)}, s32[8,128]{1,0:T(8,128)S(1)}) custom-call(bf16[4096,128]{1,0:T(8,128)(2,1)} %refs_0_.5, bf16[4096,128]{1,0:T(8,128)(2,1)} %refs_1_.2, bf16[4096,512]{1,0:T(8,128)(2,1)} %refs_2_.1, ...), custom_call_target="tpu_custom_call" | custom-call | tf_op jit(solution)/shard_map/load_qkv/pallas_call | solution.py:98
  9.6 1.9 %collective-permute-done.2.refs_3_ = bf16[32,1152]{1,0:T(8,128)(2,1)S(1)} collective-permute-done((bf16[32,1152]{1,0:T(8,128)(2,1)S(1)}, bf16[32,1152]{1,0:T(8,128)(2,1)S(1)}, u32[]{:S(2)}, u32[]{:S(2)}) %collective-permute-start.2) | collective-permute-done | bytes 73760 | tf_op jit(solution)/shard_map/ppermute | solution.py:37
  11.4 2.5 %collective-permute-start.3 = (bf16[128,640]{1,0:T(8,128)(2,1)S(1)}, bf16[128,640]{1,0:T(8,128)(2,1)S(1)}, u32[]{:S(2)}, u32[]{:S(2)}) collective-permute-start(bf16[128,640]{1,0:T(8,128)(2,1)S(1)} %get-tuple-element.53.refs_1_), channel_id=1, source_target_pairs={{0,6},{1,7},{2,4},{3,5},{4,2},{5,3},{6,0},{7,1},{8,14},{9,15},{10,... | collective-permute-start | bytes 491528 | tf_op jit(solution)/shard_map/ppermute | solution.py:37
  14.0 1.4 %collective-permute-start.4 = (bf16[128,512]{1,0:T(8,128)(2,1)S(1)}, bf16[128,512]{1,0:T(8,128)(2,1)S(1)}, u32[]{:S(2)}, u32[]{:S(2)}) collective-permute-start(bf16[128,512]{1,0:T(8,128)(2,1)S(1)} %get-tuple-element.57), channel_id=1, source_target_pairs={{0,6},{1,7},{2,4},{3,5},{4,2},{5,3},{6,0},{7,1},{8,14},{9,15},{10,... | collective-permute-start | bytes 393224 | tf_op jit(solution)/shard_map/ppermute | solution.py:37
  15.4 4.3 %load_gate.1 = (bf16[4096,1408]{1,0:T(8,128)(2,1)S(1)}, s32[1,256]{1,0:T(1,128)S(1)}) custom-call(bf16[4096,1408]{1,0:T(8,128)(2,1)} %refs_0_.6, bf16[128,640]{1,0:T(8,128)(2,1)S(1)} %get-tuple-element.53.refs_1_), custom_call_target="tpu_custom_call" | custom-call | tf_op jit(solution)/shard_map/load_gate/pallas_call | solution.py:98
  21.6 5.5 %collective-permute-start.10 = (bf16[128,512]{1,0:T(8,128)(2,1)S(1)}, bf16[128,512]{1,0:T(8,128)(2,1)S(1)}, u32[]{:S(2)}, u32[]{:S(2)}) collective-permute-start(bf16[128,512]{1,0:T(8,128)(2,1)S(1)} %convolution_convert_fusion.2.refs_1_), channel_id=1, source_target_pairs={{0,3},{1,2},{2,1},{3,0},{4,7},{5,6},{6,5},{7,4},{8,11},{9,10},{10,... | collective-permute-start | bytes 393224 | tf_op jit(solution)/shard_map/ppermute | solution.py:37
  28.0 2.6 %collective-permute-start.9 = (bf16[128,512]{1,0:T(8,128)(2,1)S(1)}, bf16[128,512]{1,0:T(8,128)(2,1)S(1)}, u32[]{:S(2)}, u32[]{:S(2)}) collective-permute-start(bf16[128,512]{1,0:T(8,128)(2,1)S(1)} %convolution_convert_fusion.3.refs_2_.refs_0_), channel_id=1, source_target_pairs={{0,3},{1,2},{2,1},{3,0},{4,7},{5,6},{6,5},{7,4},{8,11},{9,10},{10,... | collective-permute-start | bytes 393224 | tf_op jit(solution)/shard_map/ppermute | solution.py:37
  32.3 5.6 %load_out_up.1 = (bf16[512,4096]{1,0:T(8,128)(2,1)S(1)}, bf16[4096,1408]{1,0:T(8,128)(2,1)S(1)}, s32[8,128]{1,0:T(8,128)S(1)}) custom-call(bf16[512,4096]{1,0:T(8,128)(2,1)} %refs_0_.7, bf16[4096,1408]{1,0:T(8,128)(2,1)} %refs_1_.3, bf16[128,512]{1,0:T(8,128)(2,1)S(1)} %convolution_convert_fusion.3.refs_2_.refs_0_), custom_call_target="tpu_custom_call" | custom-call | tf_op jit(solution)/shard_map/load_out_up/pallas_call | solution.py:98
  38.3 1.5 %keys_values.1 = (bf16[128,4096]{1,0:T(8,128)(2,1)S(1)}, bf16[64,128]{1,0:T(8,128)(2,1)S(1)}, bf16[64,128]{1,0:T(8,128)(2,1)S(1)}, bf16[64,128]{1,0:T(8,128)(2,1)S(1)}, bf16[64,128]{1,0:T(8,128)(2,1)S(1)}) custom-call(s32[1]{0:T(128)} %bitcast.near, f32[1,4096]{1,0:T(1,128)S(1)} %bitcast.25, bf16[4096,128]{1,0:T(8,128)(2,1)S(1)} %get-tuple-element.58.key_weight, ...), custom_call_target="tpu_custom_call" | custom-call | tf_op jit(solution)/shard_map/keys_values/pallas_call | solution.py:70
  40.9 2.6 %collective-permute-start.12 = (bf16[64,128]{1,0:T(8,128)(2,1)S(1)}, bf16[64,128]{1,0:T(8,128)(2,1)S(1)}, u32[]{:S(2)}, u32[]{:S(2)}) collective-permute-start(bf16[64,128]{1,0:T(8,128)(2,1)S(1)} %get-tuple-element.65), channel_id=1, source_target_pairs={{0,2},{1,3},{2,0},{3,1},{4,6},{5,7},{6,4},{7,5},{8,10},{9,11},{10,... | collective-permute-start | bytes 49160 | tf_op jit(solution)/shard_map/ppermute | solution.py:37
  44.1 2.6 %load_down.2 = (bf16[704,4096]{1,0:T(8,128)(2,1)S(1)}, s32[8,128]{1,0:T(8,128)S(1)}) custom-call(bf16[1408,4096]{1,0:T(8,128)(2,1)} %refs_0_.9, bf16[64,128]{1,0:T(8,128)(2,1)S(1)} %get-tuple-element.63.refs_1_), custom_call_target="tpu_custom_call" | custom-call | tf_op jit(solution)/shard_map/load_down/pallas_call | solution.py:98
  48.1 2.7 %collective-permute-start.14 = (bf16[128,128]{1,0:T(8,128)(2,1)S(1)}, bf16[128,128]{1,0:T(8,128)(2,1)S(1)}, u32[]{:S(2)}, u32[]{:S(2)}) collective-permute-start(bf16[128,128]{1,0:T(8,128)(2,1)S(1)} %pad_maximum_fusion.3), channel_id=1, source_target_pairs={{0,6},{1,7},{2,4},{3,5},{4,2},{5,3},{6,0},{7,1},{8,14},{9,15},{10,... | collective-permute-start | bytes 98312 | tf_op jit(solution)/shard_map/ppermute | solution.py:37
  50.8 2.6 %load_down.3 = (bf16[704,4096]{1,0:T(8,128)(2,1)S(1)}, s32[8,128]{1,0:T(8,128)S(1)}) custom-call(bf16[1408,4096]{1,0:T(8,128)(2,1)} %refs_0_.9, bf16[128,128]{1,0:T(8,128)(2,1)S(1)} %pad_maximum_fusion.4.refs_1_), custom_call_target="tpu_custom_call" | custom-call | tf_op jit(solution)/shard_map/load_down/pallas_call | solution.py:98
  57.0 1.9 %collective-permute-start.24 = (bf16[128,512]{1,0:T(8,128)(2,1)S(1)}, bf16[128,512]{1,0:T(8,128)(2,1)S(1)}, u32[]{:S(2)}, u32[]{:S(2)}) collective-permute-start(bf16[128,512]{1,0:T(8,128)(2,1)S(1)} %get-tuple-element.77), channel_id=1, source_target_pairs={{0,2},{1,3},{2,0},{3,1},{4,6},{5,7},{6,4},{7,5},{8,10},{9,11},{10,... | collective-permute-start | bytes 393224 | tf_op jit(solution)/shard_map/ppermute | solution.py:37
  64.4 2.4 %collective-permute-start.25 = (bf16[128,512]{1,0:T(8,128)(2,1)S(1)}, bf16[128,512]{1,0:T(8,128)(2,1)S(1)}, u32[]{:S(2)}, u32[]{:S(2)}) collective-permute-start(bf16[128,512]{1,0:T(8,128)(2,1)S(1)} %add_convert_fusion.3), channel_id=1, source_target_pairs={{0,6},{1,7},{2,4},{3,5},{4,2},{5,3},{6,0},{7,1},{8,14},{9,15},{10,... | collective-permute-start | bytes 393224 | tf_op jit(solution)/shard_map/ppermute | solution.py:37
  68.0 4.0 %collective-permute-start.18 = (bf16[128,512]{1,0:T(8,128)(2,1)S(1)}, bf16[128,512]{1,0:T(8,128)(2,1)S(1)}, u32[]{:S(2)}, u32[]{:S(2)}) collective-permute-start(bf16[128,512]{1,0:T(8,128)(2,1)S(1)} %add_convert_fusion.5), channel_id=1, source_target_pairs={{0,6},{1,7},{2,4},{3,5},{4,2},{5,3},{6,0},{7,1},{8,14},{9,15},{10,... | collective-permute-start | bytes 393224 | tf_op jit(solution)/shard_map/ppermute | solution.py:37
  73.3 2.5 %collective-permute-start.27 = (bf16[128,512]{1,0:T(8,128)(2,1)S(1)}, bf16[128,512]{1,0:T(8,128)(2,1)S(1)}, u32[]{:S(2)}, u32[]{:S(2)}) collective-permute-start(bf16[128,512]{1,0:T(8,128)(2,1)S(1)} %add_convert_fusion.2.refs_0_), channel_id=1, source_target_pairs={{0,2},{1,3},{2,0},{3,1},{4,6},{5,7},{6,4},{7,5},{8,10},{9,11},{10,... | collective-permute-start | bytes 393224 | tf_op jit(solution)/shard_map/ppermute | solution.py:37
  77.3 2.0 %collective-permute-start.20 = (bf16[128,512]{1,0:T(8,128)(2,1)S(1)}, bf16[128,512]{1,0:T(8,128)(2,1)S(1)}, u32[]{:S(2)}, u32[]{:S(2)}) collective-permute-start(bf16[128,512]{1,0:T(8,128)(2,1)S(1)} %add_convert_fusion.4.refs_0_), channel_id=1, source_target_pairs={{0,2},{1,3},{2,0},{3,1},{4,6},{5,7},{6,4},{7,5},{8,10},{9,11},{10,... | collective-permute-start | bytes 393224 | tf_op jit(solution)/shard_map/ppermute | solution.py:37
  80.7 1.9 %hidden_part.1 = (f32[128,1408]{1,0:T(8,128)S(1)}, f32[128,1408]{1,0:T(8,128)S(1)}, f32[128,128]{1,0:T(8,128)S(1)}) custom-call(s32[1]{0:T(128)} %bitcast.near, f32[1,4096]{1,0:T(1,128)S(1)} %bitcast.23, bf16[4096,1408]{1,0:T(8,128)(2,1)S(1)} %get-tuple-element.55.gate, bf16[4096,1408]{1,0:T(8,128)(2,1)S(1)} %get-tuple-element.56.up, ...), custom_call_target="tpu_custom_call" | custom-call | tf_op jit(solution)/shard_map/hidden_part/pallas_call | solution.py:70
  84.1 2.8 %collective-permute-done.19.refs_1_ = bf16[128,512]{1,0:T(8,128)(2,1)S(1)} collective-permute-done((bf16[128,512]{1,0:T(8,128)(2,1)S(1)}, bf16[128,512]{1,0:T(8,128)(2,1)S(1)}, u32[]{:S(2)}, u32[]{:S(2)}) %collective-permute-start.19) | collective-permute-done | bytes 131104 | tf_op jit(solution)/shard_map/ppermute | solution.py:37
  86.9 2.0 %hidden.1.left = bf16[128,1408]{1,0:T(8,128)(2,1)S(1)} custom-call(s32[1]{0:T(128)} %bitcast.near, f32[1,4096]{1,0:T(1,128)S(1)} %bitcast.24, bf16[4096,1408]{1,0:T(8,128)(2,1)S(1)} %get-tuple-element.55.gate, bf16[4096,1408]{1,0:T(8,128)(2,1)S(1)} %get-tuple-element.56.up, bf16[128,512]{1,0:T(8,128)(2,1)S(1)} %add_convert_fusion.4.refs_0_, ...), custom_call_target="tpu_custom_call" | custom-call | tf_op jit(solution)/shard_map/hidden/pallas_call | solution.py:70
  91.4 2.1 %collective-permute-start.35 = (bf16[128,512]{1,0:T(8,128)(2,1)S(1)}, bf16[128,512]{1,0:T(8,128)(2,1)S(1)}, u32[]{:S(2)}, u32[]{:S(2)}) collective-permute-start(bf16[128,512]{1,0:T(8,128)(2,1)S(1)} %get-tuple-element.90), channel_id=1, source_target_pairs={{0,2},{1,3},{2,0},{3,1},{4,6},{5,7},{6,4},{7,5},{8,10},{9,11},{10,... | collective-permute-start | bytes 393224 | tf_op jit(solution)/shard_map/ppermute | solution.py:37
  96.3 1.6 %collective-permute-done.33 = bf16[128,512]{1,0:T(8,128)(2,1)S(1)} collective-permute-done((bf16[128,512]{1,0:T(8,128)(2,1)S(1)}, bf16[128,512]{1,0:T(8,128)(2,1)S(1)}, u32[]{:S(2)}, u32[]{:S(2)}) %collective-permute-start.33) | collective-permute-done | bytes 131104 | tf_op jit(solution)/shard_map/ppermute | solution.py:37
  101.1 1.6 %collective-permute-done.30 = bf16[128,512]{1,0:T(8,128)(2,1)S(1)} collective-permute-done((bf16[128,512]{1,0:T(8,128)(2,1)S(1)}, bf16[128,512]{1,0:T(8,128)(2,1)S(1)}, u32[]{:S(2)}, u32[]{:S(2)}) %collective-permute-start.30) | collective-permute-done | bytes 131104 | tf_op jit(solution)/shard_map/ppermute | solution.py:37
  104.4 2.6 %collective-permute-done.36 = bf16[128,512]{1,0:T(8,128)(2,1)S(1)} collective-permute-done((bf16[128,512]{1,0:T(8,128)(2,1)S(1)}, bf16[128,512]{1,0:T(8,128)(2,1)S(1)}, u32[]{:S(2)}, u32[]{:S(2)}) %collective-permute-start.36) | collective-permute-done | bytes 131104 | tf_op jit(solution)/shard_map/ppermute | solution.py:37
  107.2 3.7 %collective-permute-done.32 = bf16[128,512]{1,0:T(8,128)(2,1)S(1)} collective-permute-done((bf16[128,512]{1,0:T(8,128)(2,1)S(1)}, bf16[128,512]{1,0:T(8,128)(2,1)S(1)}, u32[]{:S(2)}, u32[]{:S(2)}) %collective-permute-start.32) | collective-permute-done | bytes 131104 | tf_op jit(solution)/shard_map/ppermute | solution.py:37
  112.3 2.5 %collective-permute-start.38 = (bf16[32,1024]{1,0:T(8,128)(2,1)S(1)}, bf16[32,1024]{1,0:T(8,128)(2,1)S(1)}, u32[]{:S(2)}, u32[]{:S(2)}) collective-permute-start(bf16[32,1024]{1,0:T(8,128)(2,1)S(1)} %get-tuple-element.94), channel_id=1, source_target_pairs={{0,2},{1,3},{2,0},{3,1},{4,6},{5,7},{6,4},{7,5},{8,10},{9,11},{10,... | collective-permute-start | bytes 196616 | tf_op jit(solution)/shard_map/ppermute | solution.py:37
  114.7 1.7 %collective-permute-done.39.refs_3_ = bf16[32,1024]{1,0:T(8,128)(2,1)S(1)} collective-permute-done((bf16[32,1024]{1,0:T(8,128)(2,1)S(1)}, bf16[32,1024]{1,0:T(8,128)(2,1)S(1)}, u32[]{:S(2)}, u32[]{:S(2)}) %collective-permute-start.39) | collective-permute-done | bytes 65568 | tf_op jit(solution)/shard_map/ppermute | solution.py:37
  117.0 1.4 %put.1 = bf16[128,4096]{1,0:T(8,128)(2,1)} custom-call(s32[1]{0:T(128)} %bitcast.near, s32[1,128]{1,0:T(1,128)S(1)} %bitcast.27, bf16[1,128]{1,0:T(2,128)(2,1)S(1)} %bitcast.28, bf16[128,4096]{1,0:T(8,128)(2,1)S(1)} %copy-done, bf16[32,1024]{1,0:T(8,128)(2,1)S(1)} %get-tuple-element.92.refs_0_, bf16[32,1024]{1,0:T(8,128)(2,1)S(1)} %collective-permute-done.37.refs_1_, ...), custom_call_target="tpu_custom_call" | custom-call | tf_op jit(solution)/shard_map/put/pallas_call | solution.py:480
  (119 shorter events, 36.4 us)
Async XLA Ops:
  1.6 7.8 %collective-permute-start = (bf16[32,1152]{1,0:T(8,128)(2,1)S(1)}, bf16[32,1152]{1,0:T(8,128)(2,1)S(1)}, u32[]{:S(2)}, u32[]{:S(2)}) collective-permute-start(bf16[32,1152]{1,0:T(8,128)(2,1)S(1)} %get-tuple-element.50), channel_id=1, source_target_pairs={{0,1},{1,0},{2,3},{3,2},{4,5},{5,4},{6,7},{7,6},{8,9},{9,8},{10,11... | collective-permute-start | bytes 221192 | tf_op jit(solution)/shard_map/ppermute | solution.py:37
  11.4 8.6 %collective-permute-start.3 = (bf16[128,640]{1,0:T(8,128)(2,1)S(1)}, bf16[128,640]{1,0:T(8,128)(2,1)S(1)}, u32[]{:S(2)}, u32[]{:S(2)}) collective-permute-start(bf16[128,640]{1,0:T(8,128)(2,1)S(1)} %get-tuple-element.53.refs_1_), channel_id=1, source_target_pairs={{0,6},{1,7},{2,4},{3,5},{4,2},{5,3},{6,0},{7,1},{8,14},{9,15},{10,... | collective-permute-start | bytes 491528 | tf_op jit(solution)/shard_map/ppermute | solution.py:37
  14.0 7.4 %collective-permute-start.4 = (bf16[128,512]{1,0:T(8,128)(2,1)S(1)}, bf16[128,512]{1,0:T(8,128)(2,1)S(1)}, u32[]{:S(2)}, u32[]{:S(2)}) collective-permute-start(bf16[128,512]{1,0:T(8,128)(2,1)S(1)} %get-tuple-element.57), channel_id=1, source_target_pairs={{0,6},{1,7},{2,4},{3,5},{4,2},{5,3},{6,0},{7,1},{8,14},{9,15},{10,... | collective-permute-start | bytes 393224 | tf_op jit(solution)/shard_map/ppermute | solution.py:37
  21.6 9.7 %collective-permute-start.10 = (bf16[128,512]{1,0:T(8,128)(2,1)S(1)}, bf16[128,512]{1,0:T(8,128)(2,1)S(1)}, u32[]{:S(2)}, u32[]{:S(2)}) collective-permute-start(bf16[128,512]{1,0:T(8,128)(2,1)S(1)} %convolution_convert_fusion.2.refs_1_), channel_id=1, source_target_pairs={{0,3},{1,2},{2,1},{3,0},{4,7},{5,6},{6,5},{7,4},{8,11},{9,10},{10,... | collective-permute-start | bytes 393224 | tf_op jit(solution)/shard_map/ppermute | solution.py:37
  27.1 10.9 %collective-permute-start.8 = (bf16[128,512]{1,0:T(8,128)(2,1)S(1)}, bf16[128,512]{1,0:T(8,128)(2,1)S(1)}, u32[]{:S(2)}, u32[]{:S(2)}) collective-permute-start(bf16[128,512]{1,0:T(8,128)(2,1)S(1)} %convolution_convert_fusion.2.refs_1_), channel_id=1, source_target_pairs={{0,2},{1,3},{2,0},{3,1},{4,6},{5,7},{6,4},{7,5},{8,10},{9,11},{10,... | collective-permute-start | bytes 393224 | tf_op jit(solution)/shard_map/ppermute | solution.py:37
  27.1 11.0 %collective-permute-start.6 = (bf16[128,512]{1,0:T(8,128)(2,1)S(1)}, bf16[128,512]{1,0:T(8,128)(2,1)S(1)}, u32[]{:S(2)}, u32[]{:S(2)}) collective-permute-start(bf16[128,512]{1,0:T(8,128)(2,1)S(1)} %convolution_convert_fusion.2.refs_1_), channel_id=1, source_target_pairs={{0,1},{1,0},{2,3},{3,2},{4,5},{5,4},{6,7},{7,6},{8,9},{9,8},{10,11... | collective-permute-start | bytes 393224 | tf_op jit(solution)/shard_map/ppermute | solution.py:37
  28.0 10.1 %collective-permute-start.9 = (bf16[128,512]{1,0:T(8,128)(2,1)S(1)}, bf16[128,512]{1,0:T(8,128)(2,1)S(1)}, u32[]{:S(2)}, u32[]{:S(2)}) collective-permute-start(bf16[128,512]{1,0:T(8,128)(2,1)S(1)} %convolution_convert_fusion.3.refs_2_.refs_0_), channel_id=1, source_target_pairs={{0,3},{1,2},{2,1},{3,0},{4,7},{5,6},{6,5},{7,4},{8,11},{9,10},{10,... | collective-permute-start | bytes 393224 | tf_op jit(solution)/shard_map/ppermute | solution.py:37
  30.6 7.5 %collective-permute-start.7 = (bf16[128,512]{1,0:T(8,128)(2,1)S(1)}, bf16[128,512]{1,0:T(8,128)(2,1)S(1)}, u32[]{:S(2)}, u32[]{:S(2)}) collective-permute-start(bf16[128,512]{1,0:T(8,128)(2,1)S(1)} %convolution_convert_fusion.3.refs_2_.refs_0_), channel_id=1, source_target_pairs={{0,2},{1,3},{2,0},{3,1},{4,6},{5,7},{6,4},{7,5},{8,10},{9,11},{10,... | collective-permute-start | bytes 393224 | tf_op jit(solution)/shard_map/ppermute | solution.py:37
  31.3 6.9 %collective-permute-start.5 = (bf16[128,512]{1,0:T(8,128)(2,1)S(1)}, bf16[128,512]{1,0:T(8,128)(2,1)S(1)}, u32[]{:S(2)}, u32[]{:S(2)}) collective-permute-start(bf16[128,512]{1,0:T(8,128)(2,1)S(1)} %convolution_convert_fusion.3.refs_2_.refs_0_), channel_id=1, source_target_pairs={{0,1},{1,0},{2,3},{3,2},{4,5},{5,4},{6,7},{7,6},{8,9},{9,8},{10,11... | collective-permute-start | bytes 393224 | tf_op jit(solution)/shard_map/ppermute | solution.py:37
  39.8 7.6 %collective-permute-start.11 = (bf16[64,128]{1,0:T(8,128)(2,1)S(1)}, bf16[64,128]{1,0:T(8,128)(2,1)S(1)}, u32[]{:S(2)}, u32[]{:S(2)}) collective-permute-start(bf16[64,128]{1,0:T(8,128)(2,1)S(1)} %get-tuple-element.64), channel_id=1, source_target_pairs={{0,1},{1,0},{2,3},{3,2},{4,5},{5,4},{6,7},{7,6},{8,9},{9,8},{10,11... | collective-permute-start | bytes 49160 | tf_op jit(solution)/shard_map/ppermute | solution.py:37
  40.9 6.6 %collective-permute-start.12 = (bf16[64,128]{1,0:T(8,128)(2,1)S(1)}, bf16[64,128]{1,0:T(8,128)(2,1)S(1)}, u32[]{:S(2)}, u32[]{:S(2)}) collective-permute-start(bf16[64,128]{1,0:T(8,128)(2,1)S(1)} %get-tuple-element.65), channel_id=1, source_target_pairs={{0,2},{1,3},{2,0},{3,1},{4,6},{5,7},{6,4},{7,5},{8,10},{9,11},{10,... | collective-permute-start | bytes 49160 | tf_op jit(solution)/shard_map/ppermute | solution.py:37
  48.1 5.8 %collective-permute-start.14 = (bf16[128,128]{1,0:T(8,128)(2,1)S(1)}, bf16[128,128]{1,0:T(8,128)(2,1)S(1)}, u32[]{:S(2)}, u32[]{:S(2)}) collective-permute-start(bf16[128,128]{1,0:T(8,128)(2,1)S(1)} %pad_maximum_fusion.3), channel_id=1, source_target_pairs={{0,6},{1,7},{2,4},{3,5},{4,2},{5,3},{6,0},{7,1},{8,14},{9,15},{10,... | collective-permute-start | bytes 98312 | tf_op jit(solution)/shard_map/ppermute | solution.py:37
  55.4 7.0 %collective-permute-start.22 = (bf16[128,512]{1,0:T(8,128)(2,1)S(1)}, bf16[128,512]{1,0:T(8,128)(2,1)S(1)}, u32[]{:S(2)}, u32[]{:S(2)}) collective-permute-start(bf16[128,512]{1,0:T(8,128)(2,1)S(1)} %get-tuple-element.75), channel_id=1, source_target_pairs={{0,3},{1,2},{2,1},{3,0},{4,7},{5,6},{6,5},{7,4},{8,11},{9,10},{10,... | collective-permute-start | bytes 393224 | tf_op jit(solution)/shard_map/ppermute | solution.py:37
  55.9 7.3 %collective-permute-start.23 = (bf16[128,512]{1,0:T(8,128)(2,1)S(1)}, bf16[128,512]{1,0:T(8,128)(2,1)S(1)}, u32[]{:S(2)}, u32[]{:S(2)}) collective-permute-start(bf16[128,512]{1,0:T(8,128)(2,1)S(1)} %get-tuple-element.76), channel_id=1, source_target_pairs={{0,1},{1,0},{2,3},{3,2},{4,5},{5,4},{6,7},{7,6},{8,9},{9,8},{10,11... | collective-permute-start | bytes 393224 | tf_op jit(solution)/shard_map/ppermute | solution.py:37
  57.0 7.4 %collective-permute-start.24 = (bf16[128,512]{1,0:T(8,128)(2,1)S(1)}, bf16[128,512]{1,0:T(8,128)(2,1)S(1)}, u32[]{:S(2)}, u32[]{:S(2)}) collective-permute-start(bf16[128,512]{1,0:T(8,128)(2,1)S(1)} %get-tuple-element.77), channel_id=1, source_target_pairs={{0,2},{1,3},{2,0},{3,1},{4,6},{5,7},{6,4},{7,5},{8,10},{9,11},{10,... | collective-permute-start | bytes 393224 | tf_op jit(solution)/shard_map/ppermute | solution.py:37
  59.4 7.5 %collective-permute-start.15 = (bf16[128,512]{1,0:T(8,128)(2,1)S(1)}, bf16[128,512]{1,0:T(8,128)(2,1)S(1)}, u32[]{:S(2)}, u32[]{:S(2)}) collective-permute-start(bf16[128,512]{1,0:T(8,128)(2,1)S(1)} %get-tuple-element.71), channel_id=1, source_target_pairs={{0,3},{1,2},{2,1},{3,0},{4,7},{5,6},{6,5},{7,4},{8,11},{9,10},{10,... | collective-permute-start | bytes 393224 | tf_op jit(solution)/shard_map/ppermute | solution.py:37
  60.1 6.8 %collective-permute-start.16 = (bf16[128,512]{1,0:T(8,128)(2,1)S(1)}, bf16[128,512]{1,0:T(8,128)(2,1)S(1)}, u32[]{:S(2)}, u32[]{:S(2)}) collective-permute-start(bf16[128,512]{1,0:T(8,128)(2,1)S(1)} %get-tuple-element.72), channel_id=1, source_target_pairs={{0,1},{1,0},{2,3},{3,2},{4,5},{5,4},{6,7},{7,6},{8,9},{9,8},{10,11... | collective-permute-start | bytes 393224 | tf_op jit(solution)/shard_map/ppermute | solution.py:37
  64.4 8.7 %collective-permute-start.25 = (bf16[128,512]{1,0:T(8,128)(2,1)S(1)}, bf16[128,512]{1,0:T(8,128)(2,1)S(1)}, u32[]{:S(2)}, u32[]{:S(2)}) collective-permute-start(bf16[128,512]{1,0:T(8,128)(2,1)S(1)} %add_convert_fusion.3), channel_id=1, source_target_pairs={{0,6},{1,7},{2,4},{3,5},{4,2},{5,3},{6,0},{7,1},{8,14},{9,15},{10,... | collective-permute-start | bytes 393224 | tf_op jit(solution)/shard_map/ppermute | solution.py:37
  68.0 8.7 %collective-permute-start.18 = (bf16[128,512]{1,0:T(8,128)(2,1)S(1)}, bf16[128,512]{1,0:T(8,128)(2,1)S(1)}, u32[]{:S(2)}, u32[]{:S(2)}) collective-permute-start(bf16[128,512]{1,0:T(8,128)(2,1)S(1)} %add_convert_fusion.5), channel_id=1, source_target_pairs={{0,6},{1,7},{2,4},{3,5},{4,2},{5,3},{6,0},{7,1},{8,14},{9,15},{10,... | collective-permute-start | bytes 393224 | tf_op jit(solution)/shard_map/ppermute | solution.py:37
  73.2 6.2 %collective-permute-start.28 = (bf16[128,512]{1,0:T(8,128)(2,1)S(1)}, bf16[128,512]{1,0:T(8,128)(2,1)S(1)}, u32[]{:S(2)}, u32[]{:S(2)}) collective-permute-start(bf16[128,512]{1,0:T(8,128)(2,1)S(1)} %add_convert_fusion.2.refs_0_), channel_id=1, source_target_pairs={{0,3},{1,2},{2,1},{3,0},{4,7},{5,6},{6,5},{7,4},{8,11},{9,10},{10,... | collective-permute-start | bytes 393224 | tf_op jit(solution)/shard_map/ppermute | solution.py:37
  73.3 7.3 %collective-permute-start.27 = (bf16[128,512]{1,0:T(8,128)(2,1)S(1)}, bf16[128,512]{1,0:T(8,128)(2,1)S(1)}, u32[]{:S(2)}, u32[]{:S(2)}) collective-permute-start(bf16[128,512]{1,0:T(8,128)(2,1)S(1)} %add_convert_fusion.2.refs_0_), channel_id=1, source_target_pairs={{0,2},{1,3},{2,0},{3,1},{4,6},{5,7},{6,4},{7,5},{8,10},{9,11},{10,... | collective-permute-start | bytes 393224 | tf_op jit(solution)/shard_map/ppermute | solution.py:37
  76.8 5.9 %collective-permute-start.21 = (bf16[128,512]{1,0:T(8,128)(2,1)S(1)}, bf16[128,512]{1,0:T(8,128)(2,1)S(1)}, u32[]{:S(2)}, u32[]{:S(2)}) collective-permute-start(bf16[128,512]{1,0:T(8,128)(2,1)S(1)} %add_convert_fusion.4.refs_0_), channel_id=1, source_target_pairs={{0,3},{1,2},{2,1},{3,0},{4,7},{5,6},{6,5},{7,4},{8,11},{9,10},{10,... | collective-permute-start | bytes 393224 | tf_op jit(solution)/shard_map/ppermute | solution.py:37
  77.3 6.7 %collective-permute-start.20 = (bf16[128,512]{1,0:T(8,128)(2,1)S(1)}, bf16[128,512]{1,0:T(8,128)(2,1)S(1)}, u32[]{:S(2)}, u32[]{:S(2)}) collective-permute-start(bf16[128,512]{1,0:T(8,128)(2,1)S(1)} %add_convert_fusion.4.refs_0_), channel_id=1, source_target_pairs={{0,2},{1,3},{2,0},{3,1},{4,6},{5,7},{6,4},{7,5},{8,10},{9,11},{10,... | collective-permute-start | bytes 393224 | tf_op jit(solution)/shard_map/ppermute | solution.py:37
  79.4 7.5 %collective-permute-start.19 = (bf16[128,512]{1,0:T(8,128)(2,1)S(1)}, bf16[128,512]{1,0:T(8,128)(2,1)S(1)}, u32[]{:S(2)}, u32[]{:S(2)}) collective-permute-start(bf16[128,512]{1,0:T(8,128)(2,1)S(1)} %add_convert_fusion.4.refs_0_), channel_id=1, source_target_pairs={{0,1},{1,0},{2,3},{3,2},{4,5},{5,4},{6,7},{7,6},{8,9},{9,8},{10,11... | collective-permute-start | bytes 393224 | tf_op jit(solution)/shard_map/ppermute | solution.py:37
  89.9 8.0 %collective-permute-start.33 = (bf16[128,512]{1,0:T(8,128)(2,1)S(1)}, bf16[128,512]{1,0:T(8,128)(2,1)S(1)}, u32[]{:S(2)}, u32[]{:S(2)}) collective-permute-start(bf16[128,512]{1,0:T(8,128)(2,1)S(1)} %get-tuple-element.88), channel_id=1, source_target_pairs={{0,3},{1,2},{2,1},{3,0},{4,7},{5,6},{6,5},{7,4},{8,11},{9,10},{10,... | collective-permute-start | bytes 393224 | tf_op jit(solution)/shard_map/ppermute | solution.py:37
  90.0 8.3 %collective-permute-start.34 = (bf16[128,512]{1,0:T(8,128)(2,1)S(1)}, bf16[128,512]{1,0:T(8,128)(2,1)S(1)}, u32[]{:S(2)}, u32[]{:S(2)}) collective-permute-start(bf16[128,512]{1,0:T(8,128)(2,1)S(1)} %get-tuple-element.89), channel_id=1, source_target_pairs={{0,1},{1,0},{2,3},{3,2},{4,5},{5,4},{6,7},{7,6},{8,9},{9,8},{10,11... | collective-permute-start | bytes 393224 | tf_op jit(solution)/shard_map/ppermute | solution.py:37
  91.4 7.7 %collective-permute-start.35 = (bf16[128,512]{1,0:T(8,128)(2,1)S(1)}, bf16[128,512]{1,0:T(8,128)(2,1)S(1)}, u32[]{:S(2)}, u32[]{:S(2)}) collective-permute-start(bf16[128,512]{1,0:T(8,128)(2,1)S(1)} %get-tuple-element.90), channel_id=1, source_target_pairs={{0,2},{1,3},{2,0},{3,1},{4,6},{5,7},{6,4},{7,5},{8,10},{9,11},{10,... | collective-permute-start | bytes 393224 | tf_op jit(solution)/shard_map/ppermute | solution.py:37
  94.8 6.2 %collective-permute-start.29 = (bf16[128,512]{1,0:T(8,128)(2,1)S(1)}, bf16[128,512]{1,0:T(8,128)(2,1)S(1)}, u32[]{:S(2)}, u32[]{:S(2)}) collective-permute-start(bf16[128,512]{1,0:T(8,128)(2,1)S(1)} %get-tuple-element.84), channel_id=1, source_target_pairs={{0,3},{1,2},{2,1},{3,0},{4,7},{5,6},{6,5},{7,4},{8,11},{9,10},{10,... | collective-permute-start | bytes 393224 | tf_op jit(solution)/shard_map/ppermute | solution.py:37
  95.4 7.3 %collective-permute-start.30 = (bf16[128,512]{1,0:T(8,128)(2,1)S(1)}, bf16[128,512]{1,0:T(8,128)(2,1)S(1)}, u32[]{:S(2)}, u32[]{:S(2)}) collective-permute-start(bf16[128,512]{1,0:T(8,128)(2,1)S(1)} %get-tuple-element.85), channel_id=1, source_target_pairs={{0,1},{1,0},{2,3},{3,2},{4,5},{5,4},{6,7},{7,6},{8,9},{9,8},{10,11... | collective-permute-start | bytes 393224 | tf_op jit(solution)/shard_map/ppermute | solution.py:37
  98.0 5.8 %collective-permute-start.31 = (bf16[128,512]{1,0:T(8,128)(2,1)S(1)}, bf16[128,512]{1,0:T(8,128)(2,1)S(1)}, u32[]{:S(2)}, u32[]{:S(2)}) collective-permute-start(bf16[128,512]{1,0:T(8,128)(2,1)S(1)} %get-tuple-element.86), channel_id=1, source_target_pairs={{0,2},{1,3},{2,0},{3,1},{4,6},{5,7},{6,4},{7,5},{8,10},{9,11},{10,... | collective-permute-start | bytes 393224 | tf_op jit(solution)/shard_map/ppermute | solution.py:37
  99.4 7.5 %collective-permute-start.36 = (bf16[128,512]{1,0:T(8,128)(2,1)S(1)}, bf16[128,512]{1,0:T(8,128)(2,1)S(1)}, u32[]{:S(2)}, u32[]{:S(2)}) collective-permute-start(bf16[128,512]{1,0:T(8,128)(2,1)S(1)} %convolution_convert_fusion), channel_id=1, source_target_pairs={{0,6},{1,7},{2,4},{3,5},{4,2},{5,3},{6,0},{7,1},{8,14},{9,15},{10,... | collective-permute-start | bytes 393224 | tf_op jit(solution)/shard_map/ppermute | solution.py:37
  104.1 6.8 %collective-permute-start.32 = (bf16[128,512]{1,0:T(8,128)(2,1)S(1)}, bf16[128,512]{1,0:T(8,128)(2,1)S(1)}, u32[]{:S(2)}, u32[]{:S(2)}) collective-permute-start(bf16[128,512]{1,0:T(8,128)(2,1)S(1)} %convolution_convert_fusion.1), channel_id=1, source_target_pairs={{0,6},{1,7},{2,4},{3,5},{4,2},{5,3},{6,0},{7,1},{8,14},{9,15},{10,... | collective-permute-start | bytes 393224 | tf_op jit(solution)/shard_map/ppermute | solution.py:37
  (13 other events, 141.9 us)

commit v5 on v4

--- a/solution.py
+++ b/solution.py
@@ -14,6 +14,7 @@
 MOST = 32
 NEAR = 4
 META = 128
+INDEX_ROWS = 16
 FRONT_CUTS = 2
 ATTN_CUTS = 2
 BACK_CUTS = 2
@@ -140,13 +141,17 @@
         outs[k][:, :META] = meta
 
 
-def pack_kernel(done, *refs):
-    blocks, outs = refs[:NEAR], refs[NEAR:]
-    start = 0
-    for out in outs:
-        for k, block in enumerate(blocks):
-            out[k * MOST : (k + 1) * MOST] = block[:, start : start + out.shape[1]]
-        start += out.shape[1]
+def pack_kernel(start, wide, done, *refs):
+    blocks, out = refs[:NEAR], refs[NEAR]
+    for k, block in enumerate(blocks):
+        out[k * MOST : (k + 1) * MOST] = block[:, start : start + wide]
+    slots = NEAR * MOST
+    if out.shape[0] > slots:
+        index = jnp.concatenate([block[:, :slots].astype(f32) for block in blocks], axis=0)
+        corner = lax.broadcasted_iota(i32, (slots, slots), 0) == lax.broadcasted_iota(i32, (slots, slots), 1)
+        row = jnp.sum(jnp.where(corner, index, 0.0), axis=0, keepdims=True)
+        out[slots:] = jnp.zeros((INDEX_ROWS, wide), bf16)
+        out[slots:, :slots] = jnp.broadcast_to(row, (INDEX_ROWS, slots)).astype(bf16)
 
 
 def put_kernel(near, flags, scales, tokens, *refs):
@@ -193,7 +198,7 @@
     out[...] = dot(left[...], right[...]).astype(out.dtype)
 
 
-def attention_kernel(raw_q, raw_kv, order_k, order_v, cos_row, sin_row, cos_col, sin_col, done_a, done_b, out):
+def attention_kernel(raw_q, raw_kv, order_k, order_v, cos_row, sin_row, cos_col, sin_col, done, out):
     half = HEAD_SIZE // 2
     keys = dot(order_k[...], raw_kv[...])
     values = dot(order_v[...], raw_kv[...]).astype(bf16)
@@ -244,11 +249,14 @@
 
 
 def hidden_part_kernel(cuts, cut, near, gain, gate, up, *refs):
-    blocks, (gate_sum, up_sum, square_sum, rows) = refs[:NEAR], refs[NEAR:]
+    blocks, (down, gate_sum, up_sum, square_sum, down_first, rows, sem) = refs[:NEAR], refs[NEAR:]
+    copy = pltpu.make_async_copy(down.at[pl.ds(0, down_first.shape[0])], down_first, sem)
+    copy.start()
     total = gained(near, blocks, gain, rows, cuts, cut)
     square_sum[...] = jnp.broadcast_to(total, square_sum.shape)
     gate_sum[...] = cut_dot(near, rows, gate, cuts, cut)
     up_sum[...] = cut_dot(near, rows, up, cuts, cut)
+    copy.wait()
 
 
 def hidden_kernel(cuts, near, gain, gate, up, *refs):
@@ -336,37 +344,44 @@
             pltpu.SemaphoreType.DMA((2,)),
         ],
     )
-    key_w, value_w, query_w, done = load((key_weight, value_matrix, query_weight), parts[0], "load_qkv")
+    key_w, value_w, query_w, output_w, done = load(
+        (key_weight, value_matrix, query_weight, output_weight), parts[0], "load_qkvo"
+    )
 
     cuts = FRONT_CUTS
     wide = quarter // cuts
-    pieces = run(
-        pack_kernel,
-        "pack",
-        [shape((NEAR * MOST, wide + (0 if cut else META))) for cut in range(cuts)],
-        [ANY] + [VMEM] * NEAR,
-        done,
-        *([parts[0]] + [swap(parts[k], k) for k in (1, 2, 3)]),
-    )
-    gate_w, done = load((gate_weight,), pieces[0], "load_gate", zeros=(1, size * MOST))
-    all_rows = [
-        jnp.concatenate([piece] + [swap(piece, far_mask(k)) for k in range(1, far_size)], axis=0) for piece in pieces
-    ]
+    near_parts = [parts[0]] + [swap(parts[k], k) for k in (1, 2, 3)]
+    half_slots = NEAR * MOST
+    all_rows, index_rows = [], []
+    for cut in range(cuts):
+        piece = run(
+            functools.partial(pack_kernel, META + cut * wide, wide),
+            "pack",
+            shape((half_slots + (0 if cut else INDEX_ROWS), wide)),
+            [ANY] + [VMEM] * NEAR,
+            done,
+            *near_parts,
+        )
+        if cut == 0:
+            gate_w, done = load((gate_weight,), piece, "load_gate")
+        received = [piece] + [swap(piece, far_mask(k)) for k in range(1, far_size)]
+        if cut == 0:
+            index_rows = [rows[half_slots, :half_slots] for rows in received]
+        all_rows.append(jnp.concatenate([rows[:half_slots] for rows in received], axis=0))
     slots = size * MOST
-    all_index = all_rows[0][:, 0].astype(i32)
+    all_index = jnp.concatenate(index_rows).astype(i32)
     order = jnp.arange(slots, dtype=i32)
     far_of = far ^ (order // (NEAR * MOST))
     device_of = far_of * NEAR + (near ^ (order // MOST % NEAR) ^ (far_of & 1) * 2)
     taken = (all_index >= 0).astype(f32)
     earlier = (device_of[:, None] < device_of[None, :]).astype(f32)
-    rank_of = jnp.sum(earlier * taken[:, None], axis=0).astype(i32) + order % MOST + done[0]
+    rank_of = jnp.sum(earlier * taken[:, None], axis=0).astype(i32) + order % MOST
     pick_ids = jnp.arange(count, dtype=i32)
     select = (pick_ids[:, None] == rank_of[None, :]) & (all_index >= 0)[None, :]
     token_positions = jnp.sum(jnp.where(select, (device_of * tok_local + all_index)[None, :], 0), axis=1)
     select = select.astype(bf16)
-    all_rows[0] = all_rows[0][:, META:]
     row_parts = [dot(select, piece).astype(bf16) for piece in all_rows]
-    output_w, up_w, done = load((output_weight, up_weight), row_parts[0], "load_out_up")
+    up_w, done = load((up_weight,), row_parts[0], "load_up")
     row_blocks = near_gather(row_parts)
     rows_quarter = jnp.concatenate(row_parts, axis=1)
 
@@ -385,7 +400,7 @@
     row_id = jnp.arange(total_rows, dtype=i32)
     comp_id, is_value = row_id % comps, row_id // comps % 2
     to_far = far ^ (row_id // block_rows % far_size)
-    target = to_far * NEAR + (near ^ (row_id // (block_rows * far_size)) ^ (to_far & 1) * 2)
+    target = to_far * NEAR + (me % NEAR ^ (row_id // (block_rows * far_size)))
     column = comp_id * KEY_VALUE_HEADS + target * heads_here // group_width
     col_id = jnp.arange(key_weight.shape[1], dtype=i32)
     place = column[:, None] == col_id[None, :]
@@ -407,7 +422,6 @@
         limit=kernel_mib,
     )
     down_half = down_weight.shape[0] // 2
-    down_a, done_a = load((down_weight,), sends[0], "load_down", (0, down_half))
     got = [sends[0]] + [swap(sends[k], k) for k in (1, 2, 3)]
     raw_q = run(
         matmul_kernel, "query", shape((count, heads_here * HEAD_SIZE), f32), [VMEM, VMEM], rows_normed, query_w
@@ -415,11 +429,11 @@
     pieces = []
     for k in range(far_size):
         piece = jnp.concatenate([g[k * block_rows : (k + 1) * block_rows] for g in got], axis=0)
-        pieces.append(swap(piece, far_mask(k)) if k else piece)
-    down_b, done_b = load((down_weight,), pieces[0], "load_down", (down_half, down_half))
+        pieces.append(swap(piece, NEAR * k) if k else piece)
+    down_b, done = load((down_weight,), pieces[0], "load_down", (down_half, down_half))
     raw_kv = jnp.concatenate(pieces, axis=0)
     from_far = far ^ (row_id // (block_rows * NEAR))
-    origin = from_far * NEAR + (near ^ (row_id // block_rows % NEAR) ^ (from_far & 1) * 2)
+    origin = from_far * NEAR + (me % NEAR ^ (row_id // block_rows % NEAR))
     ordered = jnp.arange(HEAD_SIZE, dtype=i32)[:, None] == (origin * comps + comp_id)[None, :]
     order_k = (ordered & (is_value == 0)[None, :]).astype(bf16)
     order_v = (ordered & (is_value == 1)[None, :]).astype(bf16)
@@ -427,7 +441,7 @@
         attention_kernel,
         "attention",
         shape((count, heads_here * HEAD_SIZE)),
-        [VMEM] * 8 + [ANY] * 2,
+        [VMEM] * 8 + [ANY],
         raw_q,
         raw_kv,
         order_k,
@@ -436,8 +450,7 @@
         sin_row,
         cosine.T,
         sine.T,
-        done_a,
-        done_b,
+        done,
         limit=kernel_mib,
     )
 
@@ -451,19 +464,33 @@
     ]
     attn_quarter = jnp.concatenate(attn_parts, axis=1).astype(bf16)
     units = gate_weight.shape[1]
-    sums = []
-    for cut, part in enumerate(mixed_parts):
-        blocks = near_gather([part])
-        last = cut == cuts - 1
-        common = dict(scratch=[pltpu.VMEM((count, width // cuts), bf16)], limit=kernel_mib)
-        operands = (near_arr, ffn_gain, in_vmem(gate_w), in_vmem(up_w), *blocks)
-        specs = [SMEM] + [VMEM] * (3 + NEAR)
-        if not last:
-            outs = [shape((count, units), f32)] * 2 + [shape((count, 128), f32)]
-            kernel = functools.partial(hidden_part_kernel, cuts, cut)
-            sums += run(kernel, "hidden_part", outs, specs, *operands, **common)
+    rows_scratch = pltpu.VMEM((count, width // cuts), bf16)
+    weights = (near_arr, ffn_gain, in_vmem(gate_w), in_vmem(up_w))
+    specs = [SMEM] + [VMEM] * (3 + NEAR)
+    first_blocks, last_blocks = (near_gather([part]) for part in mixed_parts)
+    *sums, down_a = run(
+        functools.partial(hidden_part_kernel, cuts, 0),
+        "hidden_part",
+        [shape((count, units), f32)] * 2 + [shape((count, 128), f32), pltpu.VMEM((down_half, width), bf16)],
+        specs + [HBM],
+        *weights,
+        *first_blocks,
+        pltpu.with_memory_space_constraint(down_weight, pltpu.HBM),
+        scratch=[rows_scratch, pltpu.SemaphoreType.DMA],
+        limit=kernel_mib,
+    )
     kernel = functools.partial(hidden_kernel, cuts)
-    hidden = run(kernel, "hidden", shape((count, units)), specs + [VMEM] * len(sums), *operands, *sums, **common)
+    hidden = run(
+        kernel,
+        "hidden",
+        shape((count, units)),
+        specs + [VMEM] * len(sums),
+        *weights,
+        *last_blocks,
+        *sums,
+        scratch=[rows_scratch],
+        limit=kernel_mib,
+    )
 
     cuts = BACK_CUTS
     spread = select.reshape(count, far_size, NEAR * MOST)

time: 119 us -> 115 us (0.966)
  waiting for transfers between devices: 27.7 us -> 22 us
  starting transfers between devices: 55.3 us -> 57.9 us
    ppermute x40, waiting for transfers between devices: 27.7 us -> 22 us  [swap(): return lax.ppermute(value, 'ctx', [(i, i ^ mask) for i in range(size)])]
    pallas_call x5 -> x4, Pallas kernels: 18 us -> 15.3 us  [load(): pl.pallas_call(kernel, in_specs=[HBM] * count + [ANY], out_specs=[VMEM] *...]
    ppermute x40, starting transfers between devices: 55.3 us -> 57.9 us  [swap(): return lax.ppermute(value, 'ctx', [(i, i ^ mask) for i in range(size)])]
    pallas_call x11 -> x12, Pallas kernels: 11.6 us -> 13.5 us  [run(): pl.pallas_call(kernel, in_specs=specs, out_specs=outs, out_shape=out_shap...]
  transfers between devices with their start and end apart: 40 -> 40, of which waited for: 26 -> 20; matrix products, arithmetic and copies ran while one was open for 3% -> 3% of each run, Pallas kernels for 19% -> 19%
where the time goes in v5:
time: 115 us; the launch traced here: 114 us
  starting transfers between devices  57.9 us (50%)
  Pallas kernels  30.2 us (26%)
  waiting for transfers between devices  22 us (19%)
  matrix products  1.9 us (2%)
  other arithmetic  1.7 us (1%)
    ppermute x40, starting transfers between devices, swap(): return lax.ppermute(value, 'ctx', [(i, i ^ mask) for i in range(size)])  57.9 us
    ppermute x40, waiting for transfers between devices, swap(): return lax.ppermute(value, 'ctx', [(i, i ^ mask) for i in range(size)])  22 us
    pallas_call x4, Pallas kernels, load(): pl.pallas_call(kernel, in_specs=[HBM] * count + [ANY], out_specs=[VMEM] *...  15.3 us
    pallas_call x12, Pallas kernels, run(): pl.pallas_call(kernel, in_specs=specs, out_specs=outs, out_shape=out_shap...  13.5 us
  transfers between devices with their start and end apart: 40, of which 20 were waited for; matrix products, arithmetic and copies ran while one was open for 3% of the time, Pallas kernels for 19%

profile of v5, /device:TPU:0, one launch (start us, length us, event | category | flops | bytes accessed | tf_op | source)
XLA Modules:
  0.0 114.4 jit_solution(4303705658526138076)
XLA Ops:
  0.0 1.6 %pick.1 = (bf16[32,1152]{1,0:T(8,128)(2,1)S(1)}, bf16[32,1152]{1,0:T(8,128)(2,1)S(1)}, bf16[32,1152]{1,0:T(8,128)(2,1)S(1)}, bf16[32,1152]{1,0:T(8,128)(2,1)S(1)}) custom-call(s32[1]{0:T(128)} %bitcast.near, s32[1,128]{1,0:T(1,128)} %bitcast.29, bf16[128,4096]{1,0:T(8,128)(2,1)} %tokens.1), custom_call_target="tpu_custom_call" | custom-call | tf_op jit(solution)/shard_map/pick/pallas_call | solution.py:71
  1.6 3.0 %collective-permute-start = (bf16[32,1152]{1,0:T(8,128)(2,1)S(1)}, bf16[32,1152]{1,0:T(8,128)(2,1)S(1)}, u32[]{:S(2)}, u32[]{:S(2)}) collective-permute-start(bf16[32,1152]{1,0:T(8,128)(2,1)S(1)} %get-tuple-element.47), channel_id=1, source_target_pairs={{0,1},{1,0},{2,3},{3,2},{4,5},{5,4},{6,7},{7,6},{8,9},{9,8},{10,11... | collective-permute-start | bytes 221192 | tf_op jit(solution)/shard_map/ppermute | solution.py:38
  4.6 1.6 %collective-permute-start.1 = (bf16[32,1152]{1,0:T(8,128)(2,1)S(1)}, bf16[32,1152]{1,0:T(8,128)(2,1)S(1)}, u32[]{:S(2)}, u32[]{:S(2)}) collective-permute-start(bf16[32,1152]{1,0:T(8,128)(2,1)S(1)} %get-tuple-element.48), channel_id=1, source_target_pairs={{0,2},{1,3},{2,0},{3,1},{4,6},{5,7},{6,4},{7,5},{8,10},{9,11},{10,... | collective-permute-start | bytes 221192 | tf_op jit(solution)/shard_map/ppermute | solution.py:38
  6.4 4.1 %load_qkvo.1 = (bf16[4096,128]{1,0:T(8,128)(2,1)S(1)}, bf16[4096,128]{1,0:T(8,128)(2,1)S(1)}, bf16[4096,512]{1,0:T(8,128)(2,1)S(1)}, bf16[512,4096]{1,0:T(8,128)(2,1)S(1)}, s32[8,128]{1,0:T(8,128)S(1)}) custom-call(bf16[4096,128]{1,0:T(8,128)(2,1)} %refs_0_.4, bf16[4096,128]{1,0:T(8,128)(2,1)} %refs_1_.1, bf16[4096,512]{1,0:T(8,128)(2,1)} %refs_2_.1, ...), custom_call_target="tpu_custom_call" | custom-call | tf_op jit(solution)/shard_map/load_qkvo/pallas_call | solution.py:99
  11.5 3.2 %collective-permute-start.3 = (bf16[144,512]{1,0:T(8,128)(2,1)S(1)}, bf16[144,512]{1,0:T(8,128)(2,1)S(1)}, u32[]{:S(2)}, u32[]{:S(2)}) collective-permute-start(bf16[144,512]{1,0:T(8,128)(2,1)S(1)} %pack.2.refs_1_), channel_id=1, source_target_pairs={{0,6},{1,7},{2,4},{3,5},{4,2},{5,3},{6,0},{7,1},{8,14},{9,15},{10,... | collective-permute-start | bytes 442376 | tf_op jit(solution)/shard_map/ppermute | solution.py:38
  14.6 4.3 %load_gate.1 = (bf16[4096,1408]{1,0:T(8,128)(2,1)S(1)}, s32[8,128]{1,0:T(8,128)S(1)}) custom-call(bf16[4096,1408]{1,0:T(8,128)(2,1)} %refs_0_.5, bf16[144,512]{1,0:T(8,128)(2,1)S(1)} %pack.2.refs_1_), custom_call_target="tpu_custom_call" | custom-call | tf_op jit(solution)/shard_map/load_gate/pallas_call | solution.py:99
  20.1 3.8 %collective-permute-start.9 = (bf16[128,512]{1,0:T(8,128)(2,1)S(1)}, bf16[128,512]{1,0:T(8,128)(2,1)S(1)}, u32[]{:S(2)}, u32[]{:S(2)}) collective-permute-start(bf16[128,512]{1,0:T(8,128)(2,1)S(1)} %convolution_convert_fusion.3.refs_1_.refs_0_), channel_id=1, source_target_pairs={{0,3},{1,2},{2,1},{3,0},{4,7},{5,6},{6,5},{7,4},{8,11},{9,10},{10,... | collective-permute-start | bytes 393224 | tf_op jit(solution)/shard_map/ppermute | solution.py:38
  25.3 2.0 %collective-permute-done.4 = bf16[128,512]{1,0:T(8,128)(2,1)S(1)} collective-permute-done((bf16[128,512]{1,0:T(8,128)(2,1)S(1)}, bf16[128,512]{1,0:T(8,128)(2,1)S(1)}, u32[]{:S(2)}, u32[]{:S(2)}) %collective-permute-start.4) | collective-permute-done | bytes 131104 | tf_op jit(solution)/shard_map/ppermute | solution.py:38
  28.4 2.1 %collective-permute-start.8 = (bf16[128,512]{1,0:T(8,128)(2,1)S(1)}, bf16[128,512]{1,0:T(8,128)(2,1)S(1)}, u32[]{:S(2)}, u32[]{:S(2)}) collective-permute-start(bf16[128,512]{1,0:T(8,128)(2,1)S(1)} %convolution_convert_fusion.2.refs_1_), channel_id=1, source_target_pairs={{0,2},{1,3},{2,0},{3,1},{4,6},{5,7},{6,4},{7,5},{8,10},{9,11},{10,... | collective-permute-start | bytes 393224 | tf_op jit(solution)/shard_map/ppermute | solution.py:38
  31.2 4.3 %load_up.1 = (bf16[4096,1408]{1,0:T(8,128)(2,1)S(1)}, s32[8,128]{1,0:T(8,128)S(1)}) custom-call(bf16[4096,1408]{1,0:T(8,128)(2,1)} %refs_0_.6, bf16[128,512]{1,0:T(8,128)(2,1)S(1)} %convolution_convert_fusion.3.refs_1_.refs_0_), custom_call_target="tpu_custom_call" | custom-call | tf_op jit(solution)/shard_map/load_up/pallas_call | solution.py:99
  36.0 1.5 %keys_values.1 = (bf16[128,4096]{1,0:T(8,128)(2,1)S(1)}, bf16[64,128]{1,0:T(8,128)(2,1)S(1)}, bf16[64,128]{1,0:T(8,128)(2,1)S(1)}, bf16[64,128]{1,0:T(8,128)(2,1)S(1)}, bf16[64,128]{1,0:T(8,128)(2,1)S(1)}) custom-call(s32[1]{0:T(128)} %bitcast.near, f32[1,4096]{1,0:T(1,128)S(1)} %bitcast.28, bf16[4096,128]{1,0:T(8,128)(2,1)S(1)} %get-tuple-element.53.key_weight, ...), custom_call_target="tpu_custom_call" | custom-call | tf_op jit(solution)/shard_map/keys_values/pallas_call | solution.py:71
  39.0 2.0 %collective-permute-start.13 = (bf16[64,128]{1,0:T(8,128)(2,1)S(1)}, bf16[64,128]{1,0:T(8,128)(2,1)S(1)}, u32[]{:S(2)}, u32[]{:S(2)}) collective-permute-start(bf16[64,128]{1,0:T(8,128)(2,1)S(1)} %get-tuple-element.61), channel_id=1, source_target_pairs={{0,3},{1,2},{2,1},{3,0},{4,7},{5,6},{6,5},{7,4},{8,11},{9,10},{10,... | collective-permute-start | bytes 49160 | tf_op jit(solution)/shard_map/ppermute | solution.py:38
  43.7 2.7 %collective-permute-start.14 = (bf16[128,128]{1,0:T(8,128)(2,1)S(1)}, bf16[128,128]{1,0:T(8,128)(2,1)S(1)}, u32[]{:S(2)}, u32[]{:S(2)}) collective-permute-start(bf16[128,128]{1,0:T(8,128)(2,1)S(1)} %pad_maximum_fusion.3), channel_id=1, source_target_pairs={{0,4},{1,5},{2,6},{3,7},{4,0},{5,1},{6,2},{7,3},{8,12},{9,13},{10,... | collective-permute-start | bytes 98312 | tf_op jit(solution)/shard_map/ppermute | solution.py:38
  46.4 2.6 %load_down.1 = (bf16[704,4096]{1,0:T(8,128)(2,1)S(1)}, s32[8,128]{1,0:T(8,128)S(1)}) custom-call(bf16[1408,4096]{1,0:T(8,128)(2,1)} %refs_4_.1, bf16[128,128]{1,0:T(8,128)(2,1)S(1)} %pad_maximum_fusion.4.refs_1_), custom_call_target="tpu_custom_call" | custom-call | tf_op jit(solution)/shard_map/load_down/pallas_call | solution.py:99
  50.5 2.1 %collective-permute-start.22 = (bf16[128,512]{1,0:T(8,128)(2,1)S(1)}, bf16[128,512]{1,0:T(8,128)(2,1)S(1)}, u32[]{:S(2)}, u32[]{:S(2)}) collective-permute-start(bf16[128,512]{1,0:T(8,128)(2,1)S(1)} %get-tuple-element.69), channel_id=1, source_target_pairs={{0,3},{1,2},{2,1},{3,0},{4,7},{5,6},{6,5},{7,4},{8,11},{9,10},{10,... | collective-permute-start | bytes 393224 | tf_op jit(solution)/shard_map/ppermute | solution.py:38
  54.6 2.1 %collective-permute-start.15 = (bf16[128,512]{1,0:T(8,128)(2,1)S(1)}, bf16[128,512]{1,0:T(8,128)(2,1)S(1)}, u32[]{:S(2)}, u32[]{:S(2)}) collective-permute-start(bf16[128,512]{1,0:T(8,128)(2,1)S(1)} %get-tuple-element.65), channel_id=1, source_target_pairs={{0,3},{1,2},{2,1},{3,0},{4,7},{5,6},{6,5},{7,4},{8,11},{9,10},{10,... | collective-permute-start | bytes 393224 | tf_op jit(solution)/shard_map/ppermute | solution.py:38
  60.2 2.1 %collective-permute-start.25 = (bf16[128,512]{1,0:T(8,128)(2,1)S(1)}, bf16[128,512]{1,0:T(8,128)(2,1)S(1)}, u32[]{:S(2)}, u32[]{:S(2)}) collective-permute-start(bf16[128,512]{1,0:T(8,128)(2,1)S(1)} %add_convert_fusion.3), channel_id=1, source_target_pairs={{0,6},{1,7},{2,4},{3,5},{4,2},{5,3},{6,0},{7,1},{8,14},{9,15},{10,... | collective-permute-start | bytes 393224 | tf_op jit(solution)/shard_map/ppermute | solution.py:38
  62.9 1.9 %collective-permute-done.17 = bf16[128,512]{1,0:T(8,128)(2,1)S(1)} collective-permute-done((bf16[128,512]{1,0:T(8,128)(2,1)S(1)}, bf16[128,512]{1,0:T(8,128)(2,1)S(1)}, u32[]{:S(2)}, u32[]{:S(2)}) %collective-permute-start.17) | collective-permute-done | bytes 131104 | tf_op jit(solution)/shard_map/ppermute | solution.py:38
  64.8 2.7 %collective-permute-start.18 = (bf16[128,512]{1,0:T(8,128)(2,1)S(1)}, bf16[128,512]{1,0:T(8,128)(2,1)S(1)}, u32[]{:S(2)}, u32[]{:S(2)}) collective-permute-start(bf16[128,512]{1,0:T(8,128)(2,1)S(1)} %add_convert_fusion.5), channel_id=1, source_target_pairs={{0,6},{1,7},{2,4},{3,5},{4,2},{5,3},{6,0},{7,1},{8,14},{9,15},{10,... | collective-permute-start | bytes 393224 | tf_op jit(solution)/shard_map/ppermute | solution.py:38
  69.1 1.9 %collective-permute-start.27 = (bf16[128,512]{1,0:T(8,128)(2,1)S(1)}, bf16[128,512]{1,0:T(8,128)(2,1)S(1)}, u32[]{:S(2)}, u32[]{:S(2)}) collective-permute-start(bf16[128,512]{1,0:T(8,128)(2,1)S(1)} %add_convert_fusion.2.refs_0_), channel_id=1, source_target_pairs={{0,2},{1,3},{2,0},{3,1},{4,6},{5,7},{6,4},{7,5},{8,10},{9,11},{10,... | collective-permute-start | bytes 393224 | tf_op jit(solution)/shard_map/ppermute | solution.py:38
  71.0 1.6 %collective-permute-start.26 = (bf16[128,512]{1,0:T(8,128)(2,1)S(1)}, bf16[128,512]{1,0:T(8,128)(2,1)S(1)}, u32[]{:S(2)}, u32[]{:S(2)}) collective-permute-start(bf16[128,512]{1,0:T(8,128)(2,1)S(1)} %add_convert_fusion.2.refs_0_), channel_id=1, source_target_pairs={{0,1},{1,0},{2,3},{3,2},{4,5},{5,4},{6,7},{7,6},{8,9},{9,8},{10,11... | collective-permute-start | bytes 393224 | tf_op jit(solution)/shard_map/ppermute | solution.py:38
  75.1 1.7 %collective-permute-start.19 = (bf16[128,512]{1,0:T(8,128)(2,1)S(1)}, bf16[128,512]{1,0:T(8,128)(2,1)S(1)}, u32[]{:S(2)}, u32[]{:S(2)}) collective-permute-start(bf16[128,512]{1,0:T(8,128)(2,1)S(1)} %add_convert_fusion.4.refs_0_), channel_id=1, source_target_pairs={{0,1},{1,0},{2,3},{3,2},{4,5},{5,4},{6,7},{7,6},{8,9},{9,8},{10,11... | collective-permute-start | bytes 393224 | tf_op jit(solution)/shard_map/ppermute | solution.py:38
  77.0 3.7 %hidden_part.1 = (f32[128,1408]{1,0:T(8,128)S(1)}, f32[128,1408]{1,0:T(8,128)S(1)}, f32[128,128]{1,0:T(8,128)S(1)}, bf16[704,4096]{1,0:T(8,128)(2,1)S(1)}) custom-call(s32[1]{0:T(128)} %bitcast.near, f32[1,4096]{1,0:T(1,128)S(1)} %bitcast.26, bf16[4096,1408]{1,0:T(8,128)(2,1)S(1)} %get-tuple-element.50.gate, bf16[4096,1408]{1,0:T(8,128)(2,1)S(1)} %get-tuple-element.51.up, ...), custom_call_target="tpu_custom_call" | custom-call | tf_op jit(solution)/shard_map/hidden_part/pallas_call | solution.py:71
  80.7 2.5 %collective-permute-done.19.refs_1_ = bf16[128,512]{1,0:T(8,128)(2,1)S(1)} collective-permute-done((bf16[128,512]{1,0:T(8,128)(2,1)S(1)}, bf16[128,512]{1,0:T(8,128)(2,1)S(1)}, u32[]{:S(2)}, u32[]{:S(2)}) %collective-permute-start.19) | collective-permute-done | bytes 131104 | tf_op jit(solution)/shard_map/ppermute | solution.py:38
  83.2 2.0 %hidden.1.left = bf16[128,1408]{1,0:T(8,128)(2,1)S(1)} custom-call(s32[1]{0:T(128)} %bitcast.near, f32[1,4096]{1,0:T(1,128)S(1)} %bitcast.27, bf16[4096,1408]{1,0:T(8,128)(2,1)S(1)} %get-tuple-element.50.gate, bf16[4096,1408]{1,0:T(8,128)(2,1)S(1)} %get-tuple-element.51.up, bf16[128,512]{1,0:T(8,128)(2,1)S(1)} %add_convert_fusion.4.refs_0_, ...), custom_call_target="tpu_custom_call" | custom-call | tf_op jit(solution)/shard_map/hidden/pallas_call | solution.py:71
  87.6 2.3 %collective-permute-start.35 = (bf16[128,512]{1,0:T(8,128)(2,1)S(1)}, bf16[128,512]{1,0:T(8,128)(2,1)S(1)}, u32[]{:S(2)}, u32[]{:S(2)}) collective-permute-start(bf16[128,512]{1,0:T(8,128)(2,1)S(1)} %get-tuple-element.84), channel_id=1, source_target_pairs={{0,2},{1,3},{2,0},{3,1},{4,6},{5,7},{6,4},{7,5},{8,10},{9,11},{10,... | collective-permute-start | bytes 393224 | tf_op jit(solution)/shard_map/ppermute | solution.py:38
  95.2 2.4 %collective-permute-start.36 = (bf16[128,512]{1,0:T(8,128)(2,1)S(1)}, bf16[128,512]{1,0:T(8,128)(2,1)S(1)}, u32[]{:S(2)}, u32[]{:S(2)}) collective-permute-start(bf16[128,512]{1,0:T(8,128)(2,1)S(1)} %convolution_convert_fusion), channel_id=1, source_target_pairs={{0,6},{1,7},{2,4},{3,5},{4,2},{5,3},{6,0},{7,1},{8,14},{9,15},{10,... | collective-permute-start | bytes 393224 | tf_op jit(solution)/shard_map/ppermute | solution.py:38
  97.8 1.6 %collective-permute-done.30 = bf16[128,512]{1,0:T(8,128)(2,1)S(1)} collective-permute-done((bf16[128,512]{1,0:T(8,128)(2,1)S(1)}, bf16[128,512]{1,0:T(8,128)(2,1)S(1)}, u32[]{:S(2)}, u32[]{:S(2)}) %collective-permute-start.30) | collective-permute-done | bytes 131104 | tf_op jit(solution)/shard_map/ppermute | solution.py:38
  99.9 2.2 %collective-permute-start.32 = (bf16[128,512]{1,0:T(8,128)(2,1)S(1)}, bf16[128,512]{1,0:T(8,128)(2,1)S(1)}, u32[]{:S(2)}, u32[]{:S(2)}) collective-permute-start(bf16[128,512]{1,0:T(8,128)(2,1)S(1)} %convolution_convert_fusion.1), channel_id=1, source_target_pairs={{0,6},{1,7},{2,4},{3,5},{4,2},{5,3},{6,0},{7,1},{8,14},{9,15},{10,... | collective-permute-start | bytes 393224 | tf_op jit(solution)/shard_map/ppermute | solution.py:38
  102.5 4.2 %collective-permute-done.32 = bf16[128,512]{1,0:T(8,128)(2,1)S(1)} collective-permute-done((bf16[128,512]{1,0:T(8,128)(2,1)S(1)}, bf16[128,512]{1,0:T(8,128)(2,1)S(1)}, u32[]{:S(2)}, u32[]{:S(2)}) %collective-permute-start.32) | collective-permute-done | bytes 131104 | tf_op jit(solution)/shard_map/ppermute | solution.py:38
  108.2 2.3 %collective-permute-start.38 = (bf16[32,1024]{1,0:T(8,128)(2,1)S(1)}, bf16[32,1024]{1,0:T(8,128)(2,1)S(1)}, u32[]{:S(2)}, u32[]{:S(2)}) collective-permute-start(bf16[32,1024]{1,0:T(8,128)(2,1)S(1)} %get-tuple-element.90), channel_id=1, source_target_pairs={{0,2},{1,3},{2,0},{3,1},{4,6},{5,7},{6,4},{7,5},{8,10},{9,11},{10,... | collective-permute-start | bytes 196616 | tf_op jit(solution)/shard_map/ppermute | solution.py:38
  110.6 1.7 %collective-permute-done.39.refs_3_ = bf16[32,1024]{1,0:T(8,128)(2,1)S(1)} collective-permute-done((bf16[32,1024]{1,0:T(8,128)(2,1)S(1)}, bf16[32,1024]{1,0:T(8,128)(2,1)S(1)}, u32[]{:S(2)}, u32[]{:S(2)}) %collective-permute-start.39) | collective-permute-done | bytes 65568 | tf_op jit(solution)/shard_map/ppermute | solution.py:38
  (119 shorter events, 33.9 us)
Async XLA Ops:
  1.6 8.9 %collective-permute-start = (bf16[32,1152]{1,0:T(8,128)(2,1)S(1)}, bf16[32,1152]{1,0:T(8,128)(2,1)S(1)}, u32[]{:S(2)}, u32[]{:S(2)}) collective-permute-start(bf16[32,1152]{1,0:T(8,128)(2,1)S(1)} %get-tuple-element.47), channel_id=1, source_target_pairs={{0,1},{1,0},{2,3},{3,2},{4,5},{5,4},{6,7},{7,6},{8,9},{9,8},{10,11... | collective-permute-start | bytes 221192 | tf_op jit(solution)/shard_map/ppermute | solution.py:38
  4.6 5.9 %collective-permute-start.1 = (bf16[32,1152]{1,0:T(8,128)(2,1)S(1)}, bf16[32,1152]{1,0:T(8,128)(2,1)S(1)}, u32[]{:S(2)}, u32[]{:S(2)}) collective-permute-start(bf16[32,1152]{1,0:T(8,128)(2,1)S(1)} %get-tuple-element.48), channel_id=1, source_target_pairs={{0,2},{1,3},{2,0},{3,1},{4,6},{5,7},{6,4},{7,5},{8,10},{9,11},{10,... | collective-permute-start | bytes 221192 | tf_op jit(solution)/shard_map/ppermute | solution.py:38
  11.5 8.3 %collective-permute-start.3 = (bf16[144,512]{1,0:T(8,128)(2,1)S(1)}, bf16[144,512]{1,0:T(8,128)(2,1)S(1)}, u32[]{:S(2)}, u32[]{:S(2)}) collective-permute-start(bf16[144,512]{1,0:T(8,128)(2,1)S(1)} %pack.2.refs_1_), channel_id=1, source_target_pairs={{0,6},{1,7},{2,4},{3,5},{4,2},{5,3},{6,0},{7,1},{8,14},{9,15},{10,... | collective-permute-start | bytes 442376 | tf_op jit(solution)/shard_map/ppermute | solution.py:38
  18.9 8.3 %collective-permute-start.4 = (bf16[128,512]{1,0:T(8,128)(2,1)S(1)}, bf16[128,512]{1,0:T(8,128)(2,1)S(1)}, u32[]{:S(2)}, u32[]{:S(2)}) collective-permute-start(bf16[128,512]{1,0:T(8,128)(2,1)S(1)} %pack.3), channel_id=1, source_target_pairs={{0,6},{1,7},{2,4},{3,5},{4,2},{5,3},{6,0},{7,1},{8,14},{9,15},{10,... | collective-permute-start | bytes 393224 | tf_op jit(solution)/shard_map/ppermute | solution.py:38
  20.1 10.4 %collective-permute-start.9 = (bf16[128,512]{1,0:T(8,128)(2,1)S(1)}, bf16[128,512]{1,0:T(8,128)(2,1)S(1)}, u32[]{:S(2)}, u32[]{:S(2)}) collective-permute-start(bf16[128,512]{1,0:T(8,128)(2,1)S(1)} %convolution_convert_fusion.3.refs_1_.refs_0_), channel_id=1, source_target_pairs={{0,3},{1,2},{2,1},{3,0},{4,7},{5,6},{6,5},{7,4},{8,11},{9,10},{10,... | collective-permute-start | bytes 393224 | tf_op jit(solution)/shard_map/ppermute | solution.py:38
  24.0 11.7 %collective-permute-start.7 = (bf16[128,512]{1,0:T(8,128)(2,1)S(1)}, bf16[128,512]{1,0:T(8,128)(2,1)S(1)}, u32[]{:S(2)}, u32[]{:S(2)}) collective-permute-start(bf16[128,512]{1,0:T(8,128)(2,1)S(1)} %convolution_convert_fusion.3.refs_1_.refs_0_), channel_id=1, source_target_pairs={{0,2},{1,3},{2,0},{3,1},{4,6},{5,7},{6,4},{7,5},{8,10},{9,11},{10,... | collective-permute-start | bytes 393224 | tf_op jit(solution)/shard_map/ppermute | solution.py:38
  24.0 11.7 %collective-permute-start.5 = (bf16[128,512]{1,0:T(8,128)(2,1)S(1)}, bf16[128,512]{1,0:T(8,128)(2,1)S(1)}, u32[]{:S(2)}, u32[]{:S(2)}) collective-permute-start(bf16[128,512]{1,0:T(8,128)(2,1)S(1)} %convolution_convert_fusion.3.refs_1_.refs_0_), channel_id=1, source_target_pairs={{0,1},{1,0},{2,3},{3,2},{4,5},{5,4},{6,7},{7,6},{8,9},{9,8},{10,11... | collective-permute-start | bytes 393224 | tf_op jit(solution)/shard_map/ppermute | solution.py:38
  27.4 8.2 %collective-permute-start.10 = (bf16[128,512]{1,0:T(8,128)(2,1)S(1)}, bf16[128,512]{1,0:T(8,128)(2,1)S(1)}, u32[]{:S(2)}, u32[]{:S(2)}) collective-permute-start(bf16[128,512]{1,0:T(8,128)(2,1)S(1)} %convolution_convert_fusion.2.refs_1_), channel_id=1, source_target_pairs={{0,3},{1,2},{2,1},{3,0},{4,7},{5,6},{6,5},{7,4},{8,11},{9,10},{10,... | collective-permute-start | bytes 393224 | tf_op jit(solution)/shard_map/ppermute | solution.py:38
  28.4 7.5 %collective-permute-start.8 = (bf16[128,512]{1,0:T(8,128)(2,1)S(1)}, bf16[128,512]{1,0:T(8,128)(2,1)S(1)}, u32[]{:S(2)}, u32[]{:S(2)}) collective-permute-start(bf16[128,512]{1,0:T(8,128)(2,1)S(1)} %convolution_convert_fusion.2.refs_1_), channel_id=1, source_target_pairs={{0,2},{1,3},{2,0},{3,1},{4,6},{5,7},{6,4},{7,5},{8,10},{9,11},{10,... | collective-permute-start | bytes 393224 | tf_op jit(solution)/shard_map/ppermute | solution.py:38
  30.5 5.4 %collective-permute-start.6 = (bf16[128,512]{1,0:T(8,128)(2,1)S(1)}, bf16[128,512]{1,0:T(8,128)(2,1)S(1)}, u32[]{:S(2)}, u32[]{:S(2)}) collective-permute-start(bf16[128,512]{1,0:T(8,128)(2,1)S(1)} %convolution_convert_fusion.2.refs_1_), channel_id=1, source_target_pairs={{0,1},{1,0},{2,3},{3,2},{4,5},{5,4},{6,7},{7,6},{8,9},{9,8},{10,11... | collective-permute-start | bytes 393224 | tf_op jit(solution)/shard_map/ppermute | solution.py:38
  50.5 7.6 %collective-permute-start.22 = (bf16[128,512]{1,0:T(8,128)(2,1)S(1)}, bf16[128,512]{1,0:T(8,128)(2,1)S(1)}, u32[]{:S(2)}, u32[]{:S(2)}) collective-permute-start(bf16[128,512]{1,0:T(8,128)(2,1)S(1)} %get-tuple-element.69), channel_id=1, source_target_pairs={{0,3},{1,2},{2,1},{3,0},{4,7},{5,6},{6,5},{7,4},{8,11},{9,10},{10,... | collective-permute-start | bytes 393224 | tf_op jit(solution)/shard_map/ppermute | solution.py:38
  52.6 7.0 %collective-permute-start.23 = (bf16[128,512]{1,0:T(8,128)(2,1)S(1)}, bf16[128,512]{1,0:T(8,128)(2,1)S(1)}, u32[]{:S(2)}, u32[]{:S(2)}) collective-permute-start(bf16[128,512]{1,0:T(8,128)(2,1)S(1)} %get-tuple-element.70), channel_id=1, source_target_pairs={{0,1},{1,0},{2,3},{3,2},{4,5},{5,4},{6,7},{7,6},{8,9},{9,8},{10,11... | collective-permute-start | bytes 393224 | tf_op jit(solution)/shard_map/ppermute | solution.py:38
  54.1 6.1 %collective-permute-start.24 = (bf16[128,512]{1,0:T(8,128)(2,1)S(1)}, bf16[128,512]{1,0:T(8,128)(2,1)S(1)}, u32[]{:S(2)}, u32[]{:S(2)}) collective-permute-start(bf16[128,512]{1,0:T(8,128)(2,1)S(1)} %get-tuple-element.71), channel_id=1, source_target_pairs={{0,2},{1,3},{2,0},{3,1},{4,6},{5,7},{6,4},{7,5},{8,10},{9,11},{10,... | collective-permute-start | bytes 393224 | tf_op jit(solution)/shard_map/ppermute | solution.py:38
  54.6 7.7 %collective-permute-start.15 = (bf16[128,512]{1,0:T(8,128)(2,1)S(1)}, bf16[128,512]{1,0:T(8,128)(2,1)S(1)}, u32[]{:S(2)}, u32[]{:S(2)}) collective-permute-start(bf16[128,512]{1,0:T(8,128)(2,1)S(1)} %get-tuple-element.65), channel_id=1, source_target_pairs={{0,3},{1,2},{2,1},{3,0},{4,7},{5,6},{6,5},{7,4},{8,11},{9,10},{10,... | collective-permute-start | bytes 393224 | tf_op jit(solution)/shard_map/ppermute | solution.py:38
  56.7 6.2 %collective-permute-start.16 = (bf16[128,512]{1,0:T(8,128)(2,1)S(1)}, bf16[128,512]{1,0:T(8,128)(2,1)S(1)}, u32[]{:S(2)}, u32[]{:S(2)}) collective-permute-start(bf16[128,512]{1,0:T(8,128)(2,1)S(1)} %get-tuple-element.66), channel_id=1, source_target_pairs={{0,1},{1,0},{2,3},{3,2},{4,5},{5,4},{6,7},{7,6},{8,9},{9,8},{10,11... | collective-permute-start | bytes 393224 | tf_op jit(solution)/shard_map/ppermute | solution.py:38
  58.1 6.6 %collective-permute-start.17 = (bf16[128,512]{1,0:T(8,128)(2,1)S(1)}, bf16[128,512]{1,0:T(8,128)(2,1)S(1)}, u32[]{:S(2)}, u32[]{:S(2)}) collective-permute-start(bf16[128,512]{1,0:T(8,128)(2,1)S(1)} %get-tuple-element.67), channel_id=1, source_target_pairs={{0,2},{1,3},{2,0},{3,1},{4,6},{5,7},{6,4},{7,5},{8,10},{9,11},{10,... | collective-permute-start | bytes 393224 | tf_op jit(solution)/shard_map/ppermute | solution.py:38
  60.2 8.8 %collective-permute-start.25 = (bf16[128,512]{1,0:T(8,128)(2,1)S(1)}, bf16[128,512]{1,0:T(8,128)(2,1)S(1)}, u32[]{:S(2)}, u32[]{:S(2)}) collective-permute-start(bf16[128,512]{1,0:T(8,128)(2,1)S(1)} %add_convert_fusion.3), channel_id=1, source_target_pairs={{0,6},{1,7},{2,4},{3,5},{4,2},{5,3},{6,0},{7,1},{8,14},{9,15},{10,... | collective-permute-start | bytes 393224 | tf_op jit(solution)/shard_map/ppermute | solution.py:38
  64.8 8.3 %collective-permute-start.18 = (bf16[128,512]{1,0:T(8,128)(2,1)S(1)}, bf16[128,512]{1,0:T(8,128)(2,1)S(1)}, u32[]{:S(2)}, u32[]{:S(2)}) collective-permute-start(bf16[128,512]{1,0:T(8,128)(2,1)S(1)} %add_convert_fusion.5), channel_id=1, source_target_pairs={{0,6},{1,7},{2,4},{3,5},{4,2},{5,3},{6,0},{7,1},{8,14},{9,15},{10,... | collective-permute-start | bytes 393224 | tf_op jit(solution)/shard_map/ppermute | solution.py:38
  69.1 6.0 %collective-permute-start.28 = (bf16[128,512]{1,0:T(8,128)(2,1)S(1)}, bf16[128,512]{1,0:T(8,128)(2,1)S(1)}, u32[]{:S(2)}, u32[]{:S(2)}) collective-permute-start(bf16[128,512]{1,0:T(8,128)(2,1)S(1)} %add_convert_fusion.2.refs_0_), channel_id=1, source_target_pairs={{0,3},{1,2},{2,1},{3,0},{4,7},{5,6},{6,5},{7,4},{8,11},{9,10},{10,... | collective-permute-start | bytes 393224 | tf_op jit(solution)/shard_map/ppermute | solution.py:38
  69.1 7.8 %collective-permute-start.27 = (bf16[128,512]{1,0:T(8,128)(2,1)S(1)}, bf16[128,512]{1,0:T(8,128)(2,1)S(1)}, u32[]{:S(2)}, u32[]{:S(2)}) collective-permute-start(bf16[128,512]{1,0:T(8,128)(2,1)S(1)} %add_convert_fusion.2.refs_0_), channel_id=1, source_target_pairs={{0,2},{1,3},{2,0},{3,1},{4,6},{5,7},{6,4},{7,5},{8,10},{9,11},{10,... | collective-permute-start | bytes 393224 | tf_op jit(solution)/shard_map/ppermute | solution.py:38
  71.0 5.9 %collective-permute-start.26 = (bf16[128,512]{1,0:T(8,128)(2,1)S(1)}, bf16[128,512]{1,0:T(8,128)(2,1)S(1)}, u32[]{:S(2)}, u32[]{:S(2)}) collective-permute-start(bf16[128,512]{1,0:T(8,128)(2,1)S(1)} %add_convert_fusion.2.refs_0_), channel_id=1, source_target_pairs={{0,1},{1,0},{2,3},{3,2},{4,5},{5,4},{6,7},{7,6},{8,9},{9,8},{10,11... | collective-permute-start | bytes 393224 | tf_op jit(solution)/shard_map/ppermute | solution.py:38
  73.2 7.5 %collective-permute-start.21 = (bf16[128,512]{1,0:T(8,128)(2,1)S(1)}, bf16[128,512]{1,0:T(8,128)(2,1)S(1)}, u32[]{:S(2)}, u32[]{:S(2)}) collective-permute-start(bf16[128,512]{1,0:T(8,128)(2,1)S(1)} %add_convert_fusion.4.refs_0_), channel_id=1, source_target_pairs={{0,3},{1,2},{2,1},{3,0},{4,7},{5,6},{6,5},{7,4},{8,11},{9,10},{10,... | collective-permute-start | bytes 393224 | tf_op jit(solution)/shard_map/ppermute | solution.py:38
  73.6 7.1 %collective-permute-start.20 = (bf16[128,512]{1,0:T(8,128)(2,1)S(1)}, bf16[128,512]{1,0:T(8,128)(2,1)S(1)}, u32[]{:S(2)}, u32[]{:S(2)}) collective-permute-start(bf16[128,512]{1,0:T(8,128)(2,1)S(1)} %add_convert_fusion.4.refs_0_), channel_id=1, source_target_pairs={{0,2},{1,3},{2,0},{3,1},{4,6},{5,7},{6,4},{7,5},{8,10},{9,11},{10,... | collective-permute-start | bytes 393224 | tf_op jit(solution)/shard_map/ppermute | solution.py:38
  75.1 8.2 %collective-permute-start.19 = (bf16[128,512]{1,0:T(8,128)(2,1)S(1)}, bf16[128,512]{1,0:T(8,128)(2,1)S(1)}, u32[]{:S(2)}, u32[]{:S(2)}) collective-permute-start(bf16[128,512]{1,0:T(8,128)(2,1)S(1)} %add_convert_fusion.4.refs_0_), channel_id=1, source_target_pairs={{0,1},{1,0},{2,3},{3,2},{4,5},{5,4},{6,7},{7,6},{8,9},{9,8},{10,11... | collective-permute-start | bytes 393224 | tf_op jit(solution)/shard_map/ppermute | solution.py:38
  86.3 7.3 %collective-permute-start.33 = (bf16[128,512]{1,0:T(8,128)(2,1)S(1)}, bf16[128,512]{1,0:T(8,128)(2,1)S(1)}, u32[]{:S(2)}, u32[]{:S(2)}) collective-permute-start(bf16[128,512]{1,0:T(8,128)(2,1)S(1)} %get-tuple-element.82), channel_id=1, source_target_pairs={{0,3},{1,2},{2,1},{3,0},{4,7},{5,6},{6,5},{7,4},{8,11},{9,10},{10,... | collective-permute-start | bytes 393224 | tf_op jit(solution)/shard_map/ppermute | solution.py:38
  86.4 8.5 %collective-permute-start.34 = (bf16[128,512]{1,0:T(8,128)(2,1)S(1)}, bf16[128,512]{1,0:T(8,128)(2,1)S(1)}, u32[]{:S(2)}, u32[]{:S(2)}) collective-permute-start(bf16[128,512]{1,0:T(8,128)(2,1)S(1)} %get-tuple-element.83), channel_id=1, source_target_pairs={{0,1},{1,0},{2,3},{3,2},{4,5},{5,4},{6,7},{7,6},{8,9},{9,8},{10,11... | collective-permute-start | bytes 393224 | tf_op jit(solution)/shard_map/ppermute | solution.py:38
  87.6 7.3 %collective-permute-start.35 = (bf16[128,512]{1,0:T(8,128)(2,1)S(1)}, bf16[128,512]{1,0:T(8,128)(2,1)S(1)}, u32[]{:S(2)}, u32[]{:S(2)}) collective-permute-start(bf16[128,512]{1,0:T(8,128)(2,1)S(1)} %get-tuple-element.84), channel_id=1, source_target_pairs={{0,2},{1,3},{2,0},{3,1},{4,6},{5,7},{6,4},{7,5},{8,10},{9,11},{10,... | collective-permute-start | bytes 393224 | tf_op jit(solution)/shard_map/ppermute | solution.py:38
  91.3 6.5 %collective-permute-start.29 = (bf16[128,512]{1,0:T(8,128)(2,1)S(1)}, bf16[128,512]{1,0:T(8,128)(2,1)S(1)}, u32[]{:S(2)}, u32[]{:S(2)}) collective-permute-start(bf16[128,512]{1,0:T(8,128)(2,1)S(1)} %get-tuple-element.78), channel_id=1, source_target_pairs={{0,3},{1,2},{2,1},{3,0},{4,7},{5,6},{6,5},{7,4},{8,11},{9,10},{10,... | collective-permute-start | bytes 393224 | tf_op jit(solution)/shard_map/ppermute | solution.py:38
  91.7 7.8 %collective-permute-start.30 = (bf16[128,512]{1,0:T(8,128)(2,1)S(1)}, bf16[128,512]{1,0:T(8,128)(2,1)S(1)}, u32[]{:S(2)}, u32[]{:S(2)}) collective-permute-start(bf16[128,512]{1,0:T(8,128)(2,1)S(1)} %get-tuple-element.79), channel_id=1, source_target_pairs={{0,1},{1,0},{2,3},{3,2},{4,5},{5,4},{6,7},{7,6},{8,9},{9,8},{10,11... | collective-permute-start | bytes 393224 | tf_op jit(solution)/shard_map/ppermute | solution.py:38
  93.6 5.9 %collective-permute-start.31 = (bf16[128,512]{1,0:T(8,128)(2,1)S(1)}, bf16[128,512]{1,0:T(8,128)(2,1)S(1)}, u32[]{:S(2)}, u32[]{:S(2)}) collective-permute-start(bf16[128,512]{1,0:T(8,128)(2,1)S(1)} %get-tuple-element.80), channel_id=1, source_target_pairs={{0,2},{1,3},{2,0},{3,1},{4,6},{5,7},{6,4},{7,5},{8,10},{9,11},{10,... | collective-permute-start | bytes 393224 | tf_op jit(solution)/shard_map/ppermute | solution.py:38
  95.2 7.1 %collective-permute-start.36 = (bf16[128,512]{1,0:T(8,128)(2,1)S(1)}, bf16[128,512]{1,0:T(8,128)(2,1)S(1)}, u32[]{:S(2)}, u32[]{:S(2)}) collective-permute-start(bf16[128,512]{1,0:T(8,128)(2,1)S(1)} %convolution_convert_fusion), channel_id=1, source_target_pairs={{0,6},{1,7},{2,4},{3,5},{4,2},{5,3},{6,0},{7,1},{8,14},{9,15},{10,... | collective-permute-start | bytes 393224 | tf_op jit(solution)/shard_map/ppermute | solution.py:38
  99.9 6.9 %collective-permute-start.32 = (bf16[128,512]{1,0:T(8,128)(2,1)S(1)}, bf16[128,512]{1,0:T(8,128)(2,1)S(1)}, u32[]{:S(2)}, u32[]{:S(2)}) collective-permute-start(bf16[128,512]{1,0:T(8,128)(2,1)S(1)} %convolution_convert_fusion.1), channel_id=1, source_target_pairs={{0,6},{1,7},{2,4},{3,5},{4,2},{5,3},{6,0},{7,1},{8,14},{9,15},{10,... | collective-permute-start | bytes 393224 | tf_op jit(solution)/shard_map/ppermute | solution.py:38
  (13 other events, 137.6 us)

commit v6 on v5

--- a/solution.py
+++ b/solution.py
@@ -15,9 +15,15 @@
 NEAR = 4
 META = 128
 INDEX_ROWS = 16
+PICK_ORDER = (1, 2, 3)
+ROWS_ORDER = (1, 2, 3)
+KEYS_ORDER = (1, 2, 3)
+ATTN_ORDER = (3, 1, 2)
+MIXED_ORDER = (1, 2, 3)
+FFN_ORDER = (3, 1, 2)
+BACK_ORDER = (1, 2, 3)
 FRONT_CUTS = 2
 ATTN_CUTS = 2
-BACK_CUTS = 2
 
 norm_eps = 1e-05
 rope_base = 500000.0
@@ -80,16 +86,24 @@
 
 
 def load(weights, after, name, rows=None, zeros=(8, 128)):
-    count = len(weights)
+    groups = [weight if isinstance(weight, tuple) else (weight,) for weight in weights]
+    flat = [weight for group in groups for weight in group]
 
     def kernel(*refs):
-        sources, targets, done, sems = refs[:count], refs[count + 1 : -2], refs[-2], refs[-1]
-        if rows:
-            sources = [source.at[pl.ds(*rows)] for source in sources]
-        copies = [
-            pltpu.make_async_copy(source, target, sems.at[i])
-            for i, (source, target) in enumerate(zip(sources, targets))
-        ]
+        sources, targets, done, sems = refs[: len(flat)], refs[len(flat) + 1 : -2], refs[-2], refs[-1]
+        pairs = []
+        for group, target in zip(groups, targets):
+            start = 0
+            for weight in group:
+                source, size = sources[len(pairs)], weight.shape[1]
+                pairs.append(
+                    (
+                        source.at[pl.ds(*rows)] if rows else source,
+                        target.at[:, pl.ds(start, size)] if len(group) > 1 else target,
+                    )
+                )
+                start += size
+        copies = [pltpu.make_async_copy(source, target, sems.at[i]) for i, (source, target) in enumerate(pairs)]
         for copy in copies:
             copy.start()
         for copy in copies:
@@ -98,13 +112,17 @@
 
     return pl.pallas_call(
         kernel,
-        in_specs=[HBM] * count + [ANY],
-        out_specs=[VMEM] * (count + 1),
-        out_shape=[pltpu.VMEM((rows[1] if rows else w.shape[0], w.shape[1]), w.dtype) for w in weights] + [pltpu.VMEM(zeros, i32)],
-        scratch_shapes=[pltpu.SemaphoreType.DMA((count,))],
+        in_specs=[HBM] * len(flat) + [ANY],
+        out_specs=[VMEM] * (len(groups) + 1),
+        out_shape=[
+            pltpu.VMEM((rows[1] if rows else group[0].shape[0], sum(w.shape[1] for w in group)), group[0].dtype)
+            for group in groups
+        ]
+        + [pltpu.VMEM(zeros, i32)],
+        scratch_shapes=[pltpu.SemaphoreType.DMA((len(flat),))],
         compiler_params=pltpu.CompilerParams(vmem_limit_bytes=MIB),
         name=name,
-    )(*[pltpu.with_memory_space_constraint(w, pltpu.HBM) for w in weights], after)
+    )(*[pltpu.with_memory_space_constraint(w, pltpu.HBM) for w in flat], after)
 
 
 def in_vmem(value):
@@ -183,12 +201,11 @@
         out[:, cols] = (block[...].astype(f32) * scale * gain[:, cols]).astype(bf16)
 
 
-def kv_kernel(near, gain, key_weight, value_weight, place_k, place_v, done, *refs):
+def kv_kernel(near, gain, kv_weight, place, done, *refs):
     blocks, (rows, *outs) = refs[: -1 - NEAR], refs[-1 - NEAR :]
     normed(near, blocks, gain, rows)
-    keys = dot(rows[...], key_weight[...]).astype(bf16)
-    values = dot(rows[...], value_weight[...]).astype(bf16)
-    sends = (dot_nt(place_k[...], keys) + dot_nt(place_v[...], values)).astype(bf16)
+    both = dot(rows[...], kv_weight[...]).astype(bf16)
+    sends = dot_nt(place[...], both).astype(bf16)
     height = outs[0].shape[0]
     for k, out in enumerate(outs):
         out[...] = sends[k * height : (k + 1) * height]
@@ -218,11 +235,11 @@
         out[:, cols] = dot_nt(probs, values).astype(bf16)
 
 
-def block_kernel(cuts, cut, near, left, *refs):
+def block_kernel(start, near, left, *refs):
     rights, outs = refs[:-NEAR], refs[-NEAR:]
-    depth = rights[0].shape[0]
+    depth, quarter, wide = rights[0].shape[0], rights[0].shape[1] // NEAR, outs[0].shape[1]
     for k in (3, 1, 2, 0):
-        cols = part_cols(near, k * cuts + cut, cuts, outs[k].shape[1])
+        cols = pl.ds(pl.multiple_of((near[0] ^ k) * quarter + start, 128), wide)
         total = 0.0
         for i, right in enumerate(rights):
             total += dot(left[:, i * depth : (i + 1) * depth], right[:, cols])
@@ -272,14 +289,21 @@
     out[...] = (jax.nn.silu(gate_sum * scale) * (up_sum * scale)).astype(bf16)
 
 
-def column_blocks(near_arr, left, rights, cuts, cut, name):
-    dims = (left.shape[0], rights[0].shape[1] // NEAR // cuts)
-    kernel = functools.partial(block_kernel, cuts, cut)
-    return run(kernel, name, [shape(dims)] * NEAR, [SMEM, VMEM] + [VMEM] * len(rights), near_arr, left, *rights)
-
-
-def near_gather(parts):
-    got = [[part] + [swap(part, k) for k in (1, 2, 3)] for part in parts]
+def column_blocks(near_arr, left, rights, start, wide, name):
+    kernel = functools.partial(block_kernel, start)
+    outs = [shape((left.shape[0], wide))] * NEAR
+    return run(kernel, name, outs, [SMEM, VMEM] + [VMEM] * len(rights), near_arr, left, *rights)
+
+
+def near_swap(blocks, order):
+    got = {0: blocks[0]}
+    for k in order:
+        got[k] = swap(blocks[k], k)
+    return [got[k] for k in range(NEAR)]
+
+
+def near_gather(parts, order):
+    got = [near_swap([part] * NEAR, order) for part in parts]
     return [cut[k] for k in range(NEAR) for cut in got]
 
 
@@ -288,11 +312,8 @@
     return [matrix[:, i * width : (i + 1) * width] for i in range(cuts)]
 
 
-def near_scatter(blocks):
-    total = blocks[0].astype(f32)
-    for k in (3, 1, 2):
-        total = total + swap(blocks[k], k).astype(f32)
-    return total
+def near_scatter(blocks, order):
+    return sum(block.astype(f32) for block in near_swap(blocks, order))
 
 
 def far_sum(block, far_size):
@@ -344,13 +365,14 @@
             pltpu.SemaphoreType.DMA((2,)),
         ],
     )
-    key_w, value_w, query_w, output_w, done = load(
-        (key_weight, value_matrix, query_weight, output_weight), parts[0], "load_qkvo"
-    )
+    side_by_side = key_weight.shape[1] % 128 == 0
+    kv_weights = ((key_weight, value_matrix),) if side_by_side else (key_weight, value_matrix)
+    *kv_parts, query_w, output_w, done = load((*kv_weights, query_weight, output_weight), parts[0], "load_qkvo")
+    kv_w = kv_parts[0] if side_by_side else jnp.concatenate(kv_parts, axis=1)
 
     cuts = FRONT_CUTS
     wide = quarter // cuts
-    near_parts = [parts[0]] + [swap(parts[k], k) for k in (1, 2, 3)]
+    near_parts = near_swap(parts, PICK_ORDER)
     half_slots = NEAR * MOST
     all_rows, index_rows = [], []
     for cut in range(cuts):
@@ -382,7 +404,7 @@
     select = select.astype(bf16)
     row_parts = [dot(select, piece).astype(bf16) for piece in all_rows]
     up_w, done = load((up_weight,), row_parts[0], "load_up")
-    row_blocks = near_gather(row_parts)
+    row_blocks = near_gather(row_parts, ROWS_ORDER)
     rows_quarter = jnp.concatenate(row_parts, axis=1)
 
     half_dim = HEAD_SIZE // 2
@@ -404,25 +426,22 @@
     column = comp_id * KEY_VALUE_HEADS + target * heads_here // group_width
     col_id = jnp.arange(key_weight.shape[1], dtype=i32)
     place = column[:, None] == col_id[None, :]
-    place_k = (place & (is_value == 0)[:, None]).astype(bf16)
-    place_v = (place & (is_value == 1)[:, None]).astype(bf16)
+    place = jnp.concatenate([place & (is_value == part)[:, None] for part in (0, 1)], axis=1).astype(bf16)
     rows_normed, *sends = run(
         kv_kernel,
         "keys_values",
         [shape((count, width))] + [shape((total_rows // NEAR, count))] * NEAR,
-        [SMEM] + [VMEM] * 5 + [ANY] + [VMEM] * len(row_blocks),
+        [SMEM] + [VMEM] * 3 + [ANY] + [VMEM] * len(row_blocks),
         near_arr,
         attn_gain,
-        key_w,
-        value_w,
-        place_k,
-        place_v,
+        kv_w,
+        place,
         done,
         *row_blocks,
         limit=kernel_mib,
     )
     down_half = down_weight.shape[0] // 2
-    got = [sends[0]] + [swap(sends[k], k) for k in (1, 2, 3)]
+    got = near_swap(sends, KEYS_ORDER)
     raw_q = run(
         matmul_kernel, "query", shape((count, heads_here * HEAD_SIZE), f32), [VMEM, VMEM], rows_normed, query_w
     )
@@ -456,18 +475,17 @@
 
     cuts = ATTN_CUTS
     attn_near = [
-        near_scatter(column_blocks(near_arr, heads, (output_w,), cuts, cut, "attn_out")).astype(bf16) for cut in range(cuts)
+        near_scatter(column_blocks(near_arr, heads, (output_w,), cut * (quarter // cuts), quarter // cuts, "attn_out"), ATTN_ORDER).astype(bf16) for cut in range(cuts)
     ]
     attn_parts = [far_sum(part, far_size) for part in attn_near]
     mixed_parts = [
         (rows.astype(f32) + part).astype(bf16) for rows, part in zip(cut_cols(rows_quarter, cuts), attn_parts)
     ]
-    attn_quarter = jnp.concatenate(attn_parts, axis=1).astype(bf16)
     units = gate_weight.shape[1]
     rows_scratch = pltpu.VMEM((count, width // cuts), bf16)
     weights = (near_arr, ffn_gain, in_vmem(gate_w), in_vmem(up_w))
     specs = [SMEM] + [VMEM] * (3 + NEAR)
-    first_blocks, last_blocks = (near_gather([part]) for part in mixed_parts)
+    first_blocks, last_blocks = (near_gather([part], MIXED_ORDER) for part in mixed_parts)
     *sums, down_a = run(
         functools.partial(hidden_part_kernel, cuts, 0),
         "hidden_part",
@@ -492,18 +510,21 @@
         limit=kernel_mib,
     )
 
-    cuts = BACK_CUTS
+    attn_quarter = jnp.concatenate(attn_parts, axis=1).astype(bf16)
     spread = select.reshape(count, far_size, NEAR * MOST)
     deltas = []
-    for cut, attn_part in enumerate(cut_cols(attn_quarter, cuts)):
-        blocks = column_blocks(near_arr, hidden, (in_vmem(down_a), in_vmem(down_b)), cuts, cut, "ffn_out")
-        ffn_part = near_scatter(blocks).astype(bf16)
-        delta = dot_tn(spread[:, 0], ffn_part) + dot_tn(spread[:, 0], attn_part)
+    for cut in range(cuts):
+        start, stop = cut * (quarter // cuts), (cut + 1) * (quarter // cuts)
+        blocks = column_blocks(
+            near_arr, hidden, (in_vmem(down_a), in_vmem(down_b)), start, stop - start, "ffn_out"
+        )
+        ffn_part = near_scatter(blocks, FFN_ORDER).astype(bf16)
+        delta = dot_tn(spread[:, 0], ffn_part) + dot_tn(spread[:, 0], attn_quarter[:, start:stop])
         for k in range(1, far_size):
             delta = delta + swap(dot_tn(spread[:, k], ffn_part).astype(bf16), far_mask(k)).astype(f32)
         deltas.append(delta.astype(bf16))
     delta = jnp.concatenate(deltas, axis=1).reshape(NEAR, MOST, quarter)
-    back = [delta[0]] + [swap(delta[k], k) for k in (1, 2, 3)]
+    back = near_swap(delta, BACK_ORDER)
     return pl.pallas_call(
         put_kernel,
         in_specs=[SMEM] + [VMEM] * (3 + NEAR),

time: 115 us -> 114 us (level)
  waiting for transfers between devices: 22 us -> 17.9 us
  starting transfers between devices: 57.9 us -> 61.6 us
    ppermute x40, waiting for transfers between devices: 22 us -> 17.9 us  [swap(): return lax.ppermute(value, 'ctx', [(i, i ^ mask) for i in range(size)])]
    ppermute x40, starting transfers between devices: 57.9 us -> 61.6 us  [swap(): return lax.ppermute(value, 'ctx', [(i, i ^ mask) for i in range(size)])]
  transfers between devices with their start and end apart: 40 -> 40, of which waited for: 20 -> 18; matrix products, arithmetic and copies ran while one was open for 3% -> 3% of each run, Pallas kernels for 19% -> 19%
where the time goes in v6:
time: 114 us; the launch traced here: 113 us
  starting transfers between devices  61.6 us (54%)
  Pallas kernels  29.9 us (26%)
  waiting for transfers between devices  17.9 us (16%)
  matrix products  1.77 us (2%)
  other arithmetic  1.73 us (2%)
    ppermute x40, starting transfers between devices, swap(): return lax.ppermute(value, 'ctx', [(i, i ^ mask) for i in range(size)])  61.6 us
    ppermute x40, waiting for transfers between devices, swap(): return lax.ppermute(value, 'ctx', [(i, i ^ mask) for i in range(size)])  17.9 us
    pallas_call x4, Pallas kernels, load(): pl.pallas_call(kernel, in_specs=[HBM] * len(flat) + [ANY], out_specs=[VME...  15.3 us
    pallas_call x12, Pallas kernels, run(): pl.pallas_call(kernel, in_specs=specs, out_specs=outs, out_shape=out_shap...  13.2 us
  transfers between devices with their start and end apart: 40, of which 18 were waited for; matrix products, arithmetic and copies ran while one was open for 3% of the time, Pallas kernels for 19%

profile of v6, /device:TPU:0, one launch (start us, length us, event | category | flops | bytes accessed | tf_op | source)
XLA Modules:
  0.0 113.5 jit_solution(7319618923901369240)
XLA Ops:
  0.0 1.5 %pick.1 = (bf16[32,1152]{1,0:T(8,128)(2,1)S(1)}, bf16[32,1152]{1,0:T(8,128)(2,1)S(1)}, bf16[32,1152]{1,0:T(8,128)(2,1)S(1)}, bf16[32,1152]{1,0:T(8,128)(2,1)S(1)}) custom-call(s32[1]{0:T(128)} %bitcast.near, s32[1,128]{1,0:T(1,128)} %bitcast.29, bf16[128,4096]{1,0:T(8,128)(2,1)} %tokens.1), custom_call_target="tpu_custom_call" | custom-call | tf_op jit(solution)/shard_map/pick/pallas_call | solution.py:77
  1.6 3.0 %collective-permute-start = (bf16[32,1152]{1,0:T(8,128)(2,1)S(1)}, bf16[32,1152]{1,0:T(8,128)(2,1)S(1)}, u32[]{:S(2)}, u32[]{:S(2)}) collective-permute-start(bf16[32,1152]{1,0:T(8,128)(2,1)S(1)} %get-tuple-element.46), channel_id=1, source_target_pairs={{0,1},{1,0},{2,3},{3,2},{4,5},{5,4},{6,7},{7,6},{8,9},{9,8},{10,11... | collective-permute-start | bytes 221192 | tf_op jit(solution)/shard_map/ppermute | solution.py:44
  4.6 1.6 %collective-permute-start.1 = (bf16[32,1152]{1,0:T(8,128)(2,1)S(1)}, bf16[32,1152]{1,0:T(8,128)(2,1)S(1)}, u32[]{:S(2)}, u32[]{:S(2)}) collective-permute-start(bf16[32,1152]{1,0:T(8,128)(2,1)S(1)} %get-tuple-element.47), channel_id=1, source_target_pairs={{0,2},{1,3},{2,0},{3,1},{4,6},{5,7},{6,4},{7,5},{8,10},{9,11},{10,... | collective-permute-start | bytes 221192 | tf_op jit(solution)/shard_map/ppermute | solution.py:44
  6.4 4.1 %load_qkvo.1 = (bf16[4096,256]{1,0:T(8,128)(2,1)S(1)}, bf16[4096,512]{1,0:T(8,128)(2,1)S(1)}, bf16[512,4096]{1,0:T(8,128)(2,1)S(1)}, s32[8,128]{1,0:T(8,128)S(1)}) custom-call(bf16[4096,128]{1,0:T(8,128)(2,1)} %refs_0_.4, bf16[4096,128]{1,0:T(8,128)(2,1)} %refs_1_.1, bf16[4096,512]{1,0:T(8,128)(2,1)} %refs_2_.1, bf16[512,4096]{1,0:T(8,128)(2,1)} %refs_3_.1, ...), custom_call_target="tpu_custom_call" | custom-call | tf_op jit(solution)/shard_map/load_qkvo/pallas_call | solution.py:113
  11.5 3.2 %collective-permute-start.3 = (bf16[144,512]{1,0:T(8,128)(2,1)S(1)}, bf16[144,512]{1,0:T(8,128)(2,1)S(1)}, u32[]{:S(2)}, u32[]{:S(2)}) collective-permute-start(bf16[144,512]{1,0:T(8,128)(2,1)S(1)} %pack.2.refs_1_), channel_id=1, source_target_pairs={{0,6},{1,7},{2,4},{3,5},{4,2},{5,3},{6,0},{7,1},{8,14},{9,15},{10,... | collective-permute-start | bytes 442376 | tf_op jit(solution)/shard_map/ppermute | solution.py:44
  14.7 4.3 %load_gate.1 = (bf16[4096,1408]{1,0:T(8,128)(2,1)S(1)}, s32[8,128]{1,0:T(8,128)S(1)}) custom-call(bf16[4096,1408]{1,0:T(8,128)(2,1)} %refs_0_.5, bf16[144,512]{1,0:T(8,128)(2,1)S(1)} %pack.2.refs_1_), custom_call_target="tpu_custom_call" | custom-call | tf_op jit(solution)/shard_map/load_gate/pallas_call | solution.py:113
  20.1 3.9 %collective-permute-start.9 = (bf16[128,512]{1,0:T(8,128)(2,1)S(1)}, bf16[128,512]{1,0:T(8,128)(2,1)S(1)}, u32[]{:S(2)}, u32[]{:S(2)}) collective-permute-start(bf16[128,512]{1,0:T(8,128)(2,1)S(1)} %convolution_convert_fusion.3.refs_1_.refs_0_), channel_id=1, source_target_pairs={{0,3},{1,2},{2,1},{3,0},{4,7},{5,6},{6,5},{7,4},{8,11},{9,10},{10,... | collective-permute-start | bytes 393224 | tf_op jit(solution)/shard_map/ppermute | solution.py:44
  25.3 2.0 %collective-permute-done.4 = bf16[128,512]{1,0:T(8,128)(2,1)S(1)} collective-permute-done((bf16[128,512]{1,0:T(8,128)(2,1)S(1)}, bf16[128,512]{1,0:T(8,128)(2,1)S(1)}, u32[]{:S(2)}, u32[]{:S(2)}) %collective-permute-start.4) | collective-permute-done | bytes 131104 | tf_op jit(solution)/shard_map/ppermute | solution.py:44
  28.4 2.1 %collective-permute-start.8 = (bf16[128,512]{1,0:T(8,128)(2,1)S(1)}, bf16[128,512]{1,0:T(8,128)(2,1)S(1)}, u32[]{:S(2)}, u32[]{:S(2)}) collective-permute-start(bf16[128,512]{1,0:T(8,128)(2,1)S(1)} %convolution_convert_fusion.2.refs_1_), channel_id=1, source_target_pairs={{0,2},{1,3},{2,0},{3,1},{4,6},{5,7},{6,4},{7,5},{8,10},{9,11},{10,... | collective-permute-start | bytes 393224 | tf_op jit(solution)/shard_map/ppermute | solution.py:44
  31.3 4.3 %load_up.1 = (bf16[4096,1408]{1,0:T(8,128)(2,1)S(1)}, s32[8,128]{1,0:T(8,128)S(1)}) custom-call(bf16[4096,1408]{1,0:T(8,128)(2,1)} %refs_0_.6, bf16[128,512]{1,0:T(8,128)(2,1)S(1)} %convolution_convert_fusion.3.refs_1_.refs_0_), custom_call_target="tpu_custom_call" | custom-call | tf_op jit(solution)/shard_map/load_up/pallas_call | solution.py:113
  38.8 2.0 %collective-permute-start.13 = (bf16[64,128]{1,0:T(8,128)(2,1)S(1)}, bf16[64,128]{1,0:T(8,128)(2,1)S(1)}, u32[]{:S(2)}, u32[]{:S(2)}) collective-permute-start(bf16[64,128]{1,0:T(8,128)(2,1)S(1)} %get-tuple-element.59), channel_id=1, source_target_pairs={{0,3},{1,2},{2,1},{3,0},{4,7},{5,6},{6,5},{7,4},{8,11},{9,10},{10,... | collective-permute-start | bytes 49160 | tf_op jit(solution)/shard_map/ppermute | solution.py:44
  43.5 2.7 %collective-permute-start.14 = (bf16[128,128]{1,0:T(8,128)(2,1)S(1)}, bf16[128,128]{1,0:T(8,128)(2,1)S(1)}, u32[]{:S(2)}, u32[]{:S(2)}) collective-permute-start(bf16[128,128]{1,0:T(8,128)(2,1)S(1)} %pad_maximum_fusion.3), channel_id=1, source_target_pairs={{0,4},{1,5},{2,6},{3,7},{4,0},{5,1},{6,2},{7,3},{8,12},{9,13},{10,... | collective-permute-start | bytes 98312 | tf_op jit(solution)/shard_map/ppermute | solution.py:44
  46.2 2.6 %load_down.1 = (bf16[704,4096]{1,0:T(8,128)(2,1)S(1)}, s32[8,128]{1,0:T(8,128)S(1)}) custom-call(bf16[1408,4096]{1,0:T(8,128)(2,1)} %refs_4_.1, bf16[128,128]{1,0:T(8,128)(2,1)S(1)} %pad_maximum_fusion.4.refs_1_), custom_call_target="tpu_custom_call" | custom-call | tf_op jit(solution)/shard_map/load_down/pallas_call | solution.py:113
  51.1 1.9 %collective-permute-start.23 = (bf16[128,512]{1,0:T(8,128)(2,1)S(1)}, bf16[128,512]{1,0:T(8,128)(2,1)S(1)}, u32[]{:S(2)}, u32[]{:S(2)}) collective-permute-start(bf16[128,512]{1,0:T(8,128)(2,1)S(1)} %get-tuple-element.68), channel_id=1, source_target_pairs={{0,2},{1,3},{2,0},{3,1},{4,6},{5,7},{6,4},{7,5},{8,10},{9,11},{10,... | collective-permute-start | bytes 393224 | tf_op jit(solution)/shard_map/ppermute | solution.py:44
  55.1 1.9 %collective-permute-start.16 = (bf16[128,512]{1,0:T(8,128)(2,1)S(1)}, bf16[128,512]{1,0:T(8,128)(2,1)S(1)}, u32[]{:S(2)}, u32[]{:S(2)}) collective-permute-start(bf16[128,512]{1,0:T(8,128)(2,1)S(1)} %get-tuple-element.64), channel_id=1, source_target_pairs={{0,2},{1,3},{2,0},{3,1},{4,6},{5,7},{6,4},{7,5},{8,10},{9,11},{10,... | collective-permute-start | bytes 393224 | tf_op jit(solution)/shard_map/ppermute | solution.py:44
  57.0 1.8 %collective-permute-start.17 = (bf16[128,512]{1,0:T(8,128)(2,1)S(1)}, bf16[128,512]{1,0:T(8,128)(2,1)S(1)}, u32[]{:S(2)}, u32[]{:S(2)}) collective-permute-start(bf16[128,512]{1,0:T(8,128)(2,1)S(1)} %get-tuple-element.65), channel_id=1, source_target_pairs={{0,3},{1,2},{2,1},{3,0},{4,7},{5,6},{6,5},{7,4},{8,11},{9,10},{10,... | collective-permute-start | bytes 393224 | tf_op jit(solution)/shard_map/ppermute | solution.py:44
  59.8 3.8 %collective-permute-start.25 = (bf16[128,512]{1,0:T(8,128)(2,1)S(1)}, bf16[128,512]{1,0:T(8,128)(2,1)S(1)}, u32[]{:S(2)}, u32[]{:S(2)}) collective-permute-start(bf16[128,512]{1,0:T(8,128)(2,1)S(1)} %add_convert_fusion.3), channel_id=1, source_target_pairs={{0,6},{1,7},{2,4},{3,5},{4,2},{5,3},{6,0},{7,1},{8,14},{9,15},{10,... | collective-permute-start | bytes 393224 | tf_op jit(solution)/shard_map/ppermute | solution.py:44
  63.9 4.9 %collective-permute-start.18 = (bf16[128,512]{1,0:T(8,128)(2,1)S(1)}, bf16[128,512]{1,0:T(8,128)(2,1)S(1)}, u32[]{:S(2)}, u32[]{:S(2)}) collective-permute-start(bf16[128,512]{1,0:T(8,128)(2,1)S(1)} %add_convert_fusion.5), channel_id=1, source_target_pairs={{0,6},{1,7},{2,4},{3,5},{4,2},{5,3},{6,0},{7,1},{8,14},{9,15},{10,... | collective-permute-start | bytes 393224 | tf_op jit(solution)/shard_map/ppermute | solution.py:44
  71.1 2.7 %collective-permute-start.26 = (bf16[128,512]{1,0:T(8,128)(2,1)S(1)}, bf16[128,512]{1,0:T(8,128)(2,1)S(1)}, u32[]{:S(2)}, u32[]{:S(2)}) collective-permute-start(bf16[128,512]{1,0:T(8,128)(2,1)S(1)} %add_convert_fusion.2.refs_0_), channel_id=1, source_target_pairs={{0,1},{1,0},{2,3},{3,2},{4,5},{5,4},{6,7},{7,6},{8,9},{9,8},{10,11... | collective-permute-start | bytes 393224 | tf_op jit(solution)/shard_map/ppermute | solution.py:44
  74.0 2.1 %collective-permute-start.20 = (bf16[128,512]{1,0:T(8,128)(2,1)S(1)}, bf16[128,512]{1,0:T(8,128)(2,1)S(1)}, u32[]{:S(2)}, u32[]{:S(2)}) collective-permute-start(bf16[128,512]{1,0:T(8,128)(2,1)S(1)} %add_convert_fusion.4.refs_0_), channel_id=1, source_target_pairs={{0,2},{1,3},{2,0},{3,1},{4,6},{5,7},{6,4},{7,5},{8,10},{9,11},{10,... | collective-permute-start | bytes 393224 | tf_op jit(solution)/shard_map/ppermute | solution.py:44
  77.6 3.7 %hidden_part.1 = (f32[128,1408]{1,0:T(8,128)S(1)}, f32[128,1408]{1,0:T(8,128)S(1)}, f32[128,128]{1,0:T(8,128)S(1)}, bf16[704,4096]{1,0:T(8,128)(2,1)S(1)}) custom-call(s32[1]{0:T(128)} %bitcast.near, f32[1,4096]{1,0:T(1,128)S(1)} %bitcast.26, bf16[4096,1408]{1,0:T(8,128)(2,1)S(1)} %get-tuple-element.49.gate, bf16[4096,1408]{1,0:T(8,128)(2,1)S(1)} %get-tuple-element.50.up, ...), custom_call_target="tpu_custom_call" | custom-call | tf_op jit(solution)/shard_map/hidden_part/pallas_call | solution.py:77
  82.5 2.0 %hidden.1.left = bf16[128,1408]{1,0:T(8,128)(2,1)S(1)} custom-call(s32[1]{0:T(128)} %bitcast.near, f32[1,4096]{1,0:T(1,128)S(1)} %bitcast.27, bf16[4096,1408]{1,0:T(8,128)(2,1)S(1)} %get-tuple-element.49.gate, bf16[4096,1408]{1,0:T(8,128)(2,1)S(1)} %get-tuple-element.50.up, bf16[128,512]{1,0:T(8,128)(2,1)S(1)} %add_convert_fusion.4.refs_0_, ...), custom_call_target="tpu_custom_call" | custom-call | tf_op jit(solution)/shard_map/hidden/pallas_call | solution.py:77
  86.8 2.4 %collective-permute-start.35 = (bf16[128,512]{1,0:T(8,128)(2,1)S(1)}, bf16[128,512]{1,0:T(8,128)(2,1)S(1)}, u32[]{:S(2)}, u32[]{:S(2)}) collective-permute-start(bf16[128,512]{1,0:T(8,128)(2,1)S(1)} %get-tuple-element.82), channel_id=1, source_target_pairs={{0,3},{1,2},{2,1},{3,0},{4,7},{5,6},{6,5},{7,4},{8,11},{9,10},{10,... | collective-permute-start | bytes 393224 | tf_op jit(solution)/shard_map/ppermute | solution.py:44
  91.7 2.4 %collective-permute-start.31 = (bf16[128,512]{1,0:T(8,128)(2,1)S(1)}, bf16[128,512]{1,0:T(8,128)(2,1)S(1)}, u32[]{:S(2)}, u32[]{:S(2)}) collective-permute-start(bf16[128,512]{1,0:T(8,128)(2,1)S(1)} %get-tuple-element.78), channel_id=1, source_target_pairs={{0,3},{1,2},{2,1},{3,0},{4,7},{5,6},{6,5},{7,4},{8,11},{9,10},{10,... | collective-permute-start | bytes 393224 | tf_op jit(solution)/shard_map/ppermute | solution.py:44
  95.3 1.8 %collective-permute-start.36 = (bf16[128,512]{1,0:T(8,128)(2,1)S(1)}, bf16[128,512]{1,0:T(8,128)(2,1)S(1)}, u32[]{:S(2)}, u32[]{:S(2)}) collective-permute-start(bf16[128,512]{1,0:T(8,128)(2,1)S(1)} %convolution_convert_fusion), channel_id=1, source_target_pairs={{0,6},{1,7},{2,4},{3,5},{4,2},{5,3},{6,0},{7,1},{8,14},{9,15},{10,... | collective-permute-start | bytes 393224 | tf_op jit(solution)/shard_map/ppermute | solution.py:44
  97.1 1.6 %collective-permute-done.31 = bf16[128,512]{1,0:T(8,128)(2,1)S(1)} collective-permute-done((bf16[128,512]{1,0:T(8,128)(2,1)S(1)}, bf16[128,512]{1,0:T(8,128)(2,1)S(1)}, u32[]{:S(2)}, u32[]{:S(2)}) %collective-permute-start.31) | collective-permute-done | bytes 131104 | tf_op jit(solution)/shard_map/ppermute | solution.py:44
  99.0 2.6 %collective-permute-start.32 = (bf16[128,512]{1,0:T(8,128)(2,1)S(1)}, bf16[128,512]{1,0:T(8,128)(2,1)S(1)}, u32[]{:S(2)}, u32[]{:S(2)}) collective-permute-start(bf16[128,512]{1,0:T(8,128)(2,1)S(1)} %convolution_convert_fusion.1), channel_id=1, source_target_pairs={{0,6},{1,7},{2,4},{3,5},{4,2},{5,3},{6,0},{7,1},{8,14},{9,15},{10,... | collective-permute-start | bytes 393224 | tf_op jit(solution)/shard_map/ppermute | solution.py:44
  102.4 3.4 %collective-permute-done.32 = bf16[128,512]{1,0:T(8,128)(2,1)S(1)} collective-permute-done((bf16[128,512]{1,0:T(8,128)(2,1)S(1)}, bf16[128,512]{1,0:T(8,128)(2,1)S(1)}, u32[]{:S(2)}, u32[]{:S(2)}) %collective-permute-start.32) | collective-permute-done | bytes 131104 | tf_op jit(solution)/shard_map/ppermute | solution.py:44
  106.1 1.6 %collective-permute-start.39 = (bf16[32,1024]{1,0:T(8,128)(2,1)S(1)}, bf16[32,1024]{1,0:T(8,128)(2,1)S(1)}, u32[]{:S(2)}, u32[]{:S(2)}) collective-permute-start(bf16[32,1024]{1,0:T(8,128)(2,1)S(1)} %get-tuple-element.85), channel_id=1, source_target_pairs={{0,3},{1,2},{2,1},{3,0},{4,7},{5,6},{6,5},{7,4},{8,11},{9,10},{10,... | collective-permute-start | bytes 196616 | tf_op jit(solution)/shard_map/ppermute | solution.py:44
  107.7 2.0 %collective-permute-start.38 = (bf16[32,1024]{1,0:T(8,128)(2,1)S(1)}, bf16[32,1024]{1,0:T(8,128)(2,1)S(1)}, u32[]{:S(2)}, u32[]{:S(2)}) collective-permute-start(bf16[32,1024]{1,0:T(8,128)(2,1)S(1)} %get-tuple-element.88), channel_id=1, source_target_pairs={{0,2},{1,3},{2,0},{3,1},{4,6},{5,7},{6,4},{7,5},{8,10},{9,11},{10,... | collective-permute-start | bytes 196616 | tf_op jit(solution)/shard_map/ppermute | solution.py:44
  109.7 1.7 %collective-permute-done.39.refs_3_ = bf16[32,1024]{1,0:T(8,128)(2,1)S(1)} collective-permute-done((bf16[32,1024]{1,0:T(8,128)(2,1)S(1)}, bf16[32,1024]{1,0:T(8,128)(2,1)S(1)}, u32[]{:S(2)}, u32[]{:S(2)}) %collective-permute-start.39) | collective-permute-done | bytes 65568 | tf_op jit(solution)/shard_map/ppermute | solution.py:44
  112.0 1.4 %put.1 = bf16[128,4096]{1,0:T(8,128)(2,1)} custom-call(s32[1]{0:T(128)} %bitcast.near, s32[1,128]{1,0:T(1,128)S(1)} %bitcast.30, bf16[1,128]{1,0:T(2,128)(2,1)S(1)} %bitcast.31, bf16[128,4096]{1,0:T(8,128)(2,1)S(1)} %copy-done, bf16[32,1024]{1,0:T(8,128)(2,1)S(1)} %get-tuple-element.86.refs_0_, bf16[32,1024]{1,0:T(8,128)(2,1)S(1)} %collective-permute-done.37.refs_1_, ...), custom_call_target="tpu_custom_call" | custom-call | tf_op jit(solution)/shard_map/put/pallas_call | solution.py:528
  (120 shorter events, 30.2 us)
Async XLA Ops:
  1.6 9.0 %collective-permute-start = (bf16[32,1152]{1,0:T(8,128)(2,1)S(1)}, bf16[32,1152]{1,0:T(8,128)(2,1)S(1)}, u32[]{:S(2)}, u32[]{:S(2)}) collective-permute-start(bf16[32,1152]{1,0:T(8,128)(2,1)S(1)} %get-tuple-element.46), channel_id=1, source_target_pairs={{0,1},{1,0},{2,3},{3,2},{4,5},{5,4},{6,7},{7,6},{8,9},{9,8},{10,11... | collective-permute-start | bytes 221192 | tf_op jit(solution)/shard_map/ppermute | solution.py:44
  4.6 6.0 %collective-permute-start.1 = (bf16[32,1152]{1,0:T(8,128)(2,1)S(1)}, bf16[32,1152]{1,0:T(8,128)(2,1)S(1)}, u32[]{:S(2)}, u32[]{:S(2)}) collective-permute-start(bf16[32,1152]{1,0:T(8,128)(2,1)S(1)} %get-tuple-element.47), channel_id=1, source_target_pairs={{0,2},{1,3},{2,0},{3,1},{4,6},{5,7},{6,4},{7,5},{8,10},{9,11},{10,... | collective-permute-start | bytes 221192 | tf_op jit(solution)/shard_map/ppermute | solution.py:44
  11.5 8.3 %collective-permute-start.3 = (bf16[144,512]{1,0:T(8,128)(2,1)S(1)}, bf16[144,512]{1,0:T(8,128)(2,1)S(1)}, u32[]{:S(2)}, u32[]{:S(2)}) collective-permute-start(bf16[144,512]{1,0:T(8,128)(2,1)S(1)} %pack.2.refs_1_), channel_id=1, source_target_pairs={{0,6},{1,7},{2,4},{3,5},{4,2},{5,3},{6,0},{7,1},{8,14},{9,15},{10,... | collective-permute-start | bytes 442376 | tf_op jit(solution)/shard_map/ppermute | solution.py:44
  19.0 8.3 %collective-permute-start.4 = (bf16[128,512]{1,0:T(8,128)(2,1)S(1)}, bf16[128,512]{1,0:T(8,128)(2,1)S(1)}, u32[]{:S(2)}, u32[]{:S(2)}) collective-permute-start(bf16[128,512]{1,0:T(8,128)(2,1)S(1)} %pack.3), channel_id=1, source_target_pairs={{0,6},{1,7},{2,4},{3,5},{4,2},{5,3},{6,0},{7,1},{8,14},{9,15},{10,... | collective-permute-start | bytes 393224 | tf_op jit(solution)/shard_map/ppermute | solution.py:44
  20.1 10.4 %collective-permute-start.9 = (bf16[128,512]{1,0:T(8,128)(2,1)S(1)}, bf16[128,512]{1,0:T(8,128)(2,1)S(1)}, u32[]{:S(2)}, u32[]{:S(2)}) collective-permute-start(bf16[128,512]{1,0:T(8,128)(2,1)S(1)} %convolution_convert_fusion.3.refs_1_.refs_0_), channel_id=1, source_target_pairs={{0,3},{1,2},{2,1},{3,0},{4,7},{5,6},{6,5},{7,4},{8,11},{9,10},{10,... | collective-permute-start | bytes 393224 | tf_op jit(solution)/shard_map/ppermute | solution.py:44
  24.0 11.7 %collective-permute-start.7 = (bf16[128,512]{1,0:T(8,128)(2,1)S(1)}, bf16[128,512]{1,0:T(8,128)(2,1)S(1)}, u32[]{:S(2)}, u32[]{:S(2)}) collective-permute-start(bf16[128,512]{1,0:T(8,128)(2,1)S(1)} %convolution_convert_fusion.3.refs_1_.refs_0_), channel_id=1, source_target_pairs={{0,2},{1,3},{2,0},{3,1},{4,6},{5,7},{6,4},{7,5},{8,10},{9,11},{10,... | collective-permute-start | bytes 393224 | tf_op jit(solution)/shard_map/ppermute | solution.py:44
  24.0 11.7 %collective-permute-start.5 = (bf16[128,512]{1,0:T(8,128)(2,1)S(1)}, bf16[128,512]{1,0:T(8,128)(2,1)S(1)}, u32[]{:S(2)}, u32[]{:S(2)}) collective-permute-start(bf16[128,512]{1,0:T(8,128)(2,1)S(1)} %convolution_convert_fusion.3.refs_1_.refs_0_), channel_id=1, source_target_pairs={{0,1},{1,0},{2,3},{3,2},{4,5},{5,4},{6,7},{7,6},{8,9},{9,8},{10,11... | collective-permute-start | bytes 393224 | tf_op jit(solution)/shard_map/ppermute | solution.py:44
  27.5 8.2 %collective-permute-start.10 = (bf16[128,512]{1,0:T(8,128)(2,1)S(1)}, bf16[128,512]{1,0:T(8,128)(2,1)S(1)}, u32[]{:S(2)}, u32[]{:S(2)}) collective-permute-start(bf16[128,512]{1,0:T(8,128)(2,1)S(1)} %convolution_convert_fusion.2.refs_1_), channel_id=1, source_target_pairs={{0,3},{1,2},{2,1},{3,0},{4,7},{5,6},{6,5},{7,4},{8,11},{9,10},{10,... | collective-permute-start | bytes 393224 | tf_op jit(solution)/shard_map/ppermute | solution.py:44
  28.4 7.5 %collective-permute-start.8 = (bf16[128,512]{1,0:T(8,128)(2,1)S(1)}, bf16[128,512]{1,0:T(8,128)(2,1)S(1)}, u32[]{:S(2)}, u32[]{:S(2)}) collective-permute-start(bf16[128,512]{1,0:T(8,128)(2,1)S(1)} %convolution_convert_fusion.2.refs_1_), channel_id=1, source_target_pairs={{0,2},{1,3},{2,0},{3,1},{4,6},{5,7},{6,4},{7,5},{8,10},{9,11},{10,... | collective-permute-start | bytes 393224 | tf_op jit(solution)/shard_map/ppermute | solution.py:44
  30.6 5.4 %collective-permute-start.6 = (bf16[128,512]{1,0:T(8,128)(2,1)S(1)}, bf16[128,512]{1,0:T(8,128)(2,1)S(1)}, u32[]{:S(2)}, u32[]{:S(2)}) collective-permute-start(bf16[128,512]{1,0:T(8,128)(2,1)S(1)} %convolution_convert_fusion.2.refs_1_), channel_id=1, source_target_pairs={{0,1},{1,0},{2,3},{3,2},{4,5},{5,4},{6,7},{7,6},{8,9},{9,8},{10,11... | collective-permute-start | bytes 393224 | tf_op jit(solution)/shard_map/ppermute | solution.py:44
  50.3 6.7 %collective-permute-start.22 = (bf16[128,512]{1,0:T(8,128)(2,1)S(1)}, bf16[128,512]{1,0:T(8,128)(2,1)S(1)}, u32[]{:S(2)}, u32[]{:S(2)}) collective-permute-start(bf16[128,512]{1,0:T(8,128)(2,1)S(1)} %get-tuple-element.67), channel_id=1, source_target_pairs={{0,1},{1,0},{2,3},{3,2},{4,5},{5,4},{6,7},{7,6},{8,9},{9,8},{10,11... | collective-permute-start | bytes 393224 | tf_op jit(solution)/shard_map/ppermute | solution.py:44
  51.1 7.7 %collective-permute-start.23 = (bf16[128,512]{1,0:T(8,128)(2,1)S(1)}, bf16[128,512]{1,0:T(8,128)(2,1)S(1)}, u32[]{:S(2)}, u32[]{:S(2)}) collective-permute-start(bf16[128,512]{1,0:T(8,128)(2,1)S(1)} %get-tuple-element.68), channel_id=1, source_target_pairs={{0,2},{1,3},{2,0},{3,1},{4,6},{5,7},{6,4},{7,5},{8,10},{9,11},{10,... | collective-permute-start | bytes 393224 | tf_op jit(solution)/shard_map/ppermute | solution.py:44
  53.0 6.8 %collective-permute-start.24 = (bf16[128,512]{1,0:T(8,128)(2,1)S(1)}, bf16[128,512]{1,0:T(8,128)(2,1)S(1)}, u32[]{:S(2)}, u32[]{:S(2)}) collective-permute-start(bf16[128,512]{1,0:T(8,128)(2,1)S(1)} %get-tuple-element.69), channel_id=1, source_target_pairs={{0,3},{1,2},{2,1},{3,0},{4,7},{5,6},{6,5},{7,4},{8,11},{9,10},{10,... | collective-permute-start | bytes 393224 | tf_op jit(solution)/shard_map/ppermute | solution.py:44
  54.3 9.2 %collective-permute-start.15 = (bf16[128,512]{1,0:T(8,128)(2,1)S(1)}, bf16[128,512]{1,0:T(8,128)(2,1)S(1)}, u32[]{:S(2)}, u32[]{:S(2)}) collective-permute-start(bf16[128,512]{1,0:T(8,128)(2,1)S(1)} %get-tuple-element.63), channel_id=1, source_target_pairs={{0,1},{1,0},{2,3},{3,2},{4,5},{5,4},{6,7},{7,6},{8,9},{9,8},{10,11... | collective-permute-start | bytes 393224 | tf_op jit(solution)/shard_map/ppermute | solution.py:44
  55.1 8.5 %collective-permute-start.16 = (bf16[128,512]{1,0:T(8,128)(2,1)S(1)}, bf16[128,512]{1,0:T(8,128)(2,1)S(1)}, u32[]{:S(2)}, u32[]{:S(2)}) collective-permute-start(bf16[128,512]{1,0:T(8,128)(2,1)S(1)} %get-tuple-element.64), channel_id=1, source_target_pairs={{0,2},{1,3},{2,0},{3,1},{4,6},{5,7},{6,4},{7,5},{8,10},{9,11},{10,... | collective-permute-start | bytes 393224 | tf_op jit(solution)/shard_map/ppermute | solution.py:44
  57.0 6.8 %collective-permute-start.17 = (bf16[128,512]{1,0:T(8,128)(2,1)S(1)}, bf16[128,512]{1,0:T(8,128)(2,1)S(1)}, u32[]{:S(2)}, u32[]{:S(2)}) collective-permute-start(bf16[128,512]{1,0:T(8,128)(2,1)S(1)} %get-tuple-element.65), channel_id=1, source_target_pairs={{0,3},{1,2},{2,1},{3,0},{4,7},{5,6},{6,5},{7,4},{8,11},{9,10},{10,... | collective-permute-start | bytes 393224 | tf_op jit(solution)/shard_map/ppermute | solution.py:44
  59.8 10.3 %collective-permute-start.25 = (bf16[128,512]{1,0:T(8,128)(2,1)S(1)}, bf16[128,512]{1,0:T(8,128)(2,1)S(1)}, u32[]{:S(2)}, u32[]{:S(2)}) collective-permute-start(bf16[128,512]{1,0:T(8,128)(2,1)S(1)} %add_convert_fusion.3), channel_id=1, source_target_pairs={{0,6},{1,7},{2,4},{3,5},{4,2},{5,3},{6,0},{7,1},{8,14},{9,15},{10,... | collective-permute-start | bytes 393224 | tf_op jit(solution)/shard_map/ppermute | solution.py:44
  63.9 9.9 %collective-permute-start.18 = (bf16[128,512]{1,0:T(8,128)(2,1)S(1)}, bf16[128,512]{1,0:T(8,128)(2,1)S(1)}, u32[]{:S(2)}, u32[]{:S(2)}) collective-permute-start(bf16[128,512]{1,0:T(8,128)(2,1)S(1)} %add_convert_fusion.5), channel_id=1, source_target_pairs={{0,6},{1,7},{2,4},{3,5},{4,2},{5,3},{6,0},{7,1},{8,14},{9,15},{10,... | collective-permute-start | bytes 393224 | tf_op jit(solution)/shard_map/ppermute | solution.py:44
  70.2 6.0 %collective-permute-start.28 = (bf16[128,512]{1,0:T(8,128)(2,1)S(1)}, bf16[128,512]{1,0:T(8,128)(2,1)S(1)}, u32[]{:S(2)}, u32[]{:S(2)}) collective-permute-start(bf16[128,512]{1,0:T(8,128)(2,1)S(1)} %add_convert_fusion.2.refs_0_), channel_id=1, source_target_pairs={{0,3},{1,2},{2,1},{3,0},{4,7},{5,6},{6,5},{7,4},{8,11},{9,10},{10,... | collective-permute-start | bytes 393224 | tf_op jit(solution)/shard_map/ppermute | solution.py:44
  70.3 7.3 %collective-permute-start.27 = (bf16[128,512]{1,0:T(8,128)(2,1)S(1)}, bf16[128,512]{1,0:T(8,128)(2,1)S(1)}, u32[]{:S(2)}, u32[]{:S(2)}) collective-permute-start(bf16[128,512]{1,0:T(8,128)(2,1)S(1)} %add_convert_fusion.2.refs_0_), channel_id=1, source_target_pairs={{0,2},{1,3},{2,0},{3,1},{4,6},{5,7},{6,4},{7,5},{8,10},{9,11},{10,... | collective-permute-start | bytes 393224 | tf_op jit(solution)/shard_map/ppermute | solution.py:44
  71.1 6.5 %collective-permute-start.26 = (bf16[128,512]{1,0:T(8,128)(2,1)S(1)}, bf16[128,512]{1,0:T(8,128)(2,1)S(1)}, u32[]{:S(2)}, u32[]{:S(2)}) collective-permute-start(bf16[128,512]{1,0:T(8,128)(2,1)S(1)} %add_convert_fusion.2.refs_0_), channel_id=1, source_target_pairs={{0,1},{1,0},{2,3},{3,2},{4,5},{5,4},{6,7},{7,6},{8,9},{9,8},{10,11... | collective-permute-start | bytes 393224 | tf_op jit(solution)/shard_map/ppermute | solution.py:44
  73.8 7.5 %collective-permute-start.21 = (bf16[128,512]{1,0:T(8,128)(2,1)S(1)}, bf16[128,512]{1,0:T(8,128)(2,1)S(1)}, u32[]{:S(2)}, u32[]{:S(2)}) collective-permute-start(bf16[128,512]{1,0:T(8,128)(2,1)S(1)} %add_convert_fusion.4.refs_0_), channel_id=1, source_target_pairs={{0,3},{1,2},{2,1},{3,0},{4,7},{5,6},{6,5},{7,4},{8,11},{9,10},{10,... | collective-permute-start | bytes 393224 | tf_op jit(solution)/shard_map/ppermute | solution.py:44
  74.0 7.8 %collective-permute-start.20 = (bf16[128,512]{1,0:T(8,128)(2,1)S(1)}, bf16[128,512]{1,0:T(8,128)(2,1)S(1)}, u32[]{:S(2)}, u32[]{:S(2)}) collective-permute-start(bf16[128,512]{1,0:T(8,128)(2,1)S(1)} %add_convert_fusion.4.refs_0_), channel_id=1, source_target_pairs={{0,2},{1,3},{2,0},{3,1},{4,6},{5,7},{6,4},{7,5},{8,10},{9,11},{10,... | collective-permute-start | bytes 393224 | tf_op jit(solution)/shard_map/ppermute | solution.py:44
  76.2 6.3 %collective-permute-start.19 = (bf16[128,512]{1,0:T(8,128)(2,1)S(1)}, bf16[128,512]{1,0:T(8,128)(2,1)S(1)}, u32[]{:S(2)}, u32[]{:S(2)}) collective-permute-start(bf16[128,512]{1,0:T(8,128)(2,1)S(1)} %add_convert_fusion.4.refs_0_), channel_id=1, source_target_pairs={{0,1},{1,0},{2,3},{3,2},{4,5},{5,4},{6,7},{7,6},{8,9},{9,8},{10,11... | collective-permute-start | bytes 393224 | tf_op jit(solution)/shard_map/ppermute | solution.py:44
  85.6 6.0 %collective-permute-start.33 = (bf16[128,512]{1,0:T(8,128)(2,1)S(1)}, bf16[128,512]{1,0:T(8,128)(2,1)S(1)}, u32[]{:S(2)}, u32[]{:S(2)}) collective-permute-start(bf16[128,512]{1,0:T(8,128)(2,1)S(1)} %get-tuple-element.80), channel_id=1, source_target_pairs={{0,1},{1,0},{2,3},{3,2},{4,5},{5,4},{6,7},{7,6},{8,9},{9,8},{10,11... | collective-permute-start | bytes 393224 | tf_op jit(solution)/shard_map/ppermute | solution.py:44
  86.4 7.6 %collective-permute-start.34 = (bf16[128,512]{1,0:T(8,128)(2,1)S(1)}, bf16[128,512]{1,0:T(8,128)(2,1)S(1)}, u32[]{:S(2)}, u32[]{:S(2)}) collective-permute-start(bf16[128,512]{1,0:T(8,128)(2,1)S(1)} %get-tuple-element.81), channel_id=1, source_target_pairs={{0,2},{1,3},{2,0},{3,1},{4,6},{5,7},{6,4},{7,5},{8,10},{9,11},{10,... | collective-permute-start | bytes 393224 | tf_op jit(solution)/shard_map/ppermute | solution.py:44
  86.8 8.2 %collective-permute-start.35 = (bf16[128,512]{1,0:T(8,128)(2,1)S(1)}, bf16[128,512]{1,0:T(8,128)(2,1)S(1)}, u32[]{:S(2)}, u32[]{:S(2)}) collective-permute-start(bf16[128,512]{1,0:T(8,128)(2,1)S(1)} %get-tuple-element.82), channel_id=1, source_target_pairs={{0,3},{1,2},{2,1},{3,0},{4,7},{5,6},{6,5},{7,4},{8,11},{9,10},{10,... | collective-permute-start | bytes 393224 | tf_op jit(solution)/shard_map/ppermute | solution.py:44
  90.5 6.6 %collective-permute-start.29 = (bf16[128,512]{1,0:T(8,128)(2,1)S(1)}, bf16[128,512]{1,0:T(8,128)(2,1)S(1)}, u32[]{:S(2)}, u32[]{:S(2)}) collective-permute-start(bf16[128,512]{1,0:T(8,128)(2,1)S(1)} %get-tuple-element.76), channel_id=1, source_target_pairs={{0,1},{1,0},{2,3},{3,2},{4,5},{5,4},{6,7},{7,6},{8,9},{9,8},{10,11... | collective-permute-start | bytes 393224 | tf_op jit(solution)/shard_map/ppermute | solution.py:44
  91.3 5.8 %collective-permute-start.30 = (bf16[128,512]{1,0:T(8,128)(2,1)S(1)}, bf16[128,512]{1,0:T(8,128)(2,1)S(1)}, u32[]{:S(2)}, u32[]{:S(2)}) collective-permute-start(bf16[128,512]{1,0:T(8,128)(2,1)S(1)} %get-tuple-element.77), channel_id=1, source_target_pairs={{0,2},{1,3},{2,0},{3,1},{4,6},{5,7},{6,4},{7,5},{8,10},{9,11},{10,... | collective-permute-start | bytes 393224 | tf_op jit(solution)/shard_map/ppermute | solution.py:44
  91.7 7.0 %collective-permute-start.31 = (bf16[128,512]{1,0:T(8,128)(2,1)S(1)}, bf16[128,512]{1,0:T(8,128)(2,1)S(1)}, u32[]{:S(2)}, u32[]{:S(2)}) collective-permute-start(bf16[128,512]{1,0:T(8,128)(2,1)S(1)} %get-tuple-element.78), channel_id=1, source_target_pairs={{0,3},{1,2},{2,1},{3,0},{4,7},{5,6},{6,5},{7,4},{8,11},{9,10},{10,... | collective-permute-start | bytes 393224 | tf_op jit(solution)/shard_map/ppermute | solution.py:44
  95.3 6.8 %collective-permute-start.36 = (bf16[128,512]{1,0:T(8,128)(2,1)S(1)}, bf16[128,512]{1,0:T(8,128)(2,1)S(1)}, u32[]{:S(2)}, u32[]{:S(2)}) collective-permute-start(bf16[128,512]{1,0:T(8,128)(2,1)S(1)} %convolution_convert_fusion), channel_id=1, source_target_pairs={{0,6},{1,7},{2,4},{3,5},{4,2},{5,3},{6,0},{7,1},{8,14},{9,15},{10,... | collective-permute-start | bytes 393224 | tf_op jit(solution)/shard_map/ppermute | solution.py:44
  99.0 6.8 %collective-permute-start.32 = (bf16[128,512]{1,0:T(8,128)(2,1)S(1)}, bf16[128,512]{1,0:T(8,128)(2,1)S(1)}, u32[]{:S(2)}, u32[]{:S(2)}) collective-permute-start(bf16[128,512]{1,0:T(8,128)(2,1)S(1)} %convolution_convert_fusion.1), channel_id=1, source_target_pairs={{0,6},{1,7},{2,4},{3,5},{4,2},{5,3},{6,0},{7,1},{8,14},{9,15},{10,... | collective-permute-start | bytes 393224 | tf_op jit(solution)/shard_map/ppermute | solution.py:44
  (13 other events, 137.5 us)

commit v7 on v6

--- a/solution.py
+++ b/solution.py
@@ -367,7 +367,7 @@
     )
     side_by_side = key_weight.shape[1] % 128 == 0
     kv_weights = ((key_weight, value_matrix),) if side_by_side else (key_weight, value_matrix)
-    *kv_parts, query_w, output_w, done = load((*kv_weights, query_weight, output_weight), parts[0], "load_qkvo")
+    *kv_parts, output_w, done = load((*kv_weights, output_weight), parts[0], "load_kvo")
     kv_w = kv_parts[0] if side_by_side else jnp.concatenate(kv_parts, axis=1)
 
     cuts = FRONT_CUTS
@@ -441,6 +441,7 @@
         limit=kernel_mib,
     )
     down_half = down_weight.shape[0] // 2
+    query_w, _ = load((query_weight,), sends[0], "load_query")
     got = near_swap(sends, KEYS_ORDER)
     raw_q = run(
         matmul_kernel, "query", shape((count, heads_here * HEAD_SIZE), f32), [VMEM, VMEM], rows_normed, query_w

time: 114 us -> 113 us (level)
  starting transfers between devices: 61.6 us -> 49.7 us
  waiting for transfers between devices: 17.9 us -> 27.7 us
  Pallas kernels: 29.9 us -> 31.5 us
    ppermute x40, starting transfers between devices: 61.6 us -> 49.7 us  [swap(): return lax.ppermute(value, 'ctx', [(i, i ^ mask) for i in range(size)])]
    ppermute x40, waiting for transfers between devices: 17.9 us -> 27.7 us  [swap(): return lax.ppermute(value, 'ctx', [(i, i ^ mask) for i in range(size)])]
    pallas_call x4 -> x5, Pallas kernels: 15.3 us -> 16.9 us  [load(): pl.pallas_call(kernel, in_specs=[HBM] * len(flat) + [ANY], out_specs=[VME...]
  transfers between devices with their start and end apart: 40 -> 40, of which waited for: 18 -> 17; matrix products, arithmetic and copies ran while one was open for 3% -> 3% of each run, Pallas kernels for 19% -> 20%
where the time goes in v7:
time: 113 us
  starting transfers between devices  49.7 us (44%)
  Pallas kernels  31.5 us (28%)
  waiting for transfers between devices  27.7 us (25%)
  matrix products  1.76 us (2%)
  other arithmetic  1.72 us (2%)
    ppermute x40, starting transfers between devices, swap(): return lax.ppermute(value, 'ctx', [(i, i ^ mask) for i in range(size)])  49.7 us
    ppermute x40, waiting for transfers between devices, swap(): return lax.ppermute(value, 'ctx', [(i, i ^ mask) for i in range(size)])  27.7 us
    pallas_call x5, Pallas kernels, load(): pl.pallas_call(kernel, in_specs=[HBM] * len(flat) + [ANY], out_specs=[VME...  16.9 us
    pallas_call x12, Pallas kernels, run(): pl.pallas_call(kernel, in_specs=specs, out_specs=outs, out_shape=out_shap...  13.2 us
  transfers between devices with their start and end apart: 40, of which 17 were waited for; matrix products, arithmetic and copies ran while one was open for 3% of the time, Pallas kernels for 20%

profile of v7, /device:TPU:0, one launch (start us, length us, event | category | flops | bytes accessed | tf_op | source)
XLA Modules:
  0.0 113.0 jit_solution(11597270417259865743)
XLA Ops:
  0.0 1.5 %pick.1 = (bf16[32,1152]{1,0:T(8,128)(2,1)S(1)}, bf16[32,1152]{1,0:T(8,128)(2,1)S(1)}, bf16[32,1152]{1,0:T(8,128)(2,1)S(1)}, bf16[32,1152]{1,0:T(8,128)(2,1)S(1)}) custom-call(s32[1]{0:T(128)} %bitcast.near, s32[1,128]{1,0:T(1,128)} %bitcast.29, bf16[128,4096]{1,0:T(8,128)(2,1)} %tokens.1), custom_call_target="tpu_custom_call" | custom-call | tf_op jit(solution)/shard_map/pick/pallas_call | solution.py:77
  1.6 3.0 %collective-permute-start = (bf16[32,1152]{1,0:T(8,128)(2,1)S(1)}, bf16[32,1152]{1,0:T(8,128)(2,1)S(1)}, u32[]{:S(2)}, u32[]{:S(2)}) collective-permute-start(bf16[32,1152]{1,0:T(8,128)(2,1)S(1)} %get-tuple-element.46), channel_id=1, source_target_pairs={{0,1},{1,0},{2,3},{3,2},{4,5},{5,4},{6,7},{7,6},{8,9},{9,8},{10,11... | collective-permute-start | bytes 221192 | tf_op jit(solution)/shard_map/ppermute | solution.py:44
  4.6 1.6 %collective-permute-start.1 = (bf16[32,1152]{1,0:T(8,128)(2,1)S(1)}, bf16[32,1152]{1,0:T(8,128)(2,1)S(1)}, u32[]{:S(2)}, u32[]{:S(2)}) collective-permute-start(bf16[32,1152]{1,0:T(8,128)(2,1)S(1)} %get-tuple-element.47), channel_id=1, source_target_pairs={{0,2},{1,3},{2,0},{3,1},{4,6},{5,7},{6,4},{7,5},{8,10},{9,11},{10,... | collective-permute-start | bytes 221192 | tf_op jit(solution)/shard_map/ppermute | solution.py:44
  6.4 2.9 %load_kvo.1 = (bf16[4096,256]{1,0:T(8,128)(2,1)S(1)}, bf16[512,4096]{1,0:T(8,128)(2,1)S(1)}, s32[8,128]{1,0:T(8,128)S(1)}) custom-call(bf16[4096,128]{1,0:T(8,128)(2,1)} %refs_0_.5, bf16[4096,128]{1,0:T(8,128)(2,1)} %refs_1_.1, bf16[512,4096]{1,0:T(8,128)(2,1)} %refs_2_.1, bf16[32,1152]{1,0:T(8,128)(2,1)S(1)} %get-tuple-element.44.refs_3_.refs_0_), custom_call_target="tpu_custom_call" | custom-call | tf_op jit(solution)/shard_map/load_kvo/pallas_call | solution.py:113
  9.6 1.9 %collective-permute-done.2.refs_3_ = bf16[32,1152]{1,0:T(8,128)(2,1)S(1)} collective-permute-done((bf16[32,1152]{1,0:T(8,128)(2,1)S(1)}, bf16[32,1152]{1,0:T(8,128)(2,1)S(1)}, u32[]{:S(2)}, u32[]{:S(2)}) %collective-permute-start.2) | collective-permute-done | bytes 73760 | tf_op jit(solution)/shard_map/ppermute | solution.py:44
  11.5 2.5 %collective-permute-start.3 = (bf16[144,512]{1,0:T(8,128)(2,1)S(1)}, bf16[144,512]{1,0:T(8,128)(2,1)S(1)}, u32[]{:S(2)}, u32[]{:S(2)}) collective-permute-start(bf16[144,512]{1,0:T(8,128)(2,1)S(1)} %pack.2.refs_1_), channel_id=1, source_target_pairs={{0,6},{1,7},{2,4},{3,5},{4,2},{5,3},{6,0},{7,1},{8,14},{9,15},{10,... | collective-permute-start | bytes 442376 | tf_op jit(solution)/shard_map/ppermute | solution.py:44
  14.0 4.3 %load_gate.1 = (bf16[4096,1408]{1,0:T(8,128)(2,1)S(1)}, s32[8,128]{1,0:T(8,128)S(1)}) custom-call(bf16[4096,1408]{1,0:T(8,128)(2,1)} %refs_0_.6, bf16[144,512]{1,0:T(8,128)(2,1)S(1)} %pack.2.refs_1_), custom_call_target="tpu_custom_call" | custom-call | tf_op jit(solution)/shard_map/load_gate/pallas_call | solution.py:113
  20.1 2.6 %collective-permute-start.9 = (bf16[128,512]{1,0:T(8,128)(2,1)S(1)}, bf16[128,512]{1,0:T(8,128)(2,1)S(1)}, u32[]{:S(2)}, u32[]{:S(2)}) collective-permute-start(bf16[128,512]{1,0:T(8,128)(2,1)S(1)} %convolution_convert_fusion.3.refs_1_.refs_0_), channel_id=1, source_target_pairs={{0,3},{1,2},{2,1},{3,0},{4,7},{5,6},{6,5},{7,4},{8,11},{9,10},{10,... | collective-permute-start | bytes 393224 | tf_op jit(solution)/shard_map/ppermute | solution.py:44
  24.3 2.3 %collective-permute-done.4 = bf16[128,512]{1,0:T(8,128)(2,1)S(1)} collective-permute-done((bf16[128,512]{1,0:T(8,128)(2,1)S(1)}, bf16[128,512]{1,0:T(8,128)(2,1)S(1)}, u32[]{:S(2)}, u32[]{:S(2)}) %collective-permute-start.4) | collective-permute-done | bytes 131104 | tf_op jit(solution)/shard_map/ppermute | solution.py:44
  27.1 2.3 %collective-permute-start.8 = (bf16[128,512]{1,0:T(8,128)(2,1)S(1)}, bf16[128,512]{1,0:T(8,128)(2,1)S(1)}, u32[]{:S(2)}, u32[]{:S(2)}) collective-permute-start(bf16[128,512]{1,0:T(8,128)(2,1)S(1)} %convolution_convert_fusion.2.refs_1_), channel_id=1, source_target_pairs={{0,2},{1,3},{2,0},{3,1},{4,6},{5,7},{6,4},{7,5},{8,10},{9,11},{10,... | collective-permute-start | bytes 393224 | tf_op jit(solution)/shard_map/ppermute | solution.py:44
  30.6 4.3 %load_up.1 = (bf16[4096,1408]{1,0:T(8,128)(2,1)S(1)}, s32[8,128]{1,0:T(8,128)S(1)}) custom-call(bf16[4096,1408]{1,0:T(8,128)(2,1)} %refs_0_.7, bf16[128,512]{1,0:T(8,128)(2,1)S(1)} %convolution_convert_fusion.3.refs_1_.refs_0_), custom_call_target="tpu_custom_call" | custom-call | tf_op jit(solution)/shard_map/load_up/pallas_call | solution.py:113
  38.0 2.0 %collective-permute-start.13 = (bf16[64,128]{1,0:T(8,128)(2,1)S(1)}, bf16[64,128]{1,0:T(8,128)(2,1)S(1)}, u32[]{:S(2)}, u32[]{:S(2)}) collective-permute-start(bf16[64,128]{1,0:T(8,128)(2,1)S(1)} %get-tuple-element.59), channel_id=1, source_target_pairs={{0,3},{1,2},{2,1},{3,0},{4,7},{5,6},{6,5},{7,4},{8,11},{9,10},{10,... | collective-permute-start | bytes 49160 | tf_op jit(solution)/shard_map/ppermute | solution.py:44
  40.0 2.8 %load_query.1 = (bf16[4096,512]{1,0:T(8,128)(2,1)S(1)}, s32[8,128]{1,0:T(8,128)}) custom-call(bf16[4096,512]{1,0:T(8,128)(2,1)} %refs_0_.8, bf16[64,128]{1,0:T(8,128)(2,1)S(1)} %get-tuple-element.55.refs_1_), custom_call_target="tpu_custom_call" | custom-call | tf_op jit(solution)/shard_map/load_query/pallas_call | solution.py:113
  43.6 1.8 %collective-permute-start.14 = (bf16[128,128]{1,0:T(8,128)(2,1)S(1)}, bf16[128,128]{1,0:T(8,128)(2,1)S(1)}, u32[]{:S(2)}, u32[]{:S(2)}) collective-permute-start(bf16[128,128]{1,0:T(8,128)(2,1)S(1)} %pad_maximum_fusion.3), channel_id=1, source_target_pairs={{0,4},{1,5},{2,6},{3,7},{4,0},{5,1},{6,2},{7,3},{8,12},{9,13},{10,... | collective-permute-start | bytes 98312 | tf_op jit(solution)/shard_map/ppermute | solution.py:44
  45.4 2.6 %load_down.1 = (bf16[704,4096]{1,0:T(8,128)(2,1)S(1)}, s32[8,128]{1,0:T(8,128)S(1)}) custom-call(bf16[1408,4096]{1,0:T(8,128)(2,1)} %refs_4_.1, bf16[128,128]{1,0:T(8,128)(2,1)S(1)} %pad_maximum_fusion.4.refs_1_), custom_call_target="tpu_custom_call" | custom-call | tf_op jit(solution)/shard_map/load_down/pallas_call | solution.py:113
  51.7 2.1 %collective-permute-start.24 = (bf16[128,512]{1,0:T(8,128)(2,1)S(1)}, bf16[128,512]{1,0:T(8,128)(2,1)S(1)}, u32[]{:S(2)}, u32[]{:S(2)}) collective-permute-start(bf16[128,512]{1,0:T(8,128)(2,1)S(1)} %get-tuple-element.69), channel_id=1, source_target_pairs={{0,3},{1,2},{2,1},{3,0},{4,7},{5,6},{6,5},{7,4},{8,11},{9,10},{10,... | collective-permute-start | bytes 393224 | tf_op jit(solution)/shard_map/ppermute | solution.py:44
  58.3 1.6 %collective-permute-done.24 = bf16[128,512]{1,0:T(8,128)(2,1)S(1)} collective-permute-done((bf16[128,512]{1,0:T(8,128)(2,1)S(1)}, bf16[128,512]{1,0:T(8,128)(2,1)S(1)}, u32[]{:S(2)}, u32[]{:S(2)}) %collective-permute-start.24) | collective-permute-done | bytes 131104 | tf_op jit(solution)/shard_map/ppermute | solution.py:44
  61.3 4.0 %collective-permute-done.17 = bf16[128,512]{1,0:T(8,128)(2,1)S(1)} collective-permute-done((bf16[128,512]{1,0:T(8,128)(2,1)S(1)}, bf16[128,512]{1,0:T(8,128)(2,1)S(1)}, u32[]{:S(2)}, u32[]{:S(2)}) %collective-permute-start.17) | collective-permute-done | bytes 131104 | tf_op jit(solution)/shard_map/ppermute | solution.py:44
  65.5 2.9 %collective-permute-done.25 = bf16[128,512]{1,0:T(8,128)(2,1)S(1)} collective-permute-done((bf16[128,512]{1,0:T(8,128)(2,1)S(1)}, bf16[128,512]{1,0:T(8,128)(2,1)S(1)}, u32[]{:S(2)}, u32[]{:S(2)}) %collective-permute-start.25) | collective-permute-done | bytes 131104 | tf_op jit(solution)/shard_map/ppermute | solution.py:44
  68.5 3.6 %collective-permute-start.27 = (bf16[128,512]{1,0:T(8,128)(2,1)S(1)}, bf16[128,512]{1,0:T(8,128)(2,1)S(1)}, u32[]{:S(2)}, u32[]{:S(2)}) collective-permute-start(bf16[128,512]{1,0:T(8,128)(2,1)S(1)} %add_convert_fusion.2.refs_0_), channel_id=1, source_target_pairs={{0,2},{1,3},{2,0},{3,1},{4,6},{5,7},{6,4},{7,5},{8,10},{9,11},{10,... | collective-permute-start | bytes 393224 | tf_op jit(solution)/shard_map/ppermute | solution.py:44
  73.8 1.9 %collective-permute-start.20 = (bf16[128,512]{1,0:T(8,128)(2,1)S(1)}, bf16[128,512]{1,0:T(8,128)(2,1)S(1)}, u32[]{:S(2)}, u32[]{:S(2)}) collective-permute-start(bf16[128,512]{1,0:T(8,128)(2,1)S(1)} %add_convert_fusion.4.refs_0_), channel_id=1, source_target_pairs={{0,2},{1,3},{2,0},{3,1},{4,6},{5,7},{6,4},{7,5},{8,10},{9,11},{10,... | collective-permute-start | bytes 393224 | tf_op jit(solution)/shard_map/ppermute | solution.py:44
  77.2 3.7 %hidden_part.1 = (f32[128,1408]{1,0:T(8,128)S(1)}, f32[128,1408]{1,0:T(8,128)S(1)}, f32[128,128]{1,0:T(8,128)S(1)}, bf16[704,4096]{1,0:T(8,128)(2,1)S(1)}) custom-call(s32[1]{0:T(128)} %bitcast.near, f32[1,4096]{1,0:T(1,128)S(1)} %bitcast.26, bf16[4096,1408]{1,0:T(8,128)(2,1)S(1)} %get-tuple-element.49.gate, bf16[4096,1408]{1,0:T(8,128)(2,1)S(1)} %get-tuple-element.50.up, ...), custom_call_target="tpu_custom_call" | custom-call | tf_op jit(solution)/shard_map/hidden_part/pallas_call | solution.py:77
  82.1 2.0 %hidden.1.left = bf16[128,1408]{1,0:T(8,128)(2,1)S(1)} custom-call(s32[1]{0:T(128)} %bitcast.near, f32[1,4096]{1,0:T(1,128)S(1)} %bitcast.27, bf16[4096,1408]{1,0:T(8,128)(2,1)S(1)} %get-tuple-element.49.gate, bf16[4096,1408]{1,0:T(8,128)(2,1)S(1)} %get-tuple-element.50.up, bf16[128,512]{1,0:T(8,128)(2,1)S(1)} %add_convert_fusion.4.refs_0_, ...), custom_call_target="tpu_custom_call" | custom-call | tf_op jit(solution)/shard_map/hidden/pallas_call | solution.py:77
  86.1 2.7 %collective-permute-start.35 = (bf16[128,512]{1,0:T(8,128)(2,1)S(1)}, bf16[128,512]{1,0:T(8,128)(2,1)S(1)}, u32[]{:S(2)}, u32[]{:S(2)}) collective-permute-start(bf16[128,512]{1,0:T(8,128)(2,1)S(1)} %get-tuple-element.82), channel_id=1, source_target_pairs={{0,3},{1,2},{2,1},{3,0},{4,7},{5,6},{6,5},{7,4},{8,11},{9,10},{10,... | collective-permute-start | bytes 393224 | tf_op jit(solution)/shard_map/ppermute | solution.py:44
  90.9 2.7 %collective-permute-start.31 = (bf16[128,512]{1,0:T(8,128)(2,1)S(1)}, bf16[128,512]{1,0:T(8,128)(2,1)S(1)}, u32[]{:S(2)}, u32[]{:S(2)}) collective-permute-start(bf16[128,512]{1,0:T(8,128)(2,1)S(1)} %get-tuple-element.78), channel_id=1, source_target_pairs={{0,3},{1,2},{2,1},{3,0},{4,7},{5,6},{6,5},{7,4},{8,11},{9,10},{10,... | collective-permute-start | bytes 393224 | tf_op jit(solution)/shard_map/ppermute | solution.py:44
  94.3 2.2 %collective-permute-start.36 = (bf16[128,512]{1,0:T(8,128)(2,1)S(1)}, bf16[128,512]{1,0:T(8,128)(2,1)S(1)}, u32[]{:S(2)}, u32[]{:S(2)}) collective-permute-start(bf16[128,512]{1,0:T(8,128)(2,1)S(1)} %convolution_convert_fusion), channel_id=1, source_target_pairs={{0,6},{1,7},{2,4},{3,5},{4,2},{5,3},{6,0},{7,1},{8,14},{9,15},{10,... | collective-permute-start | bytes 393224 | tf_op jit(solution)/shard_map/ppermute | solution.py:44
  96.5 1.8 %collective-permute-done.31 = bf16[128,512]{1,0:T(8,128)(2,1)S(1)} collective-permute-done((bf16[128,512]{1,0:T(8,128)(2,1)S(1)}, bf16[128,512]{1,0:T(8,128)(2,1)S(1)}, u32[]{:S(2)}, u32[]{:S(2)}) %collective-permute-start.31) | collective-permute-done | bytes 131104 | tf_op jit(solution)/shard_map/ppermute | solution.py:44
  99.6 2.1 %collective-permute-done.36 = bf16[128,512]{1,0:T(8,128)(2,1)S(1)} collective-permute-done((bf16[128,512]{1,0:T(8,128)(2,1)S(1)}, bf16[128,512]{1,0:T(8,128)(2,1)S(1)}, u32[]{:S(2)}, u32[]{:S(2)}) %collective-permute-start.36) | collective-permute-done | bytes 131104 | tf_op jit(solution)/shard_map/ppermute | solution.py:44
  102.0 3.4 %collective-permute-done.32 = bf16[128,512]{1,0:T(8,128)(2,1)S(1)} collective-permute-done((bf16[128,512]{1,0:T(8,128)(2,1)S(1)}, bf16[128,512]{1,0:T(8,128)(2,1)S(1)}, u32[]{:S(2)}, u32[]{:S(2)}) %collective-permute-start.32) | collective-permute-done | bytes 131104 | tf_op jit(solution)/shard_map/ppermute | solution.py:44
  105.7 1.7 %collective-permute-start.39 = (bf16[32,1024]{1,0:T(8,128)(2,1)S(1)}, bf16[32,1024]{1,0:T(8,128)(2,1)S(1)}, u32[]{:S(2)}, u32[]{:S(2)}) collective-permute-start(bf16[32,1024]{1,0:T(8,128)(2,1)S(1)} %get-tuple-element.85), channel_id=1, source_target_pairs={{0,3},{1,2},{2,1},{3,0},{4,7},{5,6},{6,5},{7,4},{8,11},{9,10},{10,... | collective-permute-start | bytes 196616 | tf_op jit(solution)/shard_map/ppermute | solution.py:44
  107.3 1.9 %collective-permute-start.38 = (bf16[32,1024]{1,0:T(8,128)(2,1)S(1)}, bf16[32,1024]{1,0:T(8,128)(2,1)S(1)}, u32[]{:S(2)}, u32[]{:S(2)}) collective-permute-start(bf16[32,1024]{1,0:T(8,128)(2,1)S(1)} %get-tuple-element.88), channel_id=1, source_target_pairs={{0,2},{1,3},{2,0},{3,1},{4,6},{5,7},{6,4},{7,5},{8,10},{9,11},{10,... | collective-permute-start | bytes 196616 | tf_op jit(solution)/shard_map/ppermute | solution.py:44
  109.2 1.7 %collective-permute-done.39.refs_3_ = bf16[32,1024]{1,0:T(8,128)(2,1)S(1)} collective-permute-done((bf16[32,1024]{1,0:T(8,128)(2,1)S(1)}, bf16[32,1024]{1,0:T(8,128)(2,1)S(1)}, u32[]{:S(2)}, u32[]{:S(2)}) %collective-permute-start.39) | collective-permute-done | bytes 65568 | tf_op jit(solution)/shard_map/ppermute | solution.py:44
  (121 shorter events, 32.5 us)
Async XLA Ops:
  1.6 7.8 %collective-permute-start = (bf16[32,1152]{1,0:T(8,128)(2,1)S(1)}, bf16[32,1152]{1,0:T(8,128)(2,1)S(1)}, u32[]{:S(2)}, u32[]{:S(2)}) collective-permute-start(bf16[32,1152]{1,0:T(8,128)(2,1)S(1)} %get-tuple-element.46), channel_id=1, source_target_pairs={{0,1},{1,0},{2,3},{3,2},{4,5},{5,4},{6,7},{7,6},{8,9},{9,8},{10,11... | collective-permute-start | bytes 221192 | tf_op jit(solution)/shard_map/ppermute | solution.py:44
  11.5 8.3 %collective-permute-start.3 = (bf16[144,512]{1,0:T(8,128)(2,1)S(1)}, bf16[144,512]{1,0:T(8,128)(2,1)S(1)}, u32[]{:S(2)}, u32[]{:S(2)}) collective-permute-start(bf16[144,512]{1,0:T(8,128)(2,1)S(1)} %pack.2.refs_1_), channel_id=1, source_target_pairs={{0,6},{1,7},{2,4},{3,5},{4,2},{5,3},{6,0},{7,1},{8,14},{9,15},{10,... | collective-permute-start | bytes 442376 | tf_op jit(solution)/shard_map/ppermute | solution.py:44
  18.3 8.3 %collective-permute-start.4 = (bf16[128,512]{1,0:T(8,128)(2,1)S(1)}, bf16[128,512]{1,0:T(8,128)(2,1)S(1)}, u32[]{:S(2)}, u32[]{:S(2)}) collective-permute-start(bf16[128,512]{1,0:T(8,128)(2,1)S(1)} %pack.3), channel_id=1, source_target_pairs={{0,6},{1,7},{2,4},{3,5},{4,2},{5,3},{6,0},{7,1},{8,14},{9,15},{10,... | collective-permute-start | bytes 393224 | tf_op jit(solution)/shard_map/ppermute | solution.py:44
  20.1 9.3 %collective-permute-start.9 = (bf16[128,512]{1,0:T(8,128)(2,1)S(1)}, bf16[128,512]{1,0:T(8,128)(2,1)S(1)}, u32[]{:S(2)}, u32[]{:S(2)}) collective-permute-start(bf16[128,512]{1,0:T(8,128)(2,1)S(1)} %convolution_convert_fusion.3.refs_1_.refs_0_), channel_id=1, source_target_pairs={{0,3},{1,2},{2,1},{3,0},{4,7},{5,6},{6,5},{7,4},{8,11},{9,10},{10,... | collective-permute-start | bytes 393224 | tf_op jit(solution)/shard_map/ppermute | solution.py:44
  22.7 12.3 %collective-permute-start.7 = (bf16[128,512]{1,0:T(8,128)(2,1)S(1)}, bf16[128,512]{1,0:T(8,128)(2,1)S(1)}, u32[]{:S(2)}, u32[]{:S(2)}) collective-permute-start(bf16[128,512]{1,0:T(8,128)(2,1)S(1)} %convolution_convert_fusion.3.refs_1_.refs_0_), channel_id=1, source_target_pairs={{0,2},{1,3},{2,0},{3,1},{4,6},{5,7},{6,4},{7,5},{8,10},{9,11},{10,... | collective-permute-start | bytes 393224 | tf_op jit(solution)/shard_map/ppermute | solution.py:44
  22.7 12.3 %collective-permute-start.5 = (bf16[128,512]{1,0:T(8,128)(2,1)S(1)}, bf16[128,512]{1,0:T(8,128)(2,1)S(1)}, u32[]{:S(2)}, u32[]{:S(2)}) collective-permute-start(bf16[128,512]{1,0:T(8,128)(2,1)S(1)} %convolution_convert_fusion.3.refs_1_.refs_0_), channel_id=1, source_target_pairs={{0,1},{1,0},{2,3},{3,2},{4,5},{5,4},{6,7},{7,6},{8,9},{9,8},{10,11... | collective-permute-start | bytes 393224 | tf_op jit(solution)/shard_map/ppermute | solution.py:44
  26.8 8.2 %collective-permute-start.10 = (bf16[128,512]{1,0:T(8,128)(2,1)S(1)}, bf16[128,512]{1,0:T(8,128)(2,1)S(1)}, u32[]{:S(2)}, u32[]{:S(2)}) collective-permute-start(bf16[128,512]{1,0:T(8,128)(2,1)S(1)} %convolution_convert_fusion.2.refs_1_), channel_id=1, source_target_pairs={{0,3},{1,2},{2,1},{3,0},{4,7},{5,6},{6,5},{7,4},{8,11},{9,10},{10,... | collective-permute-start | bytes 393224 | tf_op jit(solution)/shard_map/ppermute | solution.py:44
  27.1 7.9 %collective-permute-start.8 = (bf16[128,512]{1,0:T(8,128)(2,1)S(1)}, bf16[128,512]{1,0:T(8,128)(2,1)S(1)}, u32[]{:S(2)}, u32[]{:S(2)}) collective-permute-start(bf16[128,512]{1,0:T(8,128)(2,1)S(1)} %convolution_convert_fusion.2.refs_1_), channel_id=1, source_target_pairs={{0,2},{1,3},{2,0},{3,1},{4,6},{5,7},{6,4},{7,5},{8,10},{9,11},{10,... | collective-permute-start | bytes 393224 | tf_op jit(solution)/shard_map/ppermute | solution.py:44
  29.5 5.7 %collective-permute-start.6 = (bf16[128,512]{1,0:T(8,128)(2,1)S(1)}, bf16[128,512]{1,0:T(8,128)(2,1)S(1)}, u32[]{:S(2)}, u32[]{:S(2)}) collective-permute-start(bf16[128,512]{1,0:T(8,128)(2,1)S(1)} %convolution_convert_fusion.2.refs_1_), channel_id=1, source_target_pairs={{0,1},{1,0},{2,3},{3,2},{4,5},{5,4},{6,7},{7,6},{8,9},{9,8},{10,11... | collective-permute-start | bytes 393224 | tf_op jit(solution)/shard_map/ppermute | solution.py:44
  36.5 7.1 %collective-permute-start.11 = (bf16[64,128]{1,0:T(8,128)(2,1)S(1)}, bf16[64,128]{1,0:T(8,128)(2,1)S(1)}, u32[]{:S(2)}, u32[]{:S(2)}) collective-permute-start(bf16[64,128]{1,0:T(8,128)(2,1)S(1)} %get-tuple-element.57), channel_id=1, source_target_pairs={{0,1},{1,0},{2,3},{3,2},{4,5},{5,4},{6,7},{7,6},{8,9},{9,8},{10,11... | collective-permute-start | bytes 49160 | tf_op jit(solution)/shard_map/ppermute | solution.py:44
  37.5 6.1 %collective-permute-start.12 = (bf16[64,128]{1,0:T(8,128)(2,1)S(1)}, bf16[64,128]{1,0:T(8,128)(2,1)S(1)}, u32[]{:S(2)}, u32[]{:S(2)}) collective-permute-start(bf16[64,128]{1,0:T(8,128)(2,1)S(1)} %get-tuple-element.58), channel_id=1, source_target_pairs={{0,2},{1,3},{2,0},{3,1},{4,6},{5,7},{6,4},{7,5},{8,10},{9,11},{10,... | collective-permute-start | bytes 49160 | tf_op jit(solution)/shard_map/ppermute | solution.py:44
  38.0 5.6 %collective-permute-start.13 = (bf16[64,128]{1,0:T(8,128)(2,1)S(1)}, bf16[64,128]{1,0:T(8,128)(2,1)S(1)}, u32[]{:S(2)}, u32[]{:S(2)}) collective-permute-start(bf16[64,128]{1,0:T(8,128)(2,1)S(1)} %get-tuple-element.59), channel_id=1, source_target_pairs={{0,3},{1,2},{2,1},{3,0},{4,7},{5,6},{6,5},{7,4},{8,11},{9,10},{10,... | collective-permute-start | bytes 49160 | tf_op jit(solution)/shard_map/ppermute | solution.py:44
  50.3 6.9 %collective-permute-start.22 = (bf16[128,512]{1,0:T(8,128)(2,1)S(1)}, bf16[128,512]{1,0:T(8,128)(2,1)S(1)}, u32[]{:S(2)}, u32[]{:S(2)}) collective-permute-start(bf16[128,512]{1,0:T(8,128)(2,1)S(1)} %get-tuple-element.67), channel_id=1, source_target_pairs={{0,1},{1,0},{2,3},{3,2},{4,5},{5,4},{6,7},{7,6},{8,9},{9,8},{10,11... | collective-permute-start | bytes 393224 | tf_op jit(solution)/shard_map/ppermute | solution.py:44
  51.4 6.9 %collective-permute-start.23 = (bf16[128,512]{1,0:T(8,128)(2,1)S(1)}, bf16[128,512]{1,0:T(8,128)(2,1)S(1)}, u32[]{:S(2)}, u32[]{:S(2)}) collective-permute-start(bf16[128,512]{1,0:T(8,128)(2,1)S(1)} %get-tuple-element.68), channel_id=1, source_target_pairs={{0,2},{1,3},{2,0},{3,1},{4,6},{5,7},{6,4},{7,5},{8,10},{9,11},{10,... | collective-permute-start | bytes 393224 | tf_op jit(solution)/shard_map/ppermute | solution.py:44
  51.7 8.1 %collective-permute-start.24 = (bf16[128,512]{1,0:T(8,128)(2,1)S(1)}, bf16[128,512]{1,0:T(8,128)(2,1)S(1)}, u32[]{:S(2)}, u32[]{:S(2)}) collective-permute-start(bf16[128,512]{1,0:T(8,128)(2,1)S(1)} %get-tuple-element.69), channel_id=1, source_target_pairs={{0,3},{1,2},{2,1},{3,0},{4,7},{5,6},{6,5},{7,4},{8,11},{9,10},{10,... | collective-permute-start | bytes 393224 | tf_op jit(solution)/shard_map/ppermute | solution.py:44
  54.4 6.9 %collective-permute-start.15 = (bf16[128,512]{1,0:T(8,128)(2,1)S(1)}, bf16[128,512]{1,0:T(8,128)(2,1)S(1)}, u32[]{:S(2)}, u32[]{:S(2)}) collective-permute-start(bf16[128,512]{1,0:T(8,128)(2,1)S(1)} %get-tuple-element.63), channel_id=1, source_target_pairs={{0,1},{1,0},{2,3},{3,2},{4,5},{5,4},{6,7},{7,6},{8,9},{9,8},{10,11... | collective-permute-start | bytes 393224 | tf_op jit(solution)/shard_map/ppermute | solution.py:44
  55.4 5.9 %collective-permute-start.16 = (bf16[128,512]{1,0:T(8,128)(2,1)S(1)}, bf16[128,512]{1,0:T(8,128)(2,1)S(1)}, u32[]{:S(2)}, u32[]{:S(2)}) collective-permute-start(bf16[128,512]{1,0:T(8,128)(2,1)S(1)} %get-tuple-element.64), channel_id=1, source_target_pairs={{0,2},{1,3},{2,0},{3,1},{4,6},{5,7},{6,4},{7,5},{8,10},{9,11},{10,... | collective-permute-start | bytes 393224 | tf_op jit(solution)/shard_map/ppermute | solution.py:44
  57.3 8.0 %collective-permute-start.17 = (bf16[128,512]{1,0:T(8,128)(2,1)S(1)}, bf16[128,512]{1,0:T(8,128)(2,1)S(1)}, u32[]{:S(2)}, u32[]{:S(2)}) collective-permute-start(bf16[128,512]{1,0:T(8,128)(2,1)S(1)} %get-tuple-element.65), channel_id=1, source_target_pairs={{0,3},{1,2},{2,1},{3,0},{4,7},{5,6},{6,5},{7,4},{8,11},{9,10},{10,... | collective-permute-start | bytes 393224 | tf_op jit(solution)/shard_map/ppermute | solution.py:44
  59.9 8.5 %collective-permute-start.25 = (bf16[128,512]{1,0:T(8,128)(2,1)S(1)}, bf16[128,512]{1,0:T(8,128)(2,1)S(1)}, u32[]{:S(2)}, u32[]{:S(2)}) collective-permute-start(bf16[128,512]{1,0:T(8,128)(2,1)S(1)} %add_convert_fusion.3), channel_id=1, source_target_pairs={{0,6},{1,7},{2,4},{3,5},{4,2},{5,3},{6,0},{7,1},{8,14},{9,15},{10,... | collective-permute-start | bytes 393224 | tf_op jit(solution)/shard_map/ppermute | solution.py:44
  65.3 8.0 %collective-permute-start.18 = (bf16[128,512]{1,0:T(8,128)(2,1)S(1)}, bf16[128,512]{1,0:T(8,128)(2,1)S(1)}, u32[]{:S(2)}, u32[]{:S(2)}) collective-permute-start(bf16[128,512]{1,0:T(8,128)(2,1)S(1)} %add_convert_fusion.5), channel_id=1, source_target_pairs={{0,6},{1,7},{2,4},{3,5},{4,2},{5,3},{6,0},{7,1},{8,14},{9,15},{10,... | collective-permute-start | bytes 393224 | tf_op jit(solution)/shard_map/ppermute | solution.py:44
  68.4 7.3 %collective-permute-start.28 = (bf16[128,512]{1,0:T(8,128)(2,1)S(1)}, bf16[128,512]{1,0:T(8,128)(2,1)S(1)}, u32[]{:S(2)}, u32[]{:S(2)}) collective-permute-start(bf16[128,512]{1,0:T(8,128)(2,1)S(1)} %add_convert_fusion.2.refs_0_), channel_id=1, source_target_pairs={{0,3},{1,2},{2,1},{3,0},{4,7},{5,6},{6,5},{7,4},{8,11},{9,10},{10,... | collective-permute-start | bytes 393224 | tf_op jit(solution)/shard_map/ppermute | solution.py:44
  68.5 8.7 %collective-permute-start.27 = (bf16[128,512]{1,0:T(8,128)(2,1)S(1)}, bf16[128,512]{1,0:T(8,128)(2,1)S(1)}, u32[]{:S(2)}, u32[]{:S(2)}) collective-permute-start(bf16[128,512]{1,0:T(8,128)(2,1)S(1)} %add_convert_fusion.2.refs_0_), channel_id=1, source_target_pairs={{0,2},{1,3},{2,0},{3,1},{4,6},{5,7},{6,4},{7,5},{8,10},{9,11},{10,... | collective-permute-start | bytes 393224 | tf_op jit(solution)/shard_map/ppermute | solution.py:44
  73.4 7.5 %collective-permute-start.21 = (bf16[128,512]{1,0:T(8,128)(2,1)S(1)}, bf16[128,512]{1,0:T(8,128)(2,1)S(1)}, u32[]{:S(2)}, u32[]{:S(2)}) collective-permute-start(bf16[128,512]{1,0:T(8,128)(2,1)S(1)} %add_convert_fusion.4.refs_0_), channel_id=1, source_target_pairs={{0,3},{1,2},{2,1},{3,0},{4,7},{5,6},{6,5},{7,4},{8,11},{9,10},{10,... | collective-permute-start | bytes 393224 | tf_op jit(solution)/shard_map/ppermute | solution.py:44
  73.8 7.1 %collective-permute-start.20 = (bf16[128,512]{1,0:T(8,128)(2,1)S(1)}, bf16[128,512]{1,0:T(8,128)(2,1)S(1)}, u32[]{:S(2)}, u32[]{:S(2)}) collective-permute-start(bf16[128,512]{1,0:T(8,128)(2,1)S(1)} %add_convert_fusion.4.refs_0_), channel_id=1, source_target_pairs={{0,2},{1,3},{2,0},{3,1},{4,6},{5,7},{6,4},{7,5},{8,10},{9,11},{10,... | collective-permute-start | bytes 393224 | tf_op jit(solution)/shard_map/ppermute | solution.py:44
  75.7 6.4 %collective-permute-start.19 = (bf16[128,512]{1,0:T(8,128)(2,1)S(1)}, bf16[128,512]{1,0:T(8,128)(2,1)S(1)}, u32[]{:S(2)}, u32[]{:S(2)}) collective-permute-start(bf16[128,512]{1,0:T(8,128)(2,1)S(1)} %add_convert_fusion.4.refs_0_), channel_id=1, source_target_pairs={{0,1},{1,0},{2,3},{3,2},{4,5},{5,4},{6,7},{7,6},{8,9},{9,8},{10,11... | collective-permute-start | bytes 393224 | tf_op jit(solution)/shard_map/ppermute | solution.py:44
  85.2 5.7 %collective-permute-start.33 = (bf16[128,512]{1,0:T(8,128)(2,1)S(1)}, bf16[128,512]{1,0:T(8,128)(2,1)S(1)}, u32[]{:S(2)}, u32[]{:S(2)}) collective-permute-start(bf16[128,512]{1,0:T(8,128)(2,1)S(1)} %get-tuple-element.80), channel_id=1, source_target_pairs={{0,1},{1,0},{2,3},{3,2},{4,5},{5,4},{6,7},{7,6},{8,9},{9,8},{10,11... | collective-permute-start | bytes 393224 | tf_op jit(solution)/shard_map/ppermute | solution.py:44
  86.1 7.6 %collective-permute-start.34 = (bf16[128,512]{1,0:T(8,128)(2,1)S(1)}, bf16[128,512]{1,0:T(8,128)(2,1)S(1)}, u32[]{:S(2)}, u32[]{:S(2)}) collective-permute-start(bf16[128,512]{1,0:T(8,128)(2,1)S(1)} %get-tuple-element.81), channel_id=1, source_target_pairs={{0,2},{1,3},{2,0},{3,1},{4,6},{5,7},{6,4},{7,5},{8,10},{9,11},{10,... | collective-permute-start | bytes 393224 | tf_op jit(solution)/shard_map/ppermute | solution.py:44
  86.1 7.9 %collective-permute-start.35 = (bf16[128,512]{1,0:T(8,128)(2,1)S(1)}, bf16[128,512]{1,0:T(8,128)(2,1)S(1)}, u32[]{:S(2)}, u32[]{:S(2)}) collective-permute-start(bf16[128,512]{1,0:T(8,128)(2,1)S(1)} %get-tuple-element.82), channel_id=1, source_target_pairs={{0,3},{1,2},{2,1},{3,0},{4,7},{5,6},{6,5},{7,4},{8,11},{9,10},{10,... | collective-permute-start | bytes 393224 | tf_op jit(solution)/shard_map/ppermute | solution.py:44
  90.1 6.4 %collective-permute-start.29 = (bf16[128,512]{1,0:T(8,128)(2,1)S(1)}, bf16[128,512]{1,0:T(8,128)(2,1)S(1)}, u32[]{:S(2)}, u32[]{:S(2)}) collective-permute-start(bf16[128,512]{1,0:T(8,128)(2,1)S(1)} %get-tuple-element.76), channel_id=1, source_target_pairs={{0,1},{1,0},{2,3},{3,2},{4,5},{5,4},{6,7},{7,6},{8,9},{9,8},{10,11... | collective-permute-start | bytes 393224 | tf_op jit(solution)/shard_map/ppermute | solution.py:44
  90.9 7.3 %collective-permute-start.31 = (bf16[128,512]{1,0:T(8,128)(2,1)S(1)}, bf16[128,512]{1,0:T(8,128)(2,1)S(1)}, u32[]{:S(2)}, u32[]{:S(2)}) collective-permute-start(bf16[128,512]{1,0:T(8,128)(2,1)S(1)} %get-tuple-element.78), channel_id=1, source_target_pairs={{0,3},{1,2},{2,1},{3,0},{4,7},{5,6},{6,5},{7,4},{8,11},{9,10},{10,... | collective-permute-start | bytes 393224 | tf_op jit(solution)/shard_map/ppermute | solution.py:44
  94.3 7.5 %collective-permute-start.36 = (bf16[128,512]{1,0:T(8,128)(2,1)S(1)}, bf16[128,512]{1,0:T(8,128)(2,1)S(1)}, u32[]{:S(2)}, u32[]{:S(2)}) collective-permute-start(bf16[128,512]{1,0:T(8,128)(2,1)S(1)} %convolution_convert_fusion), channel_id=1, source_target_pairs={{0,6},{1,7},{2,4},{3,5},{4,2},{5,3},{6,0},{7,1},{8,14},{9,15},{10,... | collective-permute-start | bytes 393224 | tf_op jit(solution)/shard_map/ppermute | solution.py:44
  98.6 6.9 %collective-permute-start.32 = (bf16[128,512]{1,0:T(8,128)(2,1)S(1)}, bf16[128,512]{1,0:T(8,128)(2,1)S(1)}, u32[]{:S(2)}, u32[]{:S(2)}) collective-permute-start(bf16[128,512]{1,0:T(8,128)(2,1)S(1)} %convolution_convert_fusion.1), channel_id=1, source_target_pairs={{0,6},{1,7},{2,4},{3,5},{4,2},{5,3},{6,0},{7,1},{8,14},{9,15},{10,... | collective-permute-start | bytes 393224 | tf_op jit(solution)/shard_map/ppermute | solution.py:44
  (13 other events, 139.7 us)
